TPU v7x, 32 devices: a whole 2x2x4 slice. The times are simulated.
32 devices in a mesh: dp: 2 (over core), expert: 16 (over z, y, x).
Axes of the slice: x: 2, y: 2, z: 4, core: 2. Of those that a mesh axis runs over, the one named last changes fastest.
Arguments:
- tokens: bfloat16 [32768, 1024], P(('dp', 'expert')), may hold values from -6 to 6
- cotangent: bfloat16 [32768, 1024], P(('dp', 'expert')), may hold values from -6 to 6
- segment_ids: int32 [32, 1024], P(('dp', 'expert')), may hold values from 0 to 7, never falling along the last dimension, each value on 1 to 512 neighbouring positions
- expert_ids: int32 [32768, 1], P(('dp', 'expert')), may hold values from 0 to 15; in each aligned block of 1024 rows (0 to 1023, 1024 to 2047, ...) at most 96 rows name the same one
- qkv_weight: bfloat16 [3, 1024, 1024], P(None, None, 'dp'), may hold values from -0.1875 to 0.1875
- proj_weight: bfloat16 [1024, 1024], P('dp'), may hold values from -0.75 to 0.75
- proj_bias: bfloat16 [1024], replicated, may hold values from -1 to 1
- pre_gain: bfloat16 [1024], replicated, may hold values from 0.5 to 1.5
- pre_shift: bfloat16 [1024], replicated, may hold values from -1 to 1
- mid_gain: bfloat16 [1024], replicated, may hold values from 0.5 to 1.5
- mid_shift: bfloat16 [1024], replicated, may hold values from -1 to 1
- up_weight: bfloat16 [16, 4096, 1024], P('expert', 'dp'), may hold values from -0.1875 to 0.1875
- up_bias: bfloat16 [16, 4096], P('expert', 'dp'), may hold values from -1.5 to 1.5
- down_weight: bfloat16 [16, 4096, 1024], P('expert', 'dp'), may hold values from -0.09375 to 0.09375
- down_bias: bfloat16 [16, 1024], P('expert'), may hold values from -1 to 1
Outputs:
- output: bfloat16 [32768, 1024], P(('dp', 'expert'))
- input_grad: float32 [32768, 1024], P(('dp', 'expert'))
- qkv_grad: float32 [3, 1024, 1024], P(None, None, 'dp')
- proj_grad: float32 [1024, 1024], P('dp')
- projbias_grad: float32 [1024], replicated
- pregain_grad: float32 [1024], replicated
- before_offset_gradient: float32 [1024], replicated
- midgain_grad: float32 [1024], replicated
- midshift_grad: float32 [1024], replicated
- up_grad: float32 [16, 4096, 1024], P('expert', 'dp')
- upbias_grad: float32 [16, 4096], P('expert', 'dp')
- down_grad: float32 [16, 4096, 1024], P('expert', 'dp')
- downbias_grad: float32 [16, 1024], P('expert')
Inputs may be any that keep to these rules, and one draw needn't show every extreme that they name: `expert_ids`: in the rows of one device (each aligned block of 1024 rows) no expert is named more than 96 times, a bound that some block reaches. `segment_ids`: along each sequence of 1024 positions the ids never fall; a document holds at most 512 positions.
All inputs are finite; a program needn't handle non-finite values.
Results may differ from a plain program's by a relative error of at most 0.017.
Values may be sent and summed in bfloat16 or wider, within the bound.
A program may use at most 320 MiB of HBM per device.

v0:
```python
import jax
import jax.numpy as jnp
from jax import lax
from jax.sharding import PartitionSpec as P

HEAD_DIM = 64
SEQ = 1024


epsilon = 1e-05


def normalize(values, gain_vec, shift_vec):
    centre = values - jnp.mean(values, axis=-1, keepdims=True)
    variance = jnp.mean(centre * centre, axis=-1, keepdims=True)
    inverse = lax.rsqrt(variance + epsilon)
    unit_rows = centre * inverse
    return (unit_rows * gain_vec + shift_vec, unit_rows, inverse)


def norm_back(grad_out, unit_rows, inverse, gain_vec):
    scaled = grad_out * gain_vec
    inner_sum = jnp.mean(scaled, axis=-1, keepdims=True)
    projected = jnp.mean(scaled * unit_rows, axis=-1, keepdims=True)
    return inverse * (scaled - inner_sum - unit_rows * projected)


def allowed_mask(seg_row):
    places = jnp.arange(seg_row.shape[0], dtype=jnp.int32)
    return (seg_row[:, None] == seg_row[None, :]) & (places[None, :] <= places[:, None])


def masked_scores(query_rows, key_rows, seg_row):
    scaling = query_rows.shape[-1] ** (-0.5)
    scores = (
        jnp.einsum("qhd,khd->hqk", query_rows, key_rows, preferred_element_type=jnp.float32)
        * scaling
    )
    return (jnp.where(allowed_mask(seg_row)[None], scores, -1e30), scaling)


def attend_forward(pieces):
    query_rows, key_rows, value_rows, seg_row = pieces
    scores, scaling = masked_scores(query_rows, key_rows, seg_row)
    row_top = jnp.max(scores, axis=-1, keepdims=True)
    weights = jnp.exp(scores - row_top)
    totals = jnp.sum(weights, axis=-1, keepdims=True)
    probs_low = (weights / totals).astype(jnp.bfloat16)
    attended = jnp.einsum("hqk,khd->qhd", probs_low, value_rows, preferred_element_type=jnp.float32)
    return (attended.astype(jnp.bfloat16), (row_top + jnp.log(totals))[..., 0])


def attend_backward(pieces):
    query_rows, key_rows, value_rows, seg_row, log_total, grad_att = pieces
    scores, scaling = masked_scores(query_rows, key_rows, seg_row)
    attn_probs = jnp.exp(scores - log_total[..., None])
    probs_low = attn_probs.astype(jnp.bfloat16)
    grad_probs = jnp.einsum(
        "qhd,khd->hqk", grad_att, value_rows, preferred_element_type=jnp.float32
    )
    grad_values = jnp.einsum(
        "hqk,qhd->khd", probs_low, grad_att, preferred_element_type=jnp.float32
    )
    inner_sum = jnp.sum(attn_probs * grad_probs, axis=-1, keepdims=True)
    grad_scores = (attn_probs * (grad_probs - inner_sum)).astype(jnp.bfloat16)
    grad_queries = (
        jnp.einsum("hqk,khd->qhd", grad_scores, key_rows, preferred_element_type=jnp.float32)
        * scaling
    )
    grad_keys = (
        jnp.einsum("hqk,qhd->khd", grad_scores, query_rows, preferred_element_type=jnp.float32)
        * scaling
    )
    return jnp.stack([grad_queries, grad_keys, grad_values], axis=1).astype(jnp.bfloat16)


def gelu_back(hidden, grad_active):
    return jax.vjp(lambda values: jax.nn.gelu(values, approximate=True), hidden)[1](grad_active)[0]


def route(values):
    return lax.all_to_all(values, "expert", split_axis=0, concat_axis=0, tiled=True)


def route_grads(values):
    return lax.all_to_all(values, "expert", split_axis=0, concat_axis=0, tiled=True)


def on_device(
    tokens,
    cotangent,
    segment_ids,
    expert_ids,
    qkv_weight,
    proj_weight,
    proj_bias,
    pre_gain,
    pre_shift,
    mid_gain,
    mid_shift,
    up_weight,
    up_bias,
    down_weight,
    down_bias,
):
    tok_rows = tokens.shape[0]
    hidden_width = tokens.shape[1]
    groups = lax.axis_size("expert")
    halves = lax.axis_size("dp")
    local_experts = up_weight.shape[0]
    experts = local_experts * groups
    capacity = 3 * tok_rows // (2 * experts)
    pre_gain_f = pre_gain.astype(jnp.float32)
    pre_shift_f = pre_shift.astype(jnp.float32)
    mid_gain_f = mid_gain.astype(jnp.float32)
    mid_shift_f = mid_shift.astype(jnp.float32)
    proj_bias_f = proj_bias.astype(jnp.float32)
    down_bias_f = down_bias.astype(jnp.float32)
    both_rows, both_segs = (
        lax.all_gather(tokens, "dp", axis=0, tiled=True),
        lax.all_gather(segment_ids.astype(jnp.bfloat16), "dp", axis=0, tiled=True),
    )
    chip_segs = both_segs.astype(jnp.int32)
    local_heads = qkv_weight.shape[2] // HEAD_DIM
    seq_count = chip_segs.shape[0]
    normed_pre, unit_pre, inverse_pre = normalize(
        both_rows.astype(jnp.float32), pre_gain_f, pre_shift_f
    )
    normed_low = normed_pre.astype(jnp.bfloat16)
    head_rows = jnp.einsum(
        "td,cde->tce", normed_low, qkv_weight, preferred_element_type=jnp.float32
    ).astype(jnp.bfloat16)
    shaped = head_rows.reshape(seq_count, SEQ, 3, local_heads, HEAD_DIM)
    query_all = shaped[:, :, 0]
    key_all = shaped[:, :, 1]
    value_all = shaped[:, :, 2]
    attended, log_total = lax.map(attend_forward, (query_all, key_all, value_all, chip_segs))
    attended = attended.reshape(seq_count * SEQ, local_heads * HEAD_DIM)
    picked = attended
    branch = (
        lax.psum_scatter(
            jnp.dot(picked, proj_weight, preferred_element_type=jnp.float32).astype(jnp.bfloat16),
            "dp",
            scatter_dimension=0,
            tiled=True,
        ).astype(jnp.float32)
        + proj_bias_f
    )
    middle = tokens.astype(jnp.float32) + branch
    normed_mid, unit_mid, inverse_mid = normalize(middle, mid_gain_f, mid_shift_f)
    mid_low = normed_mid.astype(jnp.bfloat16)
    ids_flat = expert_ids[:, 0]
    onehot = (ids_flat[:, None] == jnp.arange(experts, dtype=jnp.int32)[None, :]).astype(jnp.int32)
    slot_rank = jnp.sum(jnp.cumsum(onehot, axis=0) * onehot, axis=1) - 1
    target = ids_flat * capacity + slot_rank
    slot_shape = (groups, local_experts, capacity, hidden_width)

    def to_slots(values):
        return (
            jnp.zeros((experts * capacity, hidden_width), jnp.bfloat16)
            .at[target]
            .set(values)
            .reshape(slot_shape)
        )

    def from_slots(values):
        return values.reshape(experts * capacity, hidden_width)[target]

    arrived = route(to_slots(mid_low))
    chip_in = lax.all_gather(arrived, "dp", axis=0, tiled=True)
    hidden = (
        jnp.einsum("secd,efd->secf", chip_in, up_weight, preferred_element_type=jnp.float32)
        + up_bias.astype(jnp.float32)[None, :, None, :]
    )
    active = jax.nn.gelu(hidden, approximate=True).astype(jnp.bfloat16)
    picked = active
    summed = lax.psum_scatter(
        jnp.einsum(
            "secf,efd->secd", picked, down_weight, preferred_element_type=jnp.float32
        ).astype(jnp.bfloat16),
        "dp",
        scatter_dimension=0,
        tiled=True,
    ).astype(jnp.float32)
    expert_out = (summed + down_bias_f[None, :, None, :]).astype(jnp.bfloat16)
    returned = route(expert_out)
    output = (middle + from_slots(returned).astype(jnp.float32)).astype(jnp.bfloat16)
    grad_slots = route_grads(to_slots(cotangent))
    chip_grad = lax.all_gather(grad_slots, "dp", axis=0, tiled=True)
    downbias_grad = jnp.sum(chip_grad, axis=(0, 2), dtype=jnp.float32)
    down_grad = jnp.einsum("secf,secd->efd", active, chip_grad, preferred_element_type=jnp.float32)
    grad_active = jnp.einsum(
        "secd,efd->secf", chip_grad, down_weight, preferred_element_type=jnp.float32
    )
    grad_hidden = gelu_back(hidden, grad_active).astype(jnp.bfloat16)
    up_grad = jnp.einsum("secf,secd->efd", grad_hidden, chip_in, preferred_element_type=jnp.float32)
    upbias_grad = jnp.sum(grad_hidden, axis=(0, 2), dtype=jnp.float32)
    picked = grad_hidden
    grad_mid_slots = lax.psum_scatter(
        jnp.einsum("secf,efd->secd", picked, up_weight, preferred_element_type=jnp.float32).astype(
            jnp.bfloat16
        ),
        "dp",
        scatter_dimension=0,
        tiled=True,
    )
    grad_mid_back = route_grads(grad_mid_slots)
    grad_normed_mid = from_slots(grad_mid_back).astype(jnp.float32)
    middle_gain_share = jnp.sum(grad_normed_mid * unit_mid, axis=0)
    middle_offset_share = jnp.sum(grad_normed_mid, axis=0)
    grad_middle = cotangent.astype(jnp.float32) + norm_back(
        grad_normed_mid, unit_mid, inverse_mid, mid_gain_f
    )
    grad_branch = grad_middle.astype(jnp.bfloat16)
    projection_bias_share = jnp.sum(grad_branch, axis=0, dtype=jnp.float32)
    chip_branch = lax.all_gather(grad_branch, "dp", axis=0, tiled=True)
    proj_part = jnp.einsum("te,td->ed", attended, chip_branch, preferred_element_type=jnp.float32)
    grad_attended = jnp.einsum(
        "td,ed->te", chip_branch, proj_weight, preferred_element_type=jnp.float32
    ).astype(jnp.bfloat16)
    grad_attended = grad_attended.reshape(seq_count, SEQ, local_heads, HEAD_DIM)
    grad_heads = lax.map(
        attend_backward, (query_all, key_all, value_all, chip_segs, log_total, grad_attended)
    )
    grad_heads = grad_heads.reshape(seq_count * SEQ, 3, local_heads * HEAD_DIM)
    qkv_part = jnp.einsum("td,tce->cde", normed_low, grad_heads, preferred_element_type=jnp.float32)
    gradient_normalized_before = jnp.einsum(
        "tce,cde->td", grad_heads, qkv_weight, preferred_element_type=jnp.float32
    )
    before_gain_share = jnp.sum(gradient_normalized_before * unit_pre, axis=0)
    before_offset_share = jnp.sum(gradient_normalized_before, axis=0)
    grad_chip = norm_back(gradient_normalized_before, unit_pre, inverse_pre, pre_gain_f)
    small_grads = jnp.concatenate(
        [
            before_gain_share,
            before_offset_share,
            middle_gain_share,
            middle_offset_share,
            projection_bias_share,
        ]
    )
    doubled_small = jnp.broadcast_to(small_grads[None, :], (halves, small_grads.shape[0]))
    grad_own, small_pair = (
        lax.psum_scatter(
            grad_chip.astype(jnp.bfloat16), "dp", scatter_dimension=0, tiled=True
        ).astype(jnp.float32),
        lax.psum_scatter(
            doubled_small.astype(jnp.bfloat16), "dp", scatter_dimension=0, tiled=True
        ).astype(jnp.float32),
    )
    input_grad = grad_middle + grad_own
    qkv_grad, proj_grad, small_total = lax.psum((qkv_part, proj_part, small_pair), "expert")
    compact_row = small_total[0]
    pregain_grad = compact_row[0:hidden_width]
    before_offset_gradient = compact_row[hidden_width : 2 * hidden_width]
    midgain_grad = compact_row[2 * hidden_width : 3 * hidden_width]
    midshift_grad = compact_row[3 * hidden_width : 4 * hidden_width]
    projbias_grad = compact_row[4 * hidden_width : 5 * hidden_width]
    return (
        output,
        input_grad,
        qkv_grad,
        proj_grad,
        projbias_grad,
        pregain_grad,
        before_offset_gradient,
        midgain_grad,
        midshift_grad,
        up_grad,
        upbias_grad,
        down_grad,
        downbias_grad,
    )


def solution(mesh):
    in_specs = (
        P(("dp", "expert"), None),
        P(("dp", "expert"), None),
        P(("dp", "expert"), None),
        P(("dp", "expert"), None),
        P(None, None, "dp"),
        P("dp", None),
        P(),
        P(),
        P(),
        P(),
        P(),
        P("expert", "dp", None),
        P("expert", "dp"),
        P("expert", "dp", None),
        P("expert", None),
    )
    out_specs = (
        P(("dp", "expert"), None),
        P(("dp", "expert"), None),
        P(None, None, "dp"),
        P("dp", None),
        P(),
        P(),
        P(),
        P(),
        P(),
        P("expert", "dp", None),
        P("expert", "dp"),
        P("expert", "dp", None),
        P("expert", None),
    )
    return jax.shard_map(
        on_device, mesh=mesh, in_specs=in_specs, out_specs=out_specs, check_vma=False
    )
```

profile of v0, /device:TPU:0, one launch (start us, length us, event | category | flops | bytes accessed | tf_op | source)
XLA Modules:
  0.0 1229.3 jit_solution(16342227529308051257)
XLA Ops:
  12.2 13.8 %all-gather.6.cloned.1.call-done = bf16[2048,1024]{1,0:T(8,128)(2,1)} async-done(((bf16[1024,1024]{1,0:T(8,128)(2,1)}), bf16[2048,1024]{1,0:T(8,128)(2,1)}) %all-gather.6.cloned.1.call-update) | async-done | bytes 4194320 | tf_op jit(solution)/shard_map/all_gather | solution.py:120
  72.2 91.5 %while.22 = (s32[]{:T(128)}, bf16[2,1024,8,64]{1,3,2,0:T(8,128)(2,1)}, f32[2,8,1024]{2,1,0:T(8,128)S(1)}, bf16[2,1024,8,64]{1,3,2,0:T(8,128)(2,1)}, s32[2,1024]{...) while((s32[]{:T(128)}, ...), condition=%wide.region_5.6_spmd, body=%wide.region_2.5_spmd.sunk | while | flops 2251808768 | bytes 117717128 | solution.py:137
  73.2 15.0 %fusion.183 = (f32[8,1024]{1,0:T(8,128)S(1)}, f32[8,1024,1024]{1,2,0:T(8,128)}) fusion(pred[1024,1024]{0,1:T(8,128)(4,1)S(1)} %fusion.182, bf16[2,1024,8,64]{1,3,2,0:T(8,128)(2,1)} %get-tuple-element.356, s32[]{:T(128)S(6)} %copy.101, bf16[2,1024,8,64]{1,3,2,0:T(8,128)(2,1)} %get-tuple-element.355), kind=kOutput, calls=%fused_computation.7.clone.1 | convolution fusion | flops 1098899456 | bytes 36733952 | tf_op jit(solution)/shard_map/while/body/eval_jaxpr/qhd,khd->hqk/dot_general | solution.py:36
  88.2 14.3 %fusion.184 = f32[8,1024]{1,0:T(8,128)S(1)} fusion(f32[8,1024,1024]{1,2,0:T(8,128)} %get-tuple-element.322, f32[8,1024]{1,0:T(8,128)S(1)} %get-tuple-element.323, pred[1024,1024]{0,1:T(8,128)(4,1)S(1)} %fusion.182), kind=kLoop, calls=%fused_computation.8.clone.1 | loop fusion | flops 33546240 | bytes 34668544 | tf_op jit(solution)/shard_map/while/body/eval_jaxpr/reduce_sum | solution.py:47
  102.5 15.5 %fusion.185 = bf16[2,1024,8,64]{1,3,2,0:T(8,128)(2,1)} fusion(bf16[2,1024,8,64]{1,3,2,0:T(8,128)(2,1)} %get-tuple-element.343, s32[]{:T(128)S(6)} %copy.101, f32[8,1024,1024]{1,2,0:T(8,128)} %get-tuple-element.322, f32[8,1024]{1,0:T(8,128)S(1)} %fusion.184, f32[8,1024]{1,0:T(8,128)S(1)} %get-tuple-element.323, pred[1024,1024]{0,1:T(8,128)(4,1)S(1)} %fusion.182, ...), kind=kOutput, calls=%fused_computation.14.clone.1 | convolution fusion | flops 1116209152 | bytes 36766720 | tf_op jit(solution)/shard_map/while/body/eval_jaxpr/hqk,khd->qhd/dot_general | solution.py:49
  118.7 15.0 %fusion.183 = (f32[8,1024]{1,0:T(8,128)S(1)}, f32[8,1024,1024]{1,2,0:T(8,128)}) fusion(pred[1024,1024]{0,1:T(8,128)(4,1)S(1)} %fusion.182, bf16[2,1024,8,64]{1,3,2,0:T(8,128)(2,1)} %get-tuple-element.356, s32[]{:T(128)S(6)} %copy.101, bf16[2,1024,8,64]{1,3,2,0:T(8,128)(2,1)} %get-tuple-element.355), kind=kOutput, calls=%fused_computation.7.clone.1 | convolution fusion | flops 1098899456 | bytes 36733952 | tf_op jit(solution)/shard_map/while/body/eval_jaxpr/qhd,khd->hqk/dot_general | solution.py:36
  133.6 14.3 %fusion.184 = f32[8,1024]{1,0:T(8,128)S(1)} fusion(f32[8,1024,1024]{1,2,0:T(8,128)} %get-tuple-element.322, f32[8,1024]{1,0:T(8,128)S(1)} %get-tuple-element.323, pred[1024,1024]{0,1:T(8,128)(4,1)S(1)} %fusion.182), kind=kLoop, calls=%fused_computation.8.clone.1 | loop fusion | flops 33546240 | bytes 34668544 | tf_op jit(solution)/shard_map/while/body/eval_jaxpr/reduce_sum | solution.py:47
  148.0 15.5 %fusion.185 = bf16[2,1024,8,64]{1,3,2,0:T(8,128)(2,1)} fusion(bf16[2,1024,8,64]{1,3,2,0:T(8,128)(2,1)} %get-tuple-element.343, s32[]{:T(128)S(6)} %copy.101, f32[8,1024,1024]{1,2,0:T(8,128)} %get-tuple-element.322, f32[8,1024]{1,0:T(8,128)S(1)} %fusion.184, f32[8,1024]{1,0:T(8,128)S(1)} %get-tuple-element.323, pred[1024,1024]{0,1:T(8,128)(4,1)S(1)} %fusion.182, ...), kind=kOutput, calls=%fused_computation.14.clone.1 | convolution fusion | flops 1116209152 | bytes 36766720 | tf_op jit(solution)/shard_map/while/body/eval_jaxpr/hqk,khd->qhd/dot_general | solution.py:49
  202.9 79.0 %all_to_all.20 = bf16[16,1,96,1024]{3,2,1,0:T(8,128)(2,1)} all-to-all(bf16[16,1,96,1024]{3,2,1,0:T(8,128)(2,1)} %bitcast.316), channel_id=1, replica_groups=mesh['dp'=2,'expert'=16] {'expert'}, dimensions={0} | all-to-all | bytes 6291456 | tf_op jit(solution)/shard_map/all_to_all | solution.py:82
  294.7 60.1 %all-to-all-done.2 = bf16[16,1,96,1024]{3,2,1,0:T(8,128)(2,1)} async-done(((bf16[16,1,96,1024]{3,2,1,0:T(8,128)(2,1)}), bf16[16,1,96,1024]{3,2,1,0:T(8,128)(2,1)}, u32[]{:S(2)}, u32[]{:S(2)}) %all-to-all-start.2) | async-done | bytes 3145760 | tf_op jit(solution)/shard_map/all_to_all | solution.py:86
  354.9 20.7 %fusion.91 = f32[32,96,2048]{2,1,0:T(8,128)} fusion(bf16[32,1,96,1024]{3,2,1,0:T(8,128)(2,1)} %all-gather.8.cloned.1.call-done, bf16[1,2048,1024]{2,1,0:T(8,128)(2,1)} %param.30), kind=kOutput, calls=%fused_computation.117 | convolution fusion | flops 12884901888 | bytes 35651584 | tf_op jit(solution)/shard_map/secd,efd->secf/dot_general | solution.py:172
  375.6 25.0 %convert_bitcast_fusion.1 = bf16[32,1,96,1024]{3,2,0,1:T(8,128)(2,1)} fusion(bf16[1,2048,1024]{2,1,0:T(8,128)(2,1)} %param.32, f32[32,96,2048]{2,1,0:T(8,128)} %fusion.91, f32[2048]{0:T(1024)S(1)} %bitcast.333), kind=kOutput, calls=%fused_computation.121 | convolution fusion | flops 12950962176 | bytes 35659776 | tf_op jit(solution)/shard_map/secf,efd->secd/dot_general | solution.py:178
  400.9 35.8 %convert_reduce_fusion = (f32[2048]{0:T(1024)}, bf16[32,1,96,2048]{3,2,0,1:T(8,128)(2,1)}) fusion(f32[2048]{0:T(1024)S(1)} %bitcast.334, f32[32,96,2048]{2,1,0:T(8,128)} %fusion.91, bf16[1,2048,1024]{2,1,0:T(8,128)(2,1)} %param.32, bf16[32,1,96,1024]{3,2,1,0:T(8,128)(2,1)} %all-gather.10.cloned.1.call-done), kind=kOutput, calls=%fused_computation.84 | convolution fusion | flops 13029603328 | bytes 48250880 | tf_op jit(solution)/shard_map/secd,efd->secf/dot_general | solution.py:192
  436.7 18.7 %convert_bitcast_fusion = bf16[32,1,96,1024]{3,2,0,1:T(8,128)(2,1)} fusion(bf16[1,2048,1024]{2,1,0:T(8,128)(2,1)} %param.30, bf16[32,1,96,2048]{3,2,0,1:T(8,128)(2,1)} %get-tuple-element.231), kind=kOutput, calls=%fused_computation.119 | convolution fusion | flops 12888047616 | bytes 23068672 | tf_op jit(solution)/shard_map/secf,efd->secd/dot_general | solution.py:200
  477.0 56.9 %all-to-all-done.1 = bf16[16,1,96,1024]{3,2,1,0:T(8,128)(2,1)} async-done(((bf16[16,1,96,1024]{3,2,1,0:T(8,128)(2,1)}), bf16[16,1,96,1024]{3,2,1,0:T(8,128)(2,1)}, u32[]{:S(2)}, u32[]{:S(2)}) %all-to-all-start.1) | async-done | bytes 3145760 | tf_op jit(solution)/shard_map/all_to_all | solution.py:82
  533.9 14.1 %all-to-all-start.3 = ((bf16[16,1,96,1024]{3,2,1,0:T(8,128)(2,1)}), bf16[16,1,96,1024]{3,2,1,0:T(8,128)(2,1)}, u32[]{:S(2)}, u32[]{:S(2)}) async-start(bf16[16,1,96,1024]{3,2,1,0:T(8,128)(2,1)} %bitcast.318), calls=%async_computation.6 | async-start | bytes 6291456 | tf_op jit(solution)/shard_map/all_to_all | solution.py:86
  556.4 52.3 %all-to-all-done.3 = bf16[16,1,96,1024]{3,2,1,0:T(8,128)(2,1)} async-done(((bf16[16,1,96,1024]{3,2,1,0:T(8,128)(2,1)}), bf16[16,1,96,1024]{3,2,1,0:T(8,128)(2,1)}, u32[]{:S(2)}, u32[]{:S(2)}) %all-to-all-start.3) | async-done | bytes 3145760 | tf_op jit(solution)/shard_map/all_to_all | solution.py:86
  629.2 22.2 %all-gather.12.cloned.1.call-done = bf16[2048,1024]{1,0:T(8,128)(2,1)} async-done(((bf16[1024,1024]{1,0:T(8,128)(2,1)}), bf16[2048,1024]{1,0:T(8,128)(2,1)}) %all-gather.12.cloned.1.call-update) | async-done | bytes 4194320 | tf_op jit(solution)/shard_map/all_gather | solution.py:216
  669.2 233.0 %while.23 = (s32[]{:T(128)}, bf16[2,1024,3,8,64]{1,4,3,2,0:T(8,128)(2,1)}, bf16[2,1024,8,64]{1,3,2,0:T(8,128)(2,1)}, s32[2,1024]{1,0:T(2,128)S(1)}, bf16[2,1024,...) while((s32[]{:T(128)}, ...), condition=%wide.region_20.21_spmd, body=%wide.region_18.20_spmd.sunk | while | flops 5509734400 | bytes 272873568 | solution.py:222
  671.0 17.1 %fusion.194 = f32[8,1024,1024]{1,2,0:T(8,128)} fusion(bf16[2,1024,8,64]{1,3,2,0:T(8,128)(2,1)} %get-tuple-element.380, s32[]{:T(128)S(6)} %copy.109, bf16[2,1024,8,64]{1,3,2,0:T(8,128)(2,1)} %get-tuple-element.378), kind=kOutput, calls=%fused_computation.48.clone.1 | convolution fusion | flops 1073741824 | bytes 35652608 | tf_op jit(solution)/shard_map/while/body/eval_jaxpr/qhd,khd->hqk/dot_general | solution.py:36
  688.1 16.1 %fusion.196 = bf16[1,1024,1,8,64]{1,4,3,2,0:T(8,128)(2,1)} fusion(f32[8,1024,1024]{1,2,0:T(8,128)} %fusion.194, f32[8,1024]{1,0:T(8,128)S(1)} %dynamic-slice_bitcast_fusion.2, pred[1024,1024]{0,1:T(8,128)(4,1)} %fusion.195, bf16[2,1024,8,64]{1,3,2,0:T(8,128)(2,1)} %get-tuple-element.382, s32[]{:T(128)S(6)} %copy.109), kind=kOutput, calls=%fused_computation.42.clone.1 | convolution fusion | flops 1107820544 | bytes 36732932 | tf_op jit(solution)/shard_map/while/body/eval_jaxpr/hqk,qhd->khd/dot_general | solution.py:61
  704.2 26.3 %multiply_reduce_fusion.3 = (f32[8,1024]{1,0:T(8,128)S(1)}, f32[8,1024,1024]{1,2,0:T(8,128)}) fusion(f32[8,1024,1024]{1,2,0:T(8,128)} %fusion.194, f32[8,1024]{1,0:T(8,128)S(1)} %dynamic-slice_bitcast_fusion.2, pred[1024,1024]{0,1:T(8,128)(4,1)} %fusion.195, bf16[2,1024,8,64]{1,3,2,0:T(8,128)(2,1)} %get-tuple-element.383, s32[]{:T(128)S(6)} %copy.109, ...), kind=kOutput, calls=%fused_computation.29.clone.1 | convolution fusion | flops 1115676672 | bytes 70321152 | tf_op jit(solution)/shard_map/while/body/eval_jaxpr/qhd,khd->hqk/dot_general | solution.py:58
  730.5 28.7 %multiply_convert_fusion.7 = bf16[8,1024,1024]{1,2,0:T(8,128)(2,1)} fusion(f32[8,1024,1024]{1,2,0:T(8,128)} %get-tuple-element.332, f32[8,1024,1024]{1,2,0:T(8,128)} %fusion.194, f32[8,1024]{1,0:T(8,128)S(1)} %get-tuple-element.333, f32[8,1024]{1,0:T(8,128)S(1)} %dynamic-slice_bitcast_fusion.2, pred[1024,1024]{0,1:T(8,128)(4,1)} %fusion.195), kind=kLoop, calls=%fused_computation.28.clone.1 | loop fusion | flops 50331648 | bytes 85000192 | tf_op jit(solution)/shard_map/while/body/eval_jaxpr/convert_element_type | solution.py:65
  787.1 17.1 %fusion.194 = f32[8,1024,1024]{1,2,0:T(8,128)} fusion(bf16[2,1024,8,64]{1,3,2,0:T(8,128)(2,1)} %get-tuple-element.380, s32[]{:T(128)S(6)} %copy.109, bf16[2,1024,8,64]{1,3,2,0:T(8,128)(2,1)} %get-tuple-element.378), kind=kOutput, calls=%fused_computation.48.clone.1 | convolution fusion | flops 1073741824 | bytes 35652608 | tf_op jit(solution)/shard_map/while/body/eval_jaxpr/qhd,khd->hqk/dot_general | solution.py:36
  804.3 16.2 %fusion.196 = bf16[1,1024,1,8,64]{1,4,3,2,0:T(8,128)(2,1)} fusion(f32[8,1024,1024]{1,2,0:T(8,128)} %fusion.194, f32[8,1024]{1,0:T(8,128)S(1)} %dynamic-slice_bitcast_fusion.2, pred[1024,1024]{0,1:T(8,128)(4,1)} %fusion.195, bf16[2,1024,8,64]{1,3,2,0:T(8,128)(2,1)} %get-tuple-element.382, s32[]{:T(128)S(6)} %copy.109), kind=kOutput, calls=%fused_computation.42.clone.1 | convolution fusion | flops 1107820544 | bytes 36732932 | tf_op jit(solution)/shard_map/while/body/eval_jaxpr/hqk,qhd->khd/dot_general | solution.py:61
  820.5 26.3 %multiply_reduce_fusion.3 = (f32[8,1024]{1,0:T(8,128)S(1)}, f32[8,1024,1024]{1,2,0:T(8,128)}) fusion(f32[8,1024,1024]{1,2,0:T(8,128)} %fusion.194, f32[8,1024]{1,0:T(8,128)S(1)} %dynamic-slice_bitcast_fusion.2, pred[1024,1024]{0,1:T(8,128)(4,1)} %fusion.195, bf16[2,1024,8,64]{1,3,2,0:T(8,128)(2,1)} %get-tuple-element.383, s32[]{:T(128)S(6)} %copy.109, ...), kind=kOutput, calls=%fused_computation.29.clone.1 | convolution fusion | flops 1115676672 | bytes 70321152 | tf_op jit(solution)/shard_map/while/body/eval_jaxpr/qhd,khd->hqk/dot_general | solution.py:58
  846.8 28.7 %multiply_convert_fusion.7 = bf16[8,1024,1024]{1,2,0:T(8,128)(2,1)} fusion(f32[8,1024,1024]{1,2,0:T(8,128)} %get-tuple-element.332, f32[8,1024,1024]{1,2,0:T(8,128)} %fusion.194, f32[8,1024]{1,0:T(8,128)S(1)} %get-tuple-element.333, f32[8,1024]{1,0:T(8,128)S(1)} %dynamic-slice_bitcast_fusion.2, pred[1024,1024]{0,1:T(8,128)(4,1)} %fusion.195), kind=kLoop, calls=%fused_computation.28.clone.1 | loop fusion | flops 50331648 | bytes 85000192 | tf_op jit(solution)/shard_map/while/body/eval_jaxpr/convert_element_type | solution.py:65
  902.2 12.7 %copy.79 = bf16[2,1024,3,8,64]{1,0,4,3,2:T(2,128)(2,1)} copy(bf16[2,1024,3,8,64]{1,4,3,2,0:T(8,128)(2,1)} %get-tuple-element.95) | data formatting | bytes 12582912 | tf_op jit(solution)/shard_map/while | solution.py:222
  963.7 18.9 %fusion.101 = f32[1,2048,1024]{2,1,0:T(8,128)} fusion(bf16[32,1,96,1024]{3,2,1,0:T(8,128)(2,1)} %all-gather.8.cloned.1.call-done, bf16[32,1,96,2048]{3,2,0,1:T(8,128)(2,1)} %get-tuple-element.231), kind=kOutput, calls=%fused_computation.129 | convolution fusion | flops 12884901888 | bytes 27262976 | tf_op jit(solution)/shard_map/secf,secd->efd/dot_general | solution.py:196
  982.6 27.3 %fusion.96 = f32[1,2048,1024]{2,1,0:T(8,128)} fusion(bf16[32,1,96,1024]{3,2,1,0:T(8,128)(2,1)} %all-gather.10.cloned.1.call-done, f32[32,96,2048]{2,1,0:T(8,128)} %fusion.91, f32[2048]{0:T(1024)S(1)} %bitcast.335), kind=kOutput, calls=%fused_computation.128 | convolution fusion | flops 12947816448 | bytes 39854080 | tf_op jit(solution)/shard_map/secf,secd->efd/dot_general | solution.py:191
  1014.1 78.2 %psum.23 = f32[1,5120]{1,0:T(1,128)S(1)} all-reduce(f32[1,5120]{1,0:T(1,128)S(1)} %dynamic-slice_convert_fusion), channel_id=1, replica_groups=mesh['dp'=2,'expert'=16] {'expert'}, use_global_device_ids=true, to_apply=%region_32.33 | all-reduce | flops 5120 | bytes 40960 | tf_op jit(solution)/shard_map/psum | solution.py:252
  1092.9 108.8 %all-reduce.4.cloned.1.call-done = (f32[3,1024,512]{1,2,0:T(8,128)}, f32[512,1024]{1,0:T(8,128)}) async-done(((f32[3,1024,512]{1,2,0:T(8,128)}, f32[512,1024]{1,0:T(8,128)}), (f32[3,1024,512]{1,2,0:T(8,128)}, f32[512,1024]{1,0:T(8,128)})) %all-reduce.4.cloned.1.call-update) | async-done | bytes 8388624 | tf_op jit(solution)/shard_map/psum | solution.py:252
  (216 shorter events, 302.7 us)
Async XLA Ops:
  7.2 24.3 %copy-start = (bf16[3,1024,512]{2,1,0:T(8,128)(2,1)S(1)}, bf16[3,1024,512]{2,1,0:T(8,128)(2,1)}, u32[]{:S(2)}) copy-start(bf16[3,1024,512]{2,1,0:T(8,128)(2,1)} %param.23) | copy-start | bytes 9437188
  7.2 18.8 %all-gather.6.cloned.1.call-start = ((), (), s32[]{:S(2)}) async-start(), calls=%async_computation.8 | async-start | bytes 6291456 | tf_op jit(solution)/shard_map/all_gather | solution.py:120
  7.9 179.3 %reduce-scatter.5.cloned.1.call-start = ((), (), s32[]{:S(2)}) async-start(), calls=%async_computation.9 | async-start | bytes 6291456 | tf_op jit(solution)/shard_map/reduce_scatter | solution.py:141
  8.8 31.5 %copy-start.29 = (f32[1024]{0:T(1024)}, f32[1024]{0:T(1024)S(1)}, u32[]{:S(2)}) copy-start(f32[1024]{0:T(1024)S(1)} %convert_element_type.148) | copy-start | bytes 12292
  9.5 30.8 %copy-start.39 = (f32[1024]{0:T(1024)}, f32[1024]{0:T(1024)S(1)}, u32[]{:S(2)}) copy-start(f32[1024]{0:T(1024)S(1)} %convert_element_type.149) | copy-start | bytes 12292
  88.2 14.4 %copy-start.6 = (bf16[2,1024,8,64]{1,3,2,0:T(8,128)(2,1)S(1)}, bf16[2,1024,8,64]{1,3,2,0:T(8,128)(2,1)}, u32[]{:S(2)}) copy-start(bf16[2,1024,8,64]{1,3,2,0:T(8,128)(2,1)} %get-tuple-element.353) | copy-start | bytes 6291460 | tf_op jit(solution)/shard_map/while
  133.6 14.4 %copy-start.6 = (bf16[2,1024,8,64]{1,3,2,0:T(8,128)(2,1)S(1)}, bf16[2,1024,8,64]{1,3,2,0:T(8,128)(2,1)}, u32[]{:S(2)}) copy-start(bf16[2,1024,8,64]{1,3,2,0:T(8,128)(2,1)} %get-tuple-element.353) | copy-start | bytes 6291460 | tf_op jit(solution)/shard_map/while
  163.6 10.2 copy-start.12
  173.9 181.0 %all-gather.8.cloned.1.call-start = ((), (), s32[]{:S(2)}) async-start(), calls=%async_computation.10 | async-start | bytes 9437184 | tf_op jit(solution)/shard_map/all_gather | solution.py:170
  174.0 28.9 %copy-start.16 = (f32[1024]{0:T(1024)}, f32[1024]{0:T(1024)S(1)}, u32[]{:S(2)}) copy-start(f32[1024]{0:T(1024)S(1)} %convert_element_type.156) | copy-start | bytes 12292
  174.0 28.9 %copy-start.22 = (f32[1024]{0:T(1024)}, f32[1024]{0:T(1024)S(1)}, u32[]{:S(2)}) copy-start(f32[1024]{0:T(1024)S(1)} %convert_element_type.158) | copy-start | bytes 12292
  179.1 102.9 %copy-start.31 = (s32[1024,1]{0,1:T(1,128)}, s32[1024,1]{0,1:T(1,128)S(1)}, u32[]{:S(2)}) copy-start(s32[1024,1]{0,1:T(1,128)S(1)} %compare_select_fusion) | copy-start | bytes 12292
  190.2 91.7 %copy-start.18 = (f32[1024]{0:T(1024)}, f32[1024]{0:T(1024)S(1)}, u32[]{:S(2)}) copy-start(f32[1024]{0:T(1024)S(1)} %broadcast_multiply_fusion.5) | copy-start | bytes 12292
  193.5 88.4 %copy-start.24 = (f32[1024]{0:T(1024)}, f32[1024]{0:T(1024)S(1)}, u32[]{:S(2)}) copy-start(f32[1024]{0:T(1024)S(1)} %add_rsqrt_fusion.1) | copy-start | bytes 12292
  282.0 12.7 %copy-start.36 = (bf16[1,2048]{1,0:T(2,128)(2,1)S(1)}, bf16[1,2048]{1,0:T(2,128)(2,1)}, u32[]{:S(2)}) copy-start(bf16[1,2048]{1,0:T(2,128)(2,1)} %param.31) | copy-start | bytes 12292
  290.1 64.7 %all-to-all-start.2 = ((bf16[16,1,96,1024]{3,2,1,0:T(8,128)(2,1)}), bf16[16,1,96,1024]{3,2,1,0:T(8,128)(2,1)}, u32[]{:S(2)}, u32[]{:S(2)}) async-start(bf16[16,1,96,1024]{3,2,1,0:T(8,128)(2,1)} %bitcast.315), calls=%async_computation.4 | async-start | bytes 6291456 | tf_op jit(solution)/shard_map/all_to_all | solution.py:86
  294.6 106.3 %all-gather.10.cloned.1.call-start = ((), (), s32[]{:S(2)}) async-start(), calls=%async_computation.12 | async-start | bytes 9437184 | tf_op jit(solution)/shard_map/all_gather | solution.py:189
  294.7 106.2 %copy-start.37 = (f32[1,2048]{1,0:T(1,128)}, f32[1,2048]{1,0:T(1,128)S(1)}, u32[]{:S(2)}) copy-start(f32[1,2048]{1,0:T(1,128)S(1)} %add.178) | copy-start | bytes 24580
  354.8 101.3 %reduce-scatter.7.cloned.1.call-start = ((), (), s32[]{:S(2)}) async-start(), calls=%async_computation.11 | async-start | bytes 9437184 | tf_op jit(solution)/shard_map/reduce_scatter | solution.py:177
  400.7 76.3 %reduce-scatter.9.cloned.1.call-start = ((), (), s32[]{:S(2)}) async-start(), calls=%async_computation.13 | async-start | bytes 9437184 | tf_op jit(solution)/shard_map/reduce_scatter | solution.py:199
  460.6 87.5 %copy-start.32 = (s32[1024,1]{0,1:T(1,128)S(1)}, s32[1024,1]{0,1:T(1,128)}, u32[]{:S(2)}) copy-start(s32[1024,1]{0,1:T(1,128)} %copy-done.31) | copy-start | bytes 12292
  460.6 73.3 %all-to-all-start.1 = ((bf16[16,1,96,1024]{3,2,1,0:T(8,128)(2,1)}), bf16[16,1,96,1024]{3,2,1,0:T(8,128)(2,1)}, u32[]{:S(2)}, u32[]{:S(2)}) async-start(bf16[16,1,96,1024]{3,2,1,0:T(8,128)(2,1)} %fusion.124), calls=%async_computation.3 | async-start | bytes 6291456 | tf_op jit(solution)/shard_map/all_to_all | solution.py:82
  533.9 74.8 %all-to-all-start.3 = ((bf16[16,1,96,1024]{3,2,1,0:T(8,128)(2,1)}), bf16[16,1,96,1024]{3,2,1,0:T(8,128)(2,1)}, u32[]{:S(2)}, u32[]{:S(2)}) async-start(bf16[16,1,96,1024]{3,2,1,0:T(8,128)(2,1)} %bitcast.318), calls=%async_computation.6 | async-start | bytes 6291456 | tf_op jit(solution)/shard_map/all_to_all | solution.py:86
  548.0 103.4 %all-gather.12.cloned.1.call-start = ((), (), s32[]{:S(2)}) async-start(), calls=%async_computation.14 | async-start | bytes 6291456 | tf_op jit(solution)/shard_map/all_gather | solution.py:216
  629.1 572.6 %all-reduce.4.cloned.1.call-start = ((), (), s32[]{:S(2)}) async-start(), calls=%async_computation.16 | async-start | bytes 16777216 | tf_op jit(solution)/shard_map/psum | solution.py:252
  657.6 11.6 copy-start.13
  657.6 11.6 copy-start.15
  941.8 273.3 %reduce-scatter.11.cloned.1.call-start = ((), (), s32[]{:S(2)}) async-start(), calls=%async_computation.15 | async-start | bytes 6291456 | tf_op jit(solution)/shard_map/reduce_scatter | solution.py:244
  963.7 18.9 %copy-start.38 = (f32[1,2048]{1,0:T(1,128)S(1)}, f32[1,2048]{1,0:T(1,128)}, u32[]{:S(2)}) copy-start(f32[1,2048]{1,0:T(1,128)} %copy-done.37) | copy-start | bytes 24580
  982.6 27.3 %copy-start.33 = (bf16[1024]{0:T(1024)(128)(2,1)S(1)}, bf16[1024]{0:T(1024)(128)(2,1)}, u32[]{:S(2)}) copy-start(bf16[1024]{0:T(1024)(128)(2,1)} %get-tuple-element.177) | copy-start | bytes 6148
  982.6 27.3 %copy-start.35 = (bf16[1024]{0:T(1024)(128)(2,1)S(1)}, bf16[1024]{0:T(1024)(128)(2,1)}, u32[]{:S(2)}) copy-start(bf16[1024]{0:T(1024)(128)(2,1)} %get-tuple-element.223) | copy-start | bytes 6148
  982.6 27.4 %copy-start.34 = (bf16[1024]{0:T(1024)(128)(2,1)S(1)}, bf16[1024]{0:T(1024)(128)(2,1)}, u32[]{:S(2)}) copy-start(bf16[1024]{0:T(1024)(128)(2,1)} %get-tuple-element.212) | copy-start | bytes 6148
  (28 other events, 155.6 us)
Sparse Core Ops, SparseCore 0:
  9.6 16.3 all-gather.5
  174.0 13.1 reduce-scatter.4
  282.1 15.0 all-gather.7
  354.9 25.1 all-gather.9
  400.8 21.3 reduce-scatter.6
  455.6 21.3 reduce-scatter.8
  629.2 22.0 all-gather.11
  942.0 259.7 all-reduce.3
  1204.1 11.0 reduce-scatter.10
where the time goes:
time: 1240 us; the launch traced here: 1230 us
  matrix products  418 us (34%)
  waiting for transfers between devices  334 us (27%)
  blocking collectives  163 us (13%)
  other arithmetic  157 us (13%)
  local copies, waits for them, and re-layouts  110 us (9%)
  starting transfers between devices  31.8 us (3%)
  between operations  14.7 us (1%)
    all_to_all x2, waiting for transfers between devices, route_grads(): lax.all_to_all(values, 'expert', split_axis=0, concat_axis=0, tiled=True)  112 us
    psum x1, waiting for transfers between devices, on_device(): lax.psum((qkv_part, proj_part, small_pair), 'expert')  109 us
    all_to_all x1, blocking collectives, route(): lax.all_to_all(values, 'expert', split_axis=0, concat_axis=0, tiled=True)  79 us
    psum x1, blocking collectives, on_device(): lax.psum((qkv_part, proj_part, small_pair), 'expert')  78.2 us
    dot_general x4, matrix products, masked_scores(): jnp.einsum('qhd,khd->hqk', query_rows, key_rows, preferred_element_type=j...  64.2 us
    convert_element_type x2, other arithmetic, attend_backward(): grad_scores = (attn_probs * (grad_probs - inner_sum)).astype(jnp.bfloat16)  57.4 us
    all_to_all x1, waiting for transfers between devices, route(): lax.all_to_all(values, 'expert', split_axis=0, concat_axis=0, tiled=True)  56.9 us
    dot_general x2, matrix products, attend_backward(): jnp.einsum('qhd,khd->hqk', grad_att, value_rows, preferred_element_type=j...  52.5 us
  transfers between devices with their start and end apart: 12, of which 9 were waited for; matrix products, arithmetic and copies ran while one was open for 17% of the time, Pallas kernels for 0%

commit v1 on v0

v1 whole, which is shorter than its diff:
```python
import functools

import jax
import jax.numpy as jnp
from jax import lax
from jax.experimental import pallas as pl
from jax.experimental.pallas import tpu as pltpu
from jax.sharding import PartitionSpec as P

HEAD_DIM = 64
SEQ = 1024
DOC_MAX = 512
EPS = 1e-05
QB = 256
CHUNKS = 3
BF = jnp.bfloat16
F32 = jnp.float32
MESH = pl.DeviceIdType.MESH
VMEM_LIMIT = 60 * 1024 * 1024

BLOCKS = SEQ // QB
START = [max(0, i * QB - DOC_MAX) for i in range(BLOCKS)]
WIDTH = [(i + 1) * QB - START[i] for i in range(BLOCKS)]
OFFSET = [sum(WIDTH[:i]) for i in range(BLOCKS)]
BAND = sum(WIDTH)


def dot(a, b):
    return jnp.dot(a, b, preferred_element_type=F32)


def dot_nt(a, b):
    return lax.dot_general(a, b, (((1,), (1,)), ((), ())), preferred_element_type=F32)


def dot_tn(a, b):
    return lax.dot_general(a, b, (((0,), (0,)), ((), ())), preferred_element_type=F32)


def params(**kw):
    return pltpu.CompilerParams(vmem_limit_bytes=VMEM_LIMIT, **kw)


def cost(flops, nbytes, trans=0):
    return pl.CostEstimate(flops=int(flops), bytes_accessed=int(nbytes), transcendentals=int(trans))


ANY = pl.BlockSpec(memory_space=pl.ANY)


def whole(shape):
    return pl.BlockSpec(shape, lambda *_: (0,) * len(shape))


class SideRoute:
    def __init__(self, n, pairs, sems):
        self.n, self.pairs = n, pairs
        self.send, self.recv, self.local = sems

    def copies(self):
        me = lax.axis_index("expert")
        for j, (src, dst) in enumerate(self.pairs):
            for d in range(1, self.n):
                there = lax.rem(me + d, self.n)
                yield pltpu.make_async_remote_copy(
                    src(there), dst(me), self.send.at[j, d], self.recv.at[j, d],
                    device_id={"expert": there}, device_id_type=MESH,
                )

    def own(self):
        me = lax.axis_index("expert")
        for j, (src, dst) in enumerate(self.pairs):
            yield pltpu.make_async_copy(src(me), dst(me), self.local.at[j])

    def start(self):
        me = lax.axis_index("expert")
        barrier = pltpu.get_barrier_semaphore()
        for d in range(1, self.n):
            pl.semaphore_signal(
                barrier, inc=1, device_id={"expert": lax.rem(me + d, self.n)}, device_id_type=MESH
            )
        pl.semaphore_wait(barrier, self.n - 1)
        for c in self.copies():
            c.start()
        for c in self.own():
            c.start()

    def wait(self):
        for c in self.own():
            c.wait()
        for c in self.copies():
            c.wait()


def route_sems(n, count):
    return [
        pltpu.SemaphoreType.DMA((count, n)),
        pltpu.SemaphoreType.DMA((count, n)),
        pltpu.SemaphoreType.DMA((count,)),
    ]


def slots_kernel(cc, rows, ids_ref, val_ref, tcol_ref, trow_ref, out_ref, row_s):
    step = pl.program_id(0)
    tokens = ids_ref.shape[0]

    @pl.when(step == 0)
    def _():
        ids = ids_ref[...]
        hot = (ids == lax.broadcasted_iota(jnp.int32, (tokens, 128), 1)).astype(F32)
        lower = (
            lax.broadcasted_iota(jnp.int32, (tokens, tokens), 0)
            >= lax.broadcasted_iota(jnp.int32, (tokens, tokens), 1)
        ).astype(F32).astype(BF)
        counts = dot(lower, hot.astype(BF))
        rank = jnp.sum(counts * hot, axis=1, keepdims=True) - 1.0
        chunk = jnp.floor((rank + 0.5) * (1.0 / cc))
        place = chunk * rows + ids.astype(F32) * cc + (rank - chunk * cc)
        place = jnp.broadcast_to(place, (tokens, 128))
        tcol_ref[...] = place.astype(jnp.int32)
        flat = jnp.transpose(place)[0:8, :].astype(jnp.int32)
        trow_ref[...] = flat
        row_s[...] = flat

    block = out_ref.shape[0]
    hot = (
        lax.broadcasted_iota(jnp.int32, (block, tokens), 0) + step * block == row_s[0:1, :]
    ).astype(F32).astype(BF)
    out_ref[...] = dot(hot, val_ref[...]).astype(BF)


def slots_call(ids, values, cc, rows):
    tokens, width = values.shape
    total = CHUNKS * rows
    block = 256
    return pl.pallas_call(
        functools.partial(slots_kernel, cc, rows),
        grid=(total // block,),
        in_specs=[whole((tokens, 1)), whole((tokens, width))],
        out_specs=[
            whole((tokens, 128)),
            whole((8, tokens)),
            pl.BlockSpec((block, width), lambda i: (i, 0)),
        ],
        out_shape=[
            jax.ShapeDtypeStruct((tokens, 128), jnp.int32),
            jax.ShapeDtypeStruct((8, tokens), jnp.int32),
            jax.ShapeDtypeStruct((total, width), BF),
        ],
        scratch_shapes=[pltpu.VMEM((8, tokens), jnp.int32)],
        compiler_params=params(),
        cost_estimate=cost(2 * total * tokens * width, 8e6),
        name="slots",
    )(ids, values)


def unit_of(values):
    centre = values - jnp.mean(values, axis=-1, keepdims=True)
    inverse = lax.rsqrt(jnp.mean(centre * centre, axis=-1, keepdims=True) + EPS)
    return centre * inverse, inverse


def heads_kernel(x_ref, own_ref, oth_ref, gain_ref, shift_ref, norm_ref, out_ref, norm_s):
    step = pl.program_id(0)
    tokens = x_ref.shape[0]

    @pl.when(step == 0)
    def _():
        gain, shift = gain_ref[...].astype(F32), shift_ref[...].astype(F32)

        def body(b, _):
            at = pl.ds(b * 128, 128)
            unit, _ = unit_of(x_ref[at, :].astype(F32))
            low = (unit * gain + shift).astype(BF)
            norm_s[at, :] = low
            norm_ref[at, :] = low
            return 0

        lax.fori_loop(0, tokens // 128, body, 0)

    @pl.when(step < 3)
    def _():
        out_ref[0] = dot(norm_s[...], own_ref[0]).astype(BF)

    @pl.when(step >= 3)
    def _():
        out_ref[0] = dot(norm_s[...], oth_ref[0]).astype(BF)


def heads_call(x, own, oth, gain, shift):
    tokens, width = x.shape
    half = own.shape[2]
    return pl.pallas_call(
        heads_kernel,
        grid=(6,),
        in_specs=[
            whole((tokens, width)),
            pl.BlockSpec((1, width, half), lambda i: (jnp.minimum(i, 2), 0, 0)),
            pl.BlockSpec((1, width, half), lambda i: (jnp.maximum(i - 3, 0), 0, 0)),
            whole((1, width)),
            whole((1, width)),
        ],
        out_specs=[whole((tokens, width)), pl.BlockSpec((1, tokens, half), lambda i: (i, 0, 0))],
        out_shape=[
            jax.ShapeDtypeStruct((tokens, width), BF),
            jax.ShapeDtypeStruct((6, tokens, half), BF),
        ],
        scratch_shapes=[pltpu.VMEM((tokens, width), BF)],
        compiler_params=params(),
        cost_estimate=cost(2 * tokens * width * 6 * half, 18e6),
        name="head_rows",
    )(x, own, oth, gain, shift)


def lane_pick(width, first):
    lanes = lax.broadcasted_iota(jnp.int32, (1, width), 1)
    return (lanes < HEAD_DIM) if first else (lanes >= HEAD_DIM)


def attend_kernel(
    n, pairs, x_ref, seg_ref, q_ref, k_ref, v_ref, own_ref, oth_ref, pbias_ref, gain_ref, shift_ref,
    trow_ref, cot_ref, att_ref, prob_ref, mid_ref, slot_ref, arr_ref, bias_s, low_s, send, recv, local,
):
    step = pl.program_id(0)
    tokens = x_ref.shape[0]
    route = SideRoute(
        n, [(lambda e: cot_ref.at[:, e], lambda e: arr_ref.at[:, e])], (send, recv, local)
    )

    @pl.when(step == 0)
    def _():
        route.start()
        seg = seg_ref[...].astype(F32)
        seg_col = jnp.transpose(jnp.broadcast_to(seg, (128, tokens)))
        for i in range(BLOCKS):
            w, s = WIDTH[i], START[i]
            rows = lax.broadcasted_iota(jnp.int32, (QB, w), 0) + i * QB
            keys = lax.broadcasted_iota(jnp.int32, (QB, w), 1) + s
            same = seg_col[i * QB:(i + 1) * QB, 0:1] == seg[:, s:s + w]
            bias_s[:, OFFSET[i]:OFFSET[i] + w] = jnp.where(same & (keys <= rows), 0.0, -1e30)

    @pl.when(step < pairs)
    def _():
        query = q_ref[0] * BF(HEAD_DIM ** -0.5)
        for i in range(BLOCKS):
            w, s = WIDTH[i], START[i]
            keys, values = k_ref[0, s:s + w, :], v_ref[0, s:s + w, :]
            bias = bias_s[:, OFFSET[i]:OFFSET[i] + w]
            parts = []
            for j in range(2):
                q = jnp.where(lane_pick(128, j == 0), query[i * QB:(i + 1) * QB], BF(0))
                scores = dot_nt(q, keys) + bias
                top = jnp.max(scores, axis=-1, keepdims=True)
                weights = jnp.exp(scores - top)
                probs = (weights * (1.0 / jnp.sum(weights, axis=-1, keepdims=True))).astype(BF)
                prob_ref[j, :, OFFSET[i]:OFFSET[i] + w] = probs
                parts.append(dot(probs, values))
            both = jnp.where(lane_pick(128, True), parts[0], parts[1])
            att_ref[i * QB:(i + 1) * QB, pl.ds(pl.multiple_of(step * 128, 128), 128)] = both.astype(BF)

    @pl.when(step == pairs)
    def _():
        pbias = pbias_ref[...].astype(F32)
        gain, shift = gain_ref[...].astype(F32), shift_ref[...].astype(F32)
        half = own_ref.shape[0]

        def body(b, _):
            at = pl.ds(b * 128, 128)
            branch = dot(att_ref[at, 0:half], own_ref[...]) + dot(att_ref[at, half:2 * half], oth_ref[...])
            middle = x_ref[at, :].astype(F32) + branch + pbias
            mid_ref[at, :] = middle
            unit, _ = unit_of(middle)
            low_s[at, :] = (unit * gain + shift).astype(BF)
            return 0

        lax.fori_loop(0, tokens // 128, body, 0)

        def place(b, _):
            hot = (
                lax.broadcasted_iota(jnp.int32, (256, tokens), 0) + b * 256 == trow_ref[0:1, :]
            ).astype(F32).astype(BF)
            slot_ref[pl.ds(b * 256, 256), :] = dot(hot, low_s[...]).astype(BF)
            return 0

        lax.fori_loop(0, slot_ref.shape[0] // 256, place, 0)
        route.wait()


def attend_call(n, x, seg, head_rows, proj_own, proj_oth, pbias, gain, shift, trow, cot_slots):
    tokens, width = x.shape
    half = proj_own.shape[0]
    pairs = width // 128
    per = half // 128
    slots = cot_slots.shape[1] * cot_slots.shape[2] * CHUNKS

    def head(c):
        def index(h):
            h = jnp.minimum(h, pairs - 1)
            return (3 * (h // per) + c, 0, h % per)

        return pl.BlockSpec((1, tokens, 128), index)

    return pl.pallas_call(
        functools.partial(attend_kernel, n, pairs),
        grid=(pairs + 1,),
        in_specs=[
            whole((tokens, width)), whole((1, tokens)), head(0), head(1), head(2),
            whole((half, width)), whole((half, width)), whole((1, width)), whole((1, width)),
            whole((1, width)), whole((8, tokens)), ANY,
        ],
        out_specs=[
            whole((tokens, width)),
            pl.BlockSpec((2, QB, BAND), lambda h: (jnp.minimum(h, pairs - 1), 0, 0)),
            whole((tokens, width)),
            whole((slots, width)),
            ANY,
        ],
        out_shape=[
            jax.ShapeDtypeStruct((tokens, width), BF),
            jax.ShapeDtypeStruct((2 * pairs, QB, BAND), BF),
            jax.ShapeDtypeStruct((tokens, width), F32),
            jax.ShapeDtypeStruct((slots, width), BF),
            jax.ShapeDtypeStruct(cot_slots.shape, BF),
        ],
        scratch_shapes=[
            pltpu.VMEM((QB, BAND), F32), pltpu.VMEM((tokens, width), BF), *route_sems(n, 1),
        ],
        compiler_params=params(collective_id=1, has_side_effects=True),
        cost_estimate=cost(2e10, 5e7),
        name="attend",
    )(x, seg, head_rows, head_rows, head_rows, proj_own, proj_oth, pbias, gain, shift, trow, cot_slots)


def route_kernel(n, chunk, src_ref, dst_ref, send, recv, local):
    route = SideRoute(
        n, [(lambda e: src_ref.at[chunk, e], lambda e: dst_ref.at[e])], (send, recv, local)
    )
    route.start()
    route.wait()


def route_call(n, src, chunk, cid):
    return pl.pallas_call(
        functools.partial(route_kernel, n, chunk),
        in_specs=[ANY],
        out_specs=ANY,
        out_shape=jax.ShapeDtypeStruct(src.shape[1:], BF),
        scratch_shapes=route_sems(n, 1),
        compiler_params=params(collective_id=cid, has_side_effects=True),
        name="route",
    )(src)


GELU_C = 0.7978845608028654
GELU_A = 0.044715


def expert_kernel(
    n, has_mid, has_back, tiles, x_ref, c_ref, uo_ref, ut_ref, do_ref, dt_ref, bo_ref, bt_ref, db_ref, *rest
):
    rest = list(rest)
    pairs = []
    mid_src = rest.pop(0) if has_mid is not None else None
    back_src = rest.pop(0) if has_back else None
    act_ref, gh_ref, ub_ref, y_ref, dx_ref = rest[:5]
    rest = rest[5:]
    mid_dst = rest.pop(0) if has_mid is not None else None
    back_dst = rest.pop(0) if has_back else None
    y_s, dx_s = rest[:2]
    sems = rest[2:]
    if has_mid is not None:
        pairs.append((lambda e: mid_src.at[has_mid, e], lambda e: mid_dst.at[e]))
    if has_back:
        pairs.append((lambda e: back_src.at[e], lambda e: back_dst.at[e]))
    route = SideRoute(n, pairs, sems)
    step = pl.program_id(0)

    @pl.when(step == 0)
    def _():
        route.start()
        y_s[...] = jnp.broadcast_to(db_ref[...].astype(F32), y_s.shape)
        dx_s[...] = jnp.zeros_like(dx_s)

    def work(up_ref, down_ref, b_ref):
        rows, cot = x_ref[...], c_ref[0]
        up, down = up_ref[...], down_ref[...]
        h = dot_nt(rows, up) + b_ref[...].astype(F32)
        g = dot_nt(cot, down)
        sq = h * h
        t = jnp.tanh(GELU_C * (h + GELU_A * (sq * h)))
        act = ((0.5 * h) * (1.0 + t)).astype(BF)
        act_ref[...] = act
        slope = 0.5 * (1.0 + t) + (0.5 * h) * ((1.0 - t * t) * (GELU_C * (1.0 + (3.0 * GELU_A) * sq)))
        gh = (g * slope).astype(BF)
        gh_ref[...] = gh
        ub_ref[...] = jnp.broadcast_to(jnp.sum(gh.astype(F32), axis=0, keepdims=True), ub_ref.shape)
        y_s[...] += dot(act, down)
        dx_s[...] += dot(gh, up)

    @pl.when(step < tiles // 2)
    def _():
        work(uo_ref, do_ref, bo_ref)

    @pl.when(step >= tiles // 2)
    def _():
        work(ut_ref, dt_ref, bt_ref)

    @pl.when(step == tiles - 1)
    def _():
        y_ref[...] = y_s[...].astype(BF)
        dx_ref[...] = dx_s[...].astype(BF)
        route.wait()


def expert_call(n, chunk, rows, cot, up, down, bias, down_bias, mid=None, mid_chunk=None, back=None, cid=0):
    up_own, up_oth = up
    down_own, down_oth = down
    b_own, b_oth = bias
    r, width = rows.shape
    hid = up_own.shape[0]
    ft = 512
    own_tiles = hid // ft
    tiles = 2 * own_tiles

    def first(i):
        return jnp.minimum(i, own_tiles - 1)

    def second(i):
        return jnp.maximum(i - own_tiles, 0)

    in_specs = [
        whole((r, width)),
        pl.BlockSpec((1, r, width), lambda i: (chunk, 0, 0)),
        pl.BlockSpec((ft, width), lambda i: (first(i), 0)),
        pl.BlockSpec((ft, width), lambda i: (second(i), 0)),
        pl.BlockSpec((ft, width), lambda i: (first(i), 0)),
        pl.BlockSpec((ft, width), lambda i: (second(i), 0)),
        pl.BlockSpec((1, ft), lambda i: (0, first(i))),
        pl.BlockSpec((1, ft), lambda i: (0, second(i))),
        whole((1, width)),
    ]
    args = [rows, cot, up_own, up_oth, down_own, down_oth, b_own, b_oth, down_bias]
    out_specs = [
        pl.BlockSpec((r, ft), lambda i: (0, i)),
        pl.BlockSpec((r, ft), lambda i: (0, i)),
        pl.BlockSpec((8, ft), lambda i: (0, i)),
        whole((r, width)),
        whole((r, width)),
    ]
    out_shape = [
        jax.ShapeDtypeStruct((r, 2 * hid), BF),
        jax.ShapeDtypeStruct((r, 2 * hid), BF),
        jax.ShapeDtypeStruct((8, 2 * hid), F32),
        jax.ShapeDtypeStruct((r, width), BF),
        jax.ShapeDtypeStruct((r, width), BF),
    ]
    count = 0
    if mid is not None:
        in_specs.append(ANY)
        args.append(mid)
        out_specs.append(ANY)
        out_shape.append(jax.ShapeDtypeStruct(mid.shape[1:], BF))
        count += 1
    if back is not None:
        in_specs.append(ANY)
        args.append(back)
        out_specs.append(ANY)
        out_shape.append(jax.ShapeDtypeStruct(back.shape, BF))
        count += 1
    return pl.pallas_call(
        functools.partial(expert_kernel, n, mid_chunk if mid is not None else None, back is not None, tiles),
        grid=(tiles,),
        in_specs=in_specs,
        out_specs=out_specs,
        out_shape=out_shape,
        scratch_shapes=[pltpu.VMEM((r, width), F32), pltpu.VMEM((r, width), F32), *route_sems(n, count)],
        compiler_params=params(collective_id=cid, has_side_effects=True),
        cost_estimate=cost(8 * r * width * 2 * hid, 3e7),
        name="experts",
    )(*args)


def wgrad_oth_kernel(n, tiles, a0, a1, a2, g0, g1, g2, c_ref, x0, x1, x2, back_src, do_ref, up_ref, cb_ref, back_dst, *sems):
    route = SideRoute(n, [(lambda e: back_src.at[e], lambda e: back_dst.at[e])], sems)
    step = pl.program_id(0)

    @pl.when(step == 0)
    def _():
        route.start()
        total = jnp.zeros((1, c_ref.shape[2]), F32)
        for c in range(CHUNKS):
            total = total + jnp.sum(c_ref[c].astype(F32), axis=0, keepdims=True)
        cb_ref[...] = jnp.broadcast_to(total, cb_ref.shape)

    @pl.when(step < tiles)
    def _():
        s = dot_tn(a0[...], c_ref[0]) + dot_tn(a1[...], c_ref[1]) + dot_tn(a2[...], c_ref[2])
        do_ref[...] = s.astype(BF)

    @pl.when(step >= tiles)
    def _():
        s = dot_tn(g0[...], x0[...]) + dot_tn(g1[...], x1[...]) + dot_tn(g2[...], x2[...])
        up_ref[...] = s.astype(BF)

    @pl.when(step == 2 * tiles - 1)
    def _():
        route.wait()


def wgrad_oth_call(n, acts, ghs, cot, rows, back, cid):
    r, width = rows[0].shape
    hid = acts[0].shape[1] // 2
    ft = 512
    tiles = hid // ft

    def first(i):
        return jnp.minimum(i, tiles - 1)

    def second(i):
        return jnp.maximum(i - tiles, 0)

    a_spec = pl.BlockSpec((r, ft), lambda i: (0, tiles + first(i)))
    g_spec = pl.BlockSpec((r, ft), lambda i: (0, tiles + second(i)))
    return pl.pallas_call(
        functools.partial(wgrad_oth_kernel, n, tiles),
        grid=(2 * tiles,),
        in_specs=[a_spec] * 3 + [g_spec] * 3 + [whole(cot.shape)] + [whole((r, width))] * 3 + [ANY],
        out_specs=[
            pl.BlockSpec((ft, width), lambda i: (first(i), 0)),
            pl.BlockSpec((ft, width), lambda i: (second(i), 0)),
            whole((8, width)),
            ANY,
        ],
        out_shape=[
            jax.ShapeDtypeStruct((hid, width), BF),
            jax.ShapeDtypeStruct((hid, width), BF),
            jax.ShapeDtypeStruct((8, width), F32),
            jax.ShapeDtypeStruct(back.shape, BF),
        ],
        scratch_shapes=route_sems(n, 1),
        compiler_params=params(collective_id=cid, has_side_effects=True),
        cost_estimate=cost(4 * 3 * r * hid * width, 4e7),
        name="weight_grads_other",
    )(*acts, *ghs, cot, *rows, back)


def wgrad_own_kernel(tiles, a0, a1, a2, g0, g1, g2, c_ref, x0, x1, x2, rd_ref, ru_ref, do_ref, up_ref):
    step = pl.program_id(0)

    @pl.when(step < tiles)
    def _():
        s = dot_tn(a0[...], c_ref[0]) + dot_tn(a1[...], c_ref[1]) + dot_tn(a2[...], c_ref[2])
        do_ref[...] = s + rd_ref[...].astype(F32)

    @pl.when(step >= tiles)
    def _():
        s = dot_tn(g0[...], x0[...]) + dot_tn(g1[...], x1[...]) + dot_tn(g2[...], x2[...])
        up_ref[...] = s + ru_ref[...].astype(F32)


def wgrad_own_call(acts, ghs, cot, rows, got_down, got_up):
    r, width = rows[0].shape
    hid = acts[0].shape[1] // 2
    ft = 512
    tiles = hid // ft

    def first(i):
        return jnp.minimum(i, tiles - 1)

    def second(i):
        return jnp.maximum(i - tiles, 0)

    a_spec = pl.BlockSpec((r, ft), lambda i: (0, first(i)))
    g_spec = pl.BlockSpec((r, ft), lambda i: (0, second(i)))
    d_spec = pl.BlockSpec((ft, width), lambda i: (first(i), 0))
    u_spec = pl.BlockSpec((ft, width), lambda i: (second(i), 0))
    return pl.pallas_call(
        functools.partial(wgrad_own_kernel, tiles),
        grid=(2 * tiles,),
        in_specs=[a_spec] * 3 + [g_spec] * 3 + [whole(cot.shape)] + [whole((r, width))] * 3 + [d_spec, u_spec],
        out_specs=[d_spec, u_spec],
        out_shape=[jax.ShapeDtypeStruct((hid, width), F32), jax.ShapeDtypeStruct((hid, width), F32)],
        compiler_params=params(),
        cost_estimate=cost(4 * 3 * r * hid * width, 6e7),
        name="weight_grads_own",
    )(*acts, *ghs, cot, *rows, got_down, got_up)


def gather_rows(tcol, parts):
    rows = parts[0].shape[0]
    total = None
    for c, part in enumerate(parts):
        hot = (
            lax.broadcasted_iota(jnp.int32, (tcol.shape[0], rows), 1) + c * rows == tcol[:, 0:1]
        ).astype(F32).astype(BF)
        term = dot(hot, part[...])
        total = term if total is None else total + term
    return total


def middle_back_kernel(
    n, blocks, tcol_ref, g0, g1, g2, mid_ref, cot_ref, gain_ref, own_ref, oth_ref, att_ref, y_src,
    gmid_ref, gatt_ref, pg_own, pg_oth, small_ref, y_dst, gb_s, send, recv, local,
):
    route = SideRoute(n, [(lambda e: y_src.at[e], lambda e: y_dst.at[e])], (send, recv, local))
    step = pl.program_id(0)
    half = own_ref.shape[0]
    tb, width = mid_ref.shape

    @pl.when(step == 0)
    def _():
        route.start()
        small_ref[...] = jnp.zeros_like(small_ref)

    grad = gather_rows(tcol_ref[...], (g0, g1, g2))
    grad = grad.astype(BF).astype(F32)
    unit, inverse = unit_of(mid_ref[...])
    scaled = grad * gain_ref[...].astype(F32)
    inner = jnp.mean(scaled, axis=-1, keepdims=True)
    along = jnp.mean(scaled * unit, axis=-1, keepdims=True)
    gmid = cot_ref[...].astype(F32) + inverse * (scaled - inner - unit * along)
    gmid_ref[...] = gmid
    gb = gmid.astype(BF)
    gb_s[pl.ds(pl.multiple_of(step * tb, tb), tb), :] = gb
    small_ref[0:1, :] += jnp.sum(grad * unit, axis=0, keepdims=True)
    small_ref[1:2, :] += jnp.sum(grad, axis=0, keepdims=True)
    small_ref[2:3, :] += jnp.sum(gb.astype(F32), axis=0, keepdims=True)
    gatt_ref[:, 0:half] = dot_nt(gb, own_ref[...]).astype(BF)
    gatt_ref[:, half:2 * half] = dot_nt(gb, oth_ref[...]).astype(BF)

    @pl.when(step == blocks - 1)
    def _():
        pg_own[...] = dot_tn(att_ref[:, 0:half], gb_s[...])
        pg_oth[...] = dot_tn(att_ref[:, half:2 * half], gb_s[...]).astype(BF)
        route.wait()


def middle_back_call(n, tcol, grads, middle, cot, gain, proj_own, proj_oth, att, y, cid):
    tokens, width = middle.shape
    half = proj_own.shape[0]
    tb = 256
    rows = grads[0].shape[0]
    block = pl.BlockSpec((tb, width), lambda i: (i, 0))
    return pl.pallas_call(
        functools.partial(middle_back_kernel, n, tokens // tb),
        grid=(tokens // tb,),
        in_specs=[
            pl.BlockSpec((tb, 128), lambda i: (i, 0)), *[whole((rows, width))] * 3, block, block,
            whole((1, width)), whole((half, width)), whole((half, width)), whole((tokens, width)), ANY,
        ],
        out_specs=[block, block, whole((half, width)), whole((half, width)), whole((8, width)), ANY],
        out_shape=[
            jax.ShapeDtypeStruct((tokens, width), F32),
            jax.ShapeDtypeStruct((tokens, width), BF),
            jax.ShapeDtypeStruct((half, width), F32),
            jax.ShapeDtypeStruct((half, width), BF),
            jax.ShapeDtypeStruct((8, width), F32),
            jax.ShapeDtypeStruct(y.shape, BF),
        ],
        scratch_shapes=[pltpu.VMEM((tokens, width), BF), *route_sems(n, 1)],
        compiler_params=params(collective_id=cid, has_side_effects=True),
        cost_estimate=cost(1.2e10, 3e7),
        name="middle_back",
    )(tcol, *grads, middle, cot, gain, proj_own, proj_oth, att, y)


def attend_back_kernel(
    n, pairs, q_ref, k_ref, v_ref, prob_ref, do_ref, o_ref, y_src, dq_ref, dk_ref, dv_ref, y_dst,
    dk_s, dv_s, send, recv, local,
):
    route = SideRoute(n, [(lambda e: y_src.at[e], lambda e: y_dst.at[e])], (send, recv, local))
    step = pl.program_id(0)
    scale = HEAD_DIM ** -0.5

    @pl.when(step == 0)
    def _():
        route.start()

    dk_s[...] = jnp.zeros_like(dk_s)
    dv_s[...] = jnp.zeros_like(dv_s)
    for i in range(BLOCKS):
        w, s = WIDTH[i], START[i]
        at = slice(i * QB, (i + 1) * QB)
        keys, values = k_ref[0, s:s + w, :], v_ref[0, s:s + w, :]
        go = do_ref[at, :]
        prod = go.astype(F32) * o_ref[at, :].astype(F32)
        query = q_ref[0, at, :]
        parts = []
        for j in range(2):
            pick = lane_pick(128, j == 0)
            go_j = jnp.where(pick, go, BF(0))
            q_j = jnp.where(pick, query, BF(0))
            inner = jnp.sum(jnp.where(pick, prod, 0.0), axis=-1, keepdims=True)
            probs = prob_ref[j, :, OFFSET[i]:OFFSET[i] + w]
            gp = dot_nt(go_j, values)
            gs = (probs.astype(F32) * (gp - inner)).astype(BF)
            parts.append(dot(gs, keys))
            dk_s[s:s + w, :] += dot_tn(gs, q_j)
            dv_s[s:s + w, :] += dot_tn(probs, go_j)
        dq_ref[0, at, :] = (jnp.where(lane_pick(128, True), parts[0], parts[1]) * scale).astype(BF)
    dk_ref[0] = (dk_s[...] * scale).astype(BF)
    dv_ref[0] = dv_s[...].astype(BF)

    @pl.when(step == pairs - 1)
    def _():
        route.wait()


def attend_back_call(n, head_rows, probs, gatt, att, y, cid):
    tokens, width = gatt.shape
    half = head_rows.shape[2]
    pairs, per = width // 128, half // 128

    def head(c):
        return pl.BlockSpec((1, tokens, 128), lambda h: (3 * (h // per) + c, 0, h % per))

    cols = pl.BlockSpec((tokens, 128), lambda h: (0, h))
    out = pl.BlockSpec((1, tokens, 128), lambda h: (h // per, 0, h % per))
    shape = jax.ShapeDtypeStruct((2, tokens, half), BF)
    return pl.pallas_call(
        functools.partial(attend_back_kernel, n, pairs),
        grid=(pairs,),
        in_specs=[
            head(0), head(1), head(2), pl.BlockSpec((2, QB, BAND), lambda h: (h, 0, 0)), cols, cols, ANY,
        ],
        out_specs=[out, out, out, ANY],
        out_shape=[shape, shape, shape, jax.ShapeDtypeStruct(y.shape, BF)],
        scratch_shapes=[pltpu.VMEM((tokens, 128), F32), pltpu.VMEM((tokens, 128), F32), *route_sems(n, 1)],
        compiler_params=params(collective_id=cid, has_side_effects=True),
        cost_estimate=cost(4e10, 4e7),
        name="attend_back",
    )(head_rows, head_rows, head_rows, probs, gatt, att, y)


def heads_back_kernel(
    n, x_ref, norm_ref, gq, gk, gv, own_ref, oth_ref, gmid_ref, gain_ref, y_src,
    qg_own, qg_oth, xg_ref, small_ref, y_dst, acc_s, send, recv, local,
):
    route = SideRoute(n, [(lambda e: y_src.at[e], lambda e: y_dst.at[e])], (send, recv, local))
    step = pl.program_id(0)
    tokens, width = x_ref.shape

    @pl.when(step == 0)
    def _():
        route.start()
        acc_s[...] = jnp.zeros_like(acc_s)

    for c, g_ref in enumerate((gq, gk, gv)):
        @pl.when(step == c)
        def _():
            qg_own[0] = dot_tn(norm_ref[...], g_ref[0])
            acc_s[...] += dot_nt(g_ref[0], own_ref[0])

        @pl.when(step == 3 + c)
        def _():
            qg_oth[0] = dot_tn(norm_ref[...], g_ref[0]).astype(BF)
            acc_s[...] += dot_nt(g_ref[0], oth_ref[0])

    @pl.when(step == 5)
    def _():
        small_ref[...] = jnp.zeros_like(small_ref)
        gain = gain_ref[...].astype(F32)

        def body(b, _):
            at = pl.ds(b * 128, 128)
            grad = acc_s[at, :]
            unit, inverse = unit_of(x_ref[at, :].astype(F32))
            scaled = grad * gain
            inner = jnp.mean(scaled, axis=-1, keepdims=True)
            along = jnp.mean(scaled * unit, axis=-1, keepdims=True)
            xg_ref[at, :] = gmid_ref[at, :] + inverse * (scaled - inner - unit * along)
            small_ref[0:1, :] += jnp.sum(grad * unit, axis=0, keepdims=True)
            small_ref[1:2, :] += jnp.sum(grad, axis=0, keepdims=True)
            return 0

        lax.fori_loop(0, tokens // 128, body, 0)
        route.wait()


def heads_back_call(n, x, norm, grads, own, oth, gmid, gain, y, cid):
    tokens, width = x.shape
    half = own.shape[2]
    g_spec = pl.BlockSpec((1, tokens, half), lambda i: (i // 3, 0, 0))
    first = pl.BlockSpec((1, width, half), lambda i: (jnp.minimum(i, 2), 0, 0))
    second = pl.BlockSpec((1, width, half), lambda i: (jnp.maximum(i - 3, 0), 0, 0))
    return pl.pallas_call(
        functools.partial(heads_back_kernel, n),
        grid=(6,),
        in_specs=[
            whole((tokens, width)), whole((tokens, width)), g_spec, g_spec, g_spec, first, second,
            whole((tokens, width)), whole((1, width)), ANY,
        ],
        out_specs=[first, second, whole((tokens, width)), whole((8, width)), ANY],
        out_shape=[
            jax.ShapeDtypeStruct((3, width, half), F32),
            jax.ShapeDtypeStruct((3, width, half), BF),
            jax.ShapeDtypeStruct((tokens, width), F32),
            jax.ShapeDtypeStruct((8, width), F32),
            jax.ShapeDtypeStruct(y.shape, BF),
        ],
        scratch_shapes=[pltpu.VMEM((tokens, width), F32), *route_sems(n, 1)],
        compiler_params=params(collective_id=cid, has_side_effects=True),
        cost_estimate=cost(1.3e10, 5e7),
        name="heads_back",
    )(x, norm, *grads, own, oth, gmid, gain, y)


def total_kernel(
    n, q_own, p_own, small_ref, q_oth, p_oth, q_out, p_out, small_out,
    acc, snd, rcv, res, q_got, p_got, small_got, dp_send, dp_recv, rs_send, rs_recv, ag_send, ag_recv, sm_send, sm_recv,
):
    me, core = lax.axis_index("expert"), lax.axis_index("dp")
    width, half = q_own.shape[1], q_own.shape[2]
    rows = acc.shape[0]
    bits = [1 << i for i in range(n.bit_length() - 1)]
    peers = [{"dp": 1 - core}] + [
        {"expert": me + b - 2 * b * lax.rem(lax.div(me, b), 2)} for b in bits
    ]
    barrier = pltpu.get_barrier_semaphore()
    for peer in peers:
        pl.semaphore_signal(barrier, inc=1, device_id=peer, device_id_type=MESH)
    pl.semaphore_wait(barrier, len(peers))

    def send(src, dst, s, r, peer):
        c = pltpu.make_async_remote_copy(src, dst, s, r, device_id=peer, device_id_type=MESH)
        c.start()
        return c

    first = [
        send(p_oth, p_got, dp_send.at[0], dp_recv.at[0], peers[0]),
        *[send(q_oth.at[c], q_got.at[c], dp_send.at[1 + c], dp_recv.at[1 + c], peers[0]) for c in range(3)],
    ]
    small_out[...] = small_ref[...]
    small_copy = send(small_out, small_got.at[0], sm_send.at[0], sm_recv.at[0], peers[0])

    first[0].wait()
    for b in range(width // half):
        acc[3 * width + b * half:3 * width + (b + 1) * half, :] = (
            p_own[:, b * half:(b + 1) * half] + p_got[:, b * half:(b + 1) * half].astype(F32)
        )
    for c in range(3):
        first[1 + c].wait()

        def add(b, _):
            acc[pl.ds(c * width + b * 128, 128), :] = (
                q_own[c, pl.ds(b * 128, 128), :] + q_got[c, pl.ds(b * 128, 128), :].astype(F32)
            )
            return 0

        lax.fori_loop(0, width // 128, add, 0)
    small_copy.wait()
    small_out[...] += small_got[0]

    units = rows // (16 * n)
    shares = [units // 3, units // 3, units - 2 * (units // 3)]
    order = [[(p + s) % 3 if s < 3 else s for s in range(len(bits))] if len(bits) > 3 else
             [(p + s) % len(bits) for s in range(len(bits))] for p in range(3)]
    base = [0, shares[0] * 16 * n, (shares[0] + shares[1]) * 16 * n]
    length = [share * 16 * n for share in shares]
    start = [jnp.int32(b) for b in base]
    used = list(base)

    def aligned(v):
        return pl.multiple_of(v, 16)

    for s in range(len(bits)):
        copies = []
        for p in range(3):
            if shares[p] == 0:
                continue
            k = order[p][s]
            up = lax.rem(lax.div(me, bits[k]), 2)
            hl = length[p] // 2
            step = shares[p] * 16
            away = start[p] + (1 - up) * hl
            keep = start[p] + up * hl
            slot = used[p]

            def pack(b, _):
                snd[pl.ds(aligned(slot + b * step), step), :] = acc[pl.ds(aligned(away + b * step), step), :].astype(BF)
                return 0

            lax.fori_loop(0, hl // step, pack, 0)
            copies.append((p, keep, hl, step, slot, send(
                snd.at[pl.ds(slot, hl)], rcv.at[pl.ds(slot, hl)], rs_send.at[s, p], rs_recv.at[s, p], peers[1 + k])))
        small_copy = send(small_out, small_got.at[1 + s], sm_send.at[1 + s], sm_recv.at[1 + s], peers[1 + s])
        for p, keep, hl, step, slot, copy in copies:
            copy.wait()

            def add(b, _):
                at = pl.ds(aligned(keep + b * step), step)
                acc[at, :] = acc[at, :] + rcv[pl.ds(aligned(slot + b * step), step), :].astype(F32)
                return 0

            lax.fori_loop(0, hl // step, add, 0)
            start[p], length[p], used[p] = keep, hl, slot + hl
        small_copy.wait()
        small_out[...] += small_got[1 + s]

    for p in range(3):
        if shares[p]:
            at = pl.ds(aligned(start[p]), length[p])
            res[at, :] = acc[at, :].astype(BF)
    for s in reversed(range(len(bits))):
        copies = []
        for p in range(3):
            if shares[p] == 0:
                continue
            k = order[p][s]
            at = pl.ds(aligned(start[p]), length[p])
            copies.append(send(res.at[at], res.at[at], ag_send.at[s, p], ag_recv.at[s, p], peers[1 + k]))
            start[p] = start[p] - lax.rem(lax.div(me, bits[k]), 2) * length[p]
            length[p] = 2 * length[p]
        for copy in copies:
            copy.wait()

    for c in range(3):
        def give(b, _):
            q_out[c, pl.ds(b * 128, 128), :] = res[pl.ds(c * width + b * 128, 128), :].astype(F32)
            return 0

        lax.fori_loop(0, width // 128, give, 0)
    for b in range(width // half):
        p_out[:, b * half:(b + 1) * half] = res[3 * width + b * half:3 * width + (b + 1) * half, :].astype(F32)


def total_call(n, q_own, p_own, small, q_oth, p_oth, cid):
    _, width, half = q_own.shape
    rows = 3 * width + (width // half) * half
    stages = n.bit_length() - 1
    vm = pl.BlockSpec(memory_space=pltpu.VMEM)
    dma = pltpu.SemaphoreType.DMA
    return pl.pallas_call(
        functools.partial(total_kernel, n),
        in_specs=[vm, vm, vm, ANY, ANY],
        out_specs=[vm, vm, vm],
        out_shape=[
            jax.ShapeDtypeStruct(q_own.shape, F32),
            jax.ShapeDtypeStruct(p_own.shape, F32),
            jax.ShapeDtypeStruct(small.shape, F32),
        ],
        scratch_shapes=[
            pltpu.VMEM((rows, half), F32), pltpu.VMEM((rows, half), BF), pltpu.VMEM((rows, half), BF),
            pltpu.VMEM((rows, half), BF), pltpu.VMEM(q_oth.shape, BF), pltpu.VMEM(p_oth.shape, BF),
            pltpu.VMEM((1 + stages, *small.shape), F32), dma((4,)), dma((4,)), dma((stages, 3)), dma((stages, 3)),
            dma((stages, 3)), dma((stages, 3)), dma((1 + stages,)), dma((1 + stages,)),
        ],
        compiler_params=params(collective_id=cid, has_side_effects=True),
        cost_estimate=cost(1e7, 5e7),
        name="totals",
    )(q_own, p_own, small, q_oth, p_oth)


def output_kernel(tcol_ref, y0, y1, y2, mid_ref, out_ref):
    rows = gather_rows(tcol_ref[...], (y0, y1, y2))
    out_ref[...] = (mid_ref[...] + rows.astype(BF).astype(F32)).astype(BF)


def output_call(tcol, ys, middle):
    tokens, width = middle.shape
    tb = 256
    rows = ys[0].shape[0]
    block = pl.BlockSpec((tb, width), lambda i: (i, 0))
    return pl.pallas_call(
        output_kernel,
        grid=(tokens // tb,),
        in_specs=[pl.BlockSpec((tb, 128), lambda i: (i, 0)), *[whole((rows, width))] * 3, block],
        out_specs=block,
        out_shape=jax.ShapeDtypeStruct((tokens, width), BF),
        compiler_params=params(),
        cost_estimate=cost(6 * tokens * rows * width, 1e7),
        name="output",
    )(tcol, *ys, middle)


def on_device(
    tokens, cotangent, segment_ids, expert_ids, qkv_weight, proj_weight, proj_bias, pre_gain, pre_shift,
    mid_gain, mid_shift, up_weight, up_bias, down_weight, down_bias,
):
    n = lax.axis_size("expert")
    count, width = tokens.shape
    cc = 3 * count // (2 * n) // CHUNKS
    rows = n * cc
    row = lambda v: v.reshape(1, -1)

    def swap(v):
        return lax.ppermute(v, "dp", [(0, 1), (1, 0)])

    qkv_oth = swap(qkv_weight)
    proj_oth = swap(proj_weight)
    down_own, up_own, bias_own = down_weight[0], up_weight[0], up_bias
    down_oth, up_oth, bias_oth = swap(down_own), swap(up_own), swap(bias_own)

    tcol, trow, cot_slots = slots_call(expert_ids, cotangent, cc, rows)
    norm, head_rows = heads_call(tokens, qkv_weight, qkv_oth, row(pre_gain), row(pre_shift))
    att, probs, middle, mid_slots, cot_arr = attend_call(
        n, tokens, segment_ids, head_rows, proj_weight, proj_oth, row(proj_bias), row(mid_gain), row(mid_shift),
        trow, cot_slots.reshape(CHUNKS, n, cc, width),
    )
    cot_rows = cot_arr.reshape(CHUNKS, rows, width)
    mid_slots = mid_slots.reshape(CHUNKS, n, cc, width)

    def flat(v):
        return v.reshape(rows, width)

    def routed(v):
        return v.reshape(n, cc, width)

    up, down, bias = (up_own, up_oth), (down_own, down_oth), (bias_own, bias_oth)
    arr0 = flat(route_call(n, mid_slots, 0, 2))
    act0, gh0, ub0, y0, dx0, arr1 = expert_call(
        n, 0, arr0, cot_rows, up, down, bias, down_bias, mid=mid_slots, mid_chunk=1, cid=3)
    arr1 = flat(arr1)
    act1, gh1, ub1, y1, dx1, arr2, gm0 = expert_call(
        n, 1, arr1, cot_rows, up, down, bias, down_bias, mid=mid_slots, mid_chunk=2, back=routed(dx0), cid=4)
    arr2 = flat(arr2)
    act2, gh2, ub2, y2, dx2, gm1 = expert_call(
        n, 2, arr2, cot_rows, up, down, bias, down_bias, back=routed(dx1), cid=5)
    acts, ghs, arrs = (act0, act1, act2), (gh0, gh1, gh2), (arr0, arr1, arr2)
    dw_oth, uw_oth, cot_sum, gm2 = wgrad_oth_call(n, acts, ghs, cot_rows, arrs, routed(dx2), 6)
    hid = down_own.shape[0]
    bias_sum = ub0[0] + ub1[0] + ub2[0]
    got_down, got_up = swap(dw_oth), swap(uw_oth)
    small_oth = swap(jnp.concatenate([bias_sum[hid:], cot_sum[0]]))
    upbias_grad = row(bias_sum[:hid] + small_oth[:hid])
    downbias_grad = row(cot_sum[0] + small_oth[hid:])

    gmid, gatt, pg_own, pg_oth, small_mid, z0 = middle_back_call(
        n, tcol, (flat(gm0), flat(gm1), flat(gm2)), middle, cotangent, row(mid_gain), proj_weight, proj_oth, att,
        routed(y0), 7)
    dq, dk, dv, z1 = attend_back_call(n, head_rows, probs, gatt, att, routed(y1), 8)
    qg_own, qg_oth, input_grad, small_pre, z2 = heads_back_call(
        n, tokens, norm, (dq, dk, dv), qkv_weight, qkv_oth, gmid, row(pre_gain), routed(y2), 9)
    small = jnp.concatenate([small_pre[0:2], small_mid[0:3], jnp.zeros((3, width), F32)], axis=0)
    qkv_grad, proj_grad, small = total_call(n, qg_own, pg_own, small, qg_oth, pg_oth, 10)
    down_grad, up_grad = wgrad_own_call(acts, ghs, cot_rows, arrs, got_down, got_up)
    output = output_call(tcol, (flat(z0), flat(z1), flat(z2)), middle)
    return (
        output, input_grad, qkv_grad, proj_grad, small[4], small[0], small[1], small[2], small[3],
        up_grad[None], upbias_grad, down_grad[None], downbias_grad,
    )


def solution(mesh):
    token = P(("dp", "expert"), None)
    in_specs = (
        token, token, token, token, P(None, None, "dp"), P("dp", None), P(), P(), P(), P(), P(),
        P("expert", "dp", None), P("expert", "dp"), P("expert", "dp", None), P("expert", None),
    )
    out_specs = (
        token, token, P(None, None, "dp"), P("dp", None), P(), P(), P(), P(), P(),
        P("expert", "dp", None), P("expert", "dp"), P("expert", "dp", None), P("expert", None),
    )
    return jax.shard_map(on_device, mesh=mesh, in_specs=in_specs, out_specs=out_specs, check_vma=False)
```

time: 1240 us -> 582 us (0.47)
  Pallas kernels: 0 us -> 546 us
  matrix products: 418 us -> 0 us
  waiting for transfers between devices: 334 us -> 0.02 us
  blocking collectives: 163 us -> 0 us
  other arithmetic: 157 us -> 2.94 us
  local copies, waits for them, and re-layouts: 110 us -> 22.5 us
  starting transfers between devices: 31.8 us -> 2.18 us
  between operations: 14.7 us -> 1.31 us
    pallas_call x0 -> x14, Pallas kernels: none -> 546 us  [the longest x3 136 us: expert_call(): pl.pallas_call(functools.partial(expert_kernel, n, mid_chunk if mid is no...]
    dot_general x26 -> x0, matrix products: 418 us -> none  [the longest x4 64.2 us: masked_scores(): jnp.einsum('qhd,khd->hqk', query_rows, key_rows, preferred_element_type=j...]
    all_to_all x3 -> x0, waiting for transfers between devices: 169 us -> none  [the longest x2 112 us: route_grads(): lax.all_to_all(values, 'expert', split_axis=0, concat_axis=0, tiled=True)]
    psum x1 -> x0, waiting for transfers between devices: 109 us -> none  [on_device(): lax.psum((qkv_part, proj_part, small_pair), 'expert')]
    all_to_all x1 -> x0, blocking collectives: 79 us -> none  [route(): lax.all_to_all(values, 'expert', split_axis=0, concat_axis=0, tiled=True)]
    psum x1 -> x0, blocking collectives: 78.2 us -> none  [on_device(): lax.psum((qkv_part, proj_part, small_pair), 'expert')]
    convert_element_type x12 -> x0, other arithmetic: 68.1 us -> none  [the longest x2 57.4 us: attend_backward(): grad_scores = (attn_probs * (grad_probs - inner_sum)).astype(jnp.bfloat16)]
    reduce_sum x10 -> x0, other arithmetic: 55.9 us -> none  [the longest x2 28.7 us: attend_forward(): totals = jnp.sum(weights, axis=-1, keepdims=True)]
  transfers between devices with their start and end apart: 12 -> 8, of which waited for: 9 -> 0; matrix products, arithmetic and copies ran while one was open for 17% -> 2% of each run, Pallas kernels for 0% -> 63%
where the time goes in v1:
time: 582 us; the launch traced here: 575 us
  Pallas kernels  546 us (94%)
  local copies, waits for them, and re-layouts  22.5 us (4%)
    pallas_call x3, Pallas kernels, expert_call(): pl.pallas_call(functools.partial(expert_kernel, n, mid_chunk if mid is no...  136 us
    pallas_call x1, Pallas kernels, total_call(): pl.pallas_call(functools.partial(total_kernel, n), in_specs=[vm, vm, vm,...  115 us
    pallas_call x1, Pallas kernels, attend_call(): pl.pallas_call(functools.partial(attend_kernel, n, pairs), grid=(pairs +...  71.4 us
    pallas_call x1, Pallas kernels, attend_back_call(): pl.pallas_call(functools.partial(attend_back_kernel, n, pairs), grid=(pai...  41.8 us
    pallas_call x1, Pallas kernels, route_call(): pl.pallas_call(functools.partial(route_kernel, n, chunk), in_specs=[ANY],...  40.5 us
    pallas_call x1, Pallas kernels, middle_back_call(): pl.pallas_call(functools.partial(middle_back_kernel, n, tokens // tb), gr...  33.6 us
    pallas_call x1, Pallas kernels, heads_back_call(): pl.pallas_call(functools.partial(heads_back_kernel, n), grid=(6,), in_spe...  28.1 us
    pallas_call x1, Pallas kernels, wgrad_oth_call(): pl.pallas_call(functools.partial(wgrad_oth_kernel, n, tiles), grid=(2 * t...  25.1 us
  transfers between devices with their start and end apart: 8, of which 0 were waited for; matrix products, arithmetic and copies ran while one was open for 2% of the time, Pallas kernels for 63%

profile of v1, /device:TPU:0, one launch (start us, length us, event | category | flops | bytes accessed | tf_op | source)
XLA Modules:
  0.0 574.8 jit_solution(10522081159399774345)
XLA Ops:
  2.2 1.7 copy.28.ids_ref
  3.9 1.3 reshape.107.gain_ref
  5.2 1.3 reshape.108.shift_ref
  6.4 1.3 reshape.109.pbias_ref
  7.7 1.3 reshape.110.gain_ref
  9.0 1.3 reshape.111.shift_ref
  10.3 0.6 pad.4.clone
  10.9 9.2 %slots.1 = (s32[1024,128]{1,0:T(8,128)}, s32[8,1024]{1,0:T(8,128)}, bf16[1536,1024]{1,0:T(8,128)(2,1)}) custom-call(s32[1024,1]{1,0:T(8,128)} %copy.28.ids_ref, bf16[1024,1024]{1,0:T(8,128)(2,1)} %cot_ref.1), custom_call_target="tpu_custom_call" | custom-call | flops 3221225472 | bytes 8000000 | tf_op jit(solution)/shard_map/slots/pallas_call | solution.py:136
  20.1 1.7 copy-done.5
  21.7 14.4 %head_rows.1 = (bf16[1024,1024]{1,0:T(8,128)(2,1)}, bf16[6,1024,512]{2,1,0:T(8,128)(2,1)}) custom-call(bf16[1024,1024]{1,0:T(8,128)(2,1)} %x_ref.5, bf16[3,1024,512]{2,1,0:T(8,128)(2,1)} %own_ref.7, bf16[3,1024,512]{2,1,0:T(8,128)(2,1)} %copy-done.5, bf16[1,1024]{1,0:T(2,128)(2,1)} %reshape.107.gain_ref, bf16[1,1024]{1,0:T(2,128)(2,1)} %reshape.108.shift_ref), custom_call_target="tpu_custom_call" | custom-call | flops 6442450944 | bytes 18000000 | tf_op jit(solution)/shard_map/head_rows/pallas_call | solution.py:193
  36.2 71.4 %attend.1 = (bf16[1024,1024]{1,0:T(8,128)(2,1)}, bf16[16,256,2304]{2,1,0:T(8,128)(2,1)}, f32[1024,1024]{1,0:T(8,128)}, bf16[1536,1024]{1,0:T(8,128)(2,1)}, bf16[3,16,32,1024]{3,2,1,0:T(8,128)(2,1)}) custom-call(bf16[1024,1024]{1,0:T(8,128)(2,1)} %x_ref.5, s32[1,1024]{1,0:T(1,128)} %seg_ref.1, bf16[6,1024,512]{2,1,0:T(8,128)(2,1)} %get-tuple-element.67.q_ref.k_ref.v_ref, ...), custom_call_target="tpu_custom_call" | custom-call | flops 20000000000 | bytes 50000000 | tf_op jit(solution)/shard_map/attend/pallas_call | solution.py:303
  107.6 40.5 %route.1 = bf16[16,32,1024]{2,1,0:T(8,128)(2,1)} custom-call(bf16[3,16,32,1024]{3,2,1,0:T(8,128)(2,1)} %bitcast.32), custom_call_target="tpu_custom_call" | custom-call | tf_op jit(solution)/shard_map/route/pallas_call | solution.py:343
  148.7 39.0 %experts.3 = (bf16[512,4096]{1,0:T(8,128)(2,1)}, bf16[512,4096]{1,0:T(8,128)(2,1)}, f32[8,4096]{1,0:T(8,128)}, bf16[512,1024]{1,0:T(8,128)(2,1)}, bf16[512,1024]...) custom-call(bf16[512,1024]{1,0:T(8,128)(2,1)} %bitcast.35, bf16[3,512,1024]{2,1,0:T(8,128)(2,1)} %bitcast.59, ...), custom_call_target="tpu_custom_call" | custom-call | flops 17179869184 | bytes 30000000 | tf_op jit(solution)/shard_map/experts/pallas_call | solution.py:470
  187.7 46.3 %experts.4 = (bf16[512,4096]{1,0:T(8,128)(2,1)}, bf16[512,4096]{1,0:T(8,128)(2,1)}, f32[8,4096]{1,0:T(8,128)}, bf16[512,1024]{1,0:T(8,128)(2,1)}, bf16[512,1024]...) custom-call(bf16[512,1024]{1,0:T(8,128)(2,1)} %bitcast.65, ...), custom_call_target="tpu_custom_call" | custom-call | flops 17179869184 | bytes 30000000 | tf_op jit(solution)/shard_map/experts/pallas_call | solution.py:470
  234.0 50.9 %experts.5 = (bf16[512,4096]{1,0:T(8,128)(2,1)}, bf16[512,4096]{1,0:T(8,128)(2,1)}, f32[8,4096]{1,0:T(8,128)}, bf16[512,1024]{1,0:T(8,128)(2,1)}, bf16[512,1024]...) custom-call(bf16[512,1024]{1,0:T(8,128)(2,1)} %bitcast.68, bf16[3,512,1024]{2,1,0:T(8,128)(2,1)} %bitcast.61, ...), custom_call_target="tpu_custom_call" | custom-call | flops 17179869184 | bytes 30000000 | tf_op jit(solution)/shard_map/experts/pallas_call | solution.py:470
  284.9 25.1 %weight_grads_other.1 = (bf16[2048,1024]{1,0:T(8,128)(2,1)}, bf16[2048,1024]{1,0:T(8,128)(2,1)}, f32[8,1024]{1,0:T(8,128)}, bf16[16,32,1024]{2,1,0:T(8,128)(2,1)}) custom-call(bf16[512,4096]{1,0:T(8,128)(2,1)} %get-tuple-element.78.a0, bf16[512,4096]{1,0:T(8,128)(2,1)} %get-tuple-element.79.a1, bf16[512,4096]{1,0:T(8,128)(2,1)} %get-tuple-element.80.a2, ...), custom_call_target="tpu_custom_call" | custom-call | flops 12884901888 | bytes 40000000 | tf_op jit(solution)/shard_map/weight_grads_other/pallas_call | solution.py:524
  310.5 33.6 %middle_back.1 = (f32[1024,1024]{1,0:T(8,128)}, bf16[1024,1024]{1,0:T(8,128)(2,1)}, f32[512,1024]{1,0:T(8,128)}, bf16[512,1024]{1,0:T(8,128)(2,1)}, f32[8,1024]{1,0:T(8,128)}, /*index=5*/bf16[16,32,1024]{2,1,0:T(8,128)(2,1)}) custom-call(s32[1024,128]{1,0:T(8,128)} %get-tuple-element.66.tcol_ref, bf16[512,1024]{1,0:T(8,128)(2,1)} %bitcast.77, ...), custom_call_target="tpu_custom_call" | custom-call | flops 12000000000 | bytes 30000000 | tf_op jit(solution)/shard_map/middle_back/pallas_call | solution.py:644
  344.2 41.8 %attend_back.1 = (bf16[2,1024,512]{2,1,0:T(8,128)(2,1)}, bf16[2,1024,512]{2,1,0:T(8,128)(2,1)}, bf16[2,1024,512]{2,1,0:T(8,128)(2,1)}, bf16[16,32,1024]{2,1,0:T(8,128)(2,1)}) custom-call(bf16[6,1024,512]{2,1,0:T(8,128)(2,1)} %get-tuple-element.67.q_ref.k_ref.v_ref, bf16[6,1024,512]{2,1,0:T(8,128)(2,1)} %get-tuple-element.67.q_ref.k_ref.v_ref, ...), custom_call_target="tpu_custom_call" | custom-call | flops 40000000000 | bytes 40000000 | tf_op jit(solution)/shard_map/attend_back/pallas_call | solution.py:720
  386.0 28.1 %heads_back.1 = (f32[3,1024,512]{2,1,0:T(8,128)}, bf16[3,1024,512]{2,1,0:T(8,128)(2,1)}, f32[1024,1024]{1,0:T(8,128)}, f32[8,1024]{1,0:T(8,128)}, bf16[16,32,1024]{2,1,0:T(8,128)(2,1)}) custom-call(bf16[1024,1024]{1,0:T(8,128)(2,1)} %x_ref.5, bf16[1024,1024]{1,0:T(8,128)(2,1)} %get-tuple-element.94.norm_ref, bf16[2,1024,512]{2,1,0:T(8,128)(2,1)} %get-tuple-element.95.gq, ...), custom_call_target="tpu_custom_call" | custom-call | flops 12999999488 | bytes 50000000 | tf_op jit(solution)/shard_map/heads_back/pallas_call | solution.py:786
  414.1 0.8 slice.52
  414.9 0.8 slice.66
  415.6 1.1 slice_add_fusion
  416.8 0.7 maximum_maximum_fusion.small_ref
  417.5 114.8 %totals.1 = (f32[3,1024,512]{2,1,0:T(8,128)}, f32[512,1024]{1,0:T(8,128)}, f32[8,1024]{1,0:T(8,128)}) custom-call(f32[3,1024,512]{2,1,0:T(8,128)} %get-tuple-element.102.q_own, f32[512,1024]{1,0:T(8,128)} %get-tuple-element.103.p_own, f32[8,1024]{1,0:T(8,128)} %maximum_maximum_fusion.small_ref, bf16[3,1024,512]{2,1,0:T(8,128)(2,1)} %get-tuple-element.106.q_oth, ...), custom_call_target="tpu_custom_call" | custom-call | flops 10000000 | bytes 50000000 | tf_op jit(solution)/shard_map/totals/pallas_call | solution.py:933
  532.3 7.7 %output.1 = bf16[1024,1024]{1,0:T(8,128)(2,1)} custom-call(s32[1024,128]{1,0:T(8,128)} %get-tuple-element.66.tcol_ref, bf16[512,1024]{1,0:T(8,128)(2,1)} %bitcast.71, bf16[512,1024]{1,0:T(8,128)(2,1)} %bitcast.72, bf16[512,1024]{1,0:T(8,128)(2,1)} %bitcast.75, f32[1024,1024]{1,0:T(8,128)} %get-tuple-element.86.mid_ref), custom_call_target="tpu_custom_call" | custom-call | flops 3221225472 | bytes 10000000 | tf_op jit(solution)/shard_map/output/pallas_call | solution.py:964
  540.0 0.6 fusion
  540.7 0.6 slice_add_fusion.2
  541.3 0.6 slice_add_fusion.1
  541.9 23.0 %weight_grads_own.1 = (f32[2048,1024]{1,0:T(8,128)}, f32[2048,1024]{1,0:T(8,128)}) custom-call(bf16[512,4096]{1,0:T(8,128)(2,1)} %get-tuple-element.78.a0, bf16[512,4096]{1,0:T(8,128)(2,1)} %get-tuple-element.79.a1, bf16[512,4096]{1,0:T(8,128)(2,1)} %get-tuple-element.80.a2, bf16[512,4096]{1,0:T(8,128)(2,1)} %get-tuple-element.81.g0, ...), custom_call_target="tpu_custom_call" | custom-call | flops 12884901888 | bytes 60000000 | tf_op jit(solution)/shard_map/weight_grads_own/pallas_call | solution.py:577
  564.9 4.9 copy.32
  569.9 2.8 copy.33
  573.0 1.3 copy.34
  (33 shorter events, 3.1 us)
Async XLA Ops:
  0.6 19.4 %collective-permute-start = (bf16[3,1024,512]{2,1,0:T(8,128)(2,1)}, bf16[3,1024,512]{2,1,0:T(8,128)(2,1)S(1)}, u32[]{:S(2)}, u32[]{:S(2)}) collective-permute-start(bf16[3,1024,512]{2,1,0:T(8,128)(2,1)} %own_ref.7), channel_id=1, source_target_pairs={{0,16},{16,0},{1,17},{17,1},{2,18},{18,2},{3,19},{19,3},{4,20},{20... | collective-permute-start | bytes 9437192 | tf_op jit(solution)/shard_map/ppermute | solution.py:987
  1.2 146.9 %collective-permute-start.2 = (bf16[2048,1024]{1,0:T(8,128)(2,1)}, bf16[2048,1024]{1,0:T(8,128)(2,1)}, u32[]{:S(2)}, u32[]{:S(2)}) collective-permute-start(bf16[2048,1024]{1,0:T(8,128)(2,1)} %bitcast.49), channel_id=1, source_target_pairs={{0,16},{16,0},{1,17},{17,1},{2,18},{18,2},{3,19},{19,3},{4,20},{20... | collective-permute-start | bytes 12582920 | tf_op jit(solution)/shard_map/ppermute | solution.py:987
  1.2 146.9 %collective-permute-start.3 = (bf16[2048,1024]{1,0:T(8,128)(2,1)}, bf16[2048,1024]{1,0:T(8,128)(2,1)}, u32[]{:S(2)}, u32[]{:S(2)}) collective-permute-start(bf16[2048,1024]{1,0:T(8,128)(2,1)} %bitcast.53), channel_id=1, source_target_pairs={{0,16},{16,0},{1,17},{17,1},{2,18},{18,2},{3,19},{19,3},{4,20},{20... | collective-permute-start | bytes 12582920 | tf_op jit(solution)/shard_map/ppermute | solution.py:987
  1.7 34.5 %collective-permute-start.1 = (bf16[512,1024]{1,0:T(8,128)(2,1)}, bf16[512,1024]{1,0:T(8,128)(2,1)}, u32[]{:S(2)}, u32[]{:S(2)}) collective-permute-start(bf16[512,1024]{1,0:T(8,128)(2,1)} %own_ref.6), channel_id=1, source_target_pairs={{0,16},{16,0},{1,17},{17,1},{2,18},{18,2},{3,19},{19,3},{4,20},{20... | collective-permute-start | bytes 3145736 | tf_op jit(solution)/shard_map/ppermute | solution.py:987
  1.8 146.3 %collective-permute-start.4 = (bf16[1,2048]{1,0:T(2,128)(2,1)}, bf16[1,2048]{1,0:T(2,128)(2,1)S(1)}, u32[]{:S(2)}, u32[]{:S(2)}) collective-permute-start(bf16[1,2048]{1,0:T(2,128)(2,1)} %bo_ref.5), channel_id=1, source_target_pairs={{0,16},{16,0},{1,17},{17,1},{2,18},{18,2},{3,19},{19,3},{4,20},{20... | collective-permute-start | bytes 12296 | tf_op jit(solution)/shard_map/ppermute | solution.py:987
  20.1 1.7 copy-start.5
  148.1 0.6 copy-start.6
  310.0 231.9 %collective-permute-start.5 = (bf16[2048,1024]{1,0:T(8,128)(2,1)}, bf16[2048,1024]{1,0:T(8,128)(2,1)}, u32[]{:S(2)}, u32[]{:S(2)}) collective-permute-start(bf16[2048,1024]{1,0:T(8,128)(2,1)} %get-tuple-element.111), channel_id=1, source_target_pairs={{0,16},{16,0},{1,17},{17,1},{2,18},{18,2},{3,19},{19,3},{4,20},{20... | collective-permute-start | bytes 12582920 | tf_op jit(solution)/shard_map/ppermute | solution.py:987
  310.0 231.8 %collective-permute-start.6 = (bf16[2048,1024]{1,0:T(8,128)(2,1)}, bf16[2048,1024]{1,0:T(8,128)(2,1)}, u32[]{:S(2)}, u32[]{:S(2)}) collective-permute-start(bf16[2048,1024]{1,0:T(8,128)(2,1)} %get-tuple-element.112), channel_id=1, source_target_pairs={{0,16},{16,0},{1,17},{17,1},{2,18},{18,2},{3,19},{19,3},{4,20},{20... | collective-permute-start | bytes 12582920 | tf_op jit(solution)/shard_map/ppermute | solution.py:987
  344.2 41.8 %copy-start.3 = (f32[8,1024]{1,0:T(8,128)S(1)}, f32[8,1024]{1,0:T(8,128)}, u32[]{:S(2)}) copy-start(f32[8,1024]{1,0:T(8,128)} %get-tuple-element.105) | copy-start | bytes 98308
  386.0 30.8 %copy-start.4 = (f32[8]{0:T(128)S(1)}, f32[8]{0:T(128)}, u32[]{:S(2)}) copy-start(f32[8]{0:T(128)} %pad.4.clone) | copy-start | bytes 100
  416.7 123.9 %collective-permute-start.7 = (f32[3072]{0:T(1024)S(1)}, f32[3072]{0:T(1024)S(1)}, u32[]{:S(2)}, u32[]{:S(2)}) collective-permute-start(f32[3072]{0:T(1024)S(1)} %pad_maximum_fusion), channel_id=1, source_target_pairs={{0,16},{16,0},{1,17},{17,1},{2,18},{18,2},{3,19},{19,3},{4,20},{20... | collective-permute-start | bytes 36872 | tf_op jit(solution)/shard_map/ppermute | solution.py:987
  532.3 7.7 %copy-start.2 = (f32[8,1024]{1,0:T(8,128)S(1)}, f32[8,1024]{1,0:T(8,128)}, u32[]{:S(2)}) copy-start(f32[8,1024]{1,0:T(8,128)} %get-tuple-element.110) | copy-start | bytes 98308
  564.9 5.0 copy-start
  569.9 3.1 copy-start.1

commit v2 on v0

v2 whole, which is shorter than its diff:
```python
import functools

import jax
import jax.numpy as jnp
from jax import lax
from jax.experimental import pallas as pl
from jax.experimental.pallas import tpu as pltpu
from jax.sharding import PartitionSpec as P

HEAD_DIM = 64
SEQ = 1024
DOC_MAX = 512
EPS = 1e-05
QB = 256
CHUNKS = 3
BF = jnp.bfloat16
F32 = jnp.float32
MESH = pl.DeviceIdType.MESH
VMEM_LIMIT = 60 * 1024 * 1024

BLOCKS = SEQ // QB
START = [max(0, i * QB - DOC_MAX) for i in range(BLOCKS)]
WIDTH = [(i + 1) * QB - START[i] for i in range(BLOCKS)]
OFFSET = [sum(WIDTH[:i]) for i in range(BLOCKS)]
BAND = sum(WIDTH)


def dot(a, b):
    return jnp.dot(a, b, preferred_element_type=F32)


def dot_nt(a, b):
    return lax.dot_general(a, b, (((1,), (1,)), ((), ())), preferred_element_type=F32)


def dot_tn(a, b):
    return lax.dot_general(a, b, (((0,), (0,)), ((), ())), preferred_element_type=F32)


def params(**kw):
    return pltpu.CompilerParams(vmem_limit_bytes=VMEM_LIMIT, **kw)


def cost(flops, nbytes, trans=0):
    return pl.CostEstimate(flops=int(flops), bytes_accessed=int(nbytes), transcendentals=int(trans))


ANY = pl.BlockSpec(memory_space=pl.ANY)


def whole(shape):
    return pl.BlockSpec(shape, lambda *_: (0,) * len(shape))


def block_of(index, size):
    return pl.ds(pl.multiple_of(index * size, size), size)


class Route:
    def __init__(self, n, src, dst, send, recv, local):
        self.n, self.src, self.dst = n, src, dst
        self.send, self.recv, self.local = send, recv, local

    def remote(self):
        me = lax.axis_index("expert")
        for d in range(1, self.n):
            there = lax.rem(me + d, self.n)
            yield pltpu.make_async_remote_copy(
                self.src(there), self.dst(me), self.send.at[d], self.recv.at[d],
                device_id={"expert": there}, device_id_type=MESH,
            )

    def own(self):
        me = lax.axis_index("expert")
        return pltpu.make_async_copy(self.src(me), self.dst(me), self.local)

    def start(self):
        for c in self.remote():
            c.start()
        self.own().start()

    def wait(self):
        self.own().wait()
        for c in self.remote():
            c.wait()


def route_sems(n, count):
    return [
        pltpu.SemaphoreType.DMA((count, n)),
        pltpu.SemaphoreType.DMA((count, n)),
        pltpu.SemaphoreType.DMA((count,)),
    ]


def greet(n, partner):
    me = lax.axis_index("expert")
    barrier = pltpu.get_barrier_semaphore()
    for d in range(1, n):
        pl.semaphore_signal(
            barrier, inc=1, device_id={"expert": lax.rem(me + d, n)}, device_id_type=MESH
        )
    if partner:
        pl.semaphore_signal(barrier, inc=1, device_id={"dp": 1 - lax.axis_index("dp")}, device_id_type=MESH)
    pl.semaphore_wait(barrier, n if partner else n - 1)


def to_partner(src, dst, send, recv):
    return pltpu.make_async_remote_copy(
        src, dst, send, recv, device_id={"dp": 1 - lax.axis_index("dp")}, device_id_type=MESH
    )


def unit_of(values):
    centre = values - jnp.mean(values, axis=-1, keepdims=True)
    inverse = lax.rsqrt(jnp.mean(centre * centre, axis=-1, keepdims=True) + EPS)
    return centre * inverse, inverse


def lane_pick(width, first):
    lanes = lax.broadcasted_iota(jnp.int32, (1, width), 1)
    return (lanes < HEAD_DIM) if first else (lanes >= HEAD_DIM)


PRE_GAIN, PRE_SHIFT, PROJ_BIAS, MID_GAIN, MID_SHIFT = range(5)


def front_kernel(
    n, cc, pairs, ids_ref, cot_ref, x_ref, seg_ref, vec_ref, w_ref, w_any, p_ref, p_any,
    tcol_ref, norm_ref, hr_ref, att_ref, prob_ref, mid_ref, slot_ref, arr_ref, wo_out, po_out,
    row_s, cs_s, norm_s, hr_s, wo_s, po_s, bias_s, low_s, send, recv, local, dsend, drecv, dlocal,
):
    step = pl.program_id(0)
    tokens, width = x_ref.shape
    half = p_ref.shape[0]
    rows = n * cc
    first_pair = 7
    routes = [
        Route(
            n, lambda e, c=c: cs_s.at[block_of(c * n + e, cc)], lambda d, c=c: arr_ref.at[c, block_of(d, cc)],
            send.at[c], recv.at[c], local.at[c],
        )
        for c in range(CHUNKS)
    ]

    def swaps():
        return [
            to_partner(w_any, wo_s, dsend.at[0], drecv.at[0]),
            to_partner(p_any, po_s, dsend.at[1], drecv.at[1]),
        ]

    def keeps():
        return [
            pltpu.make_async_copy(wo_s, wo_out, dlocal.at[0]),
            pltpu.make_async_copy(po_s, po_out, dlocal.at[1]),
        ]

    @pl.when(step == 0)
    def _():
        greet(n, True)
        for c in swaps():
            c.start()
        ids = jnp.transpose(jnp.broadcast_to(ids_ref[...].astype(F32), (128, tokens)))
        hot = (ids == lax.broadcasted_iota(jnp.int32, (tokens, 128), 1).astype(F32)).astype(F32)
        low_hot = hot.astype(BF)
        place = []
        for b in range(tokens // 256):
            span = (b + 1) * 256
            lower = (
                lax.broadcasted_iota(jnp.int32, (256, span), 0) + b * 256
                >= lax.broadcasted_iota(jnp.int32, (256, span), 1)
            ).astype(F32).astype(BF)
            counts = dot(lower, low_hot[0:span])
            rank = jnp.sum(counts * hot[b * 256:span], axis=1, keepdims=True) - 1.0
            chunk = jnp.floor((rank + 0.5) * (1.0 / cc))
            place.append(chunk * rows + ids[b * 256:span] * cc + (rank - chunk * cc))
        place = jnp.concatenate(place, axis=0)
        tcol_ref[...] = place.astype(jnp.int32)
        row_s[...] = jnp.transpose(place)[0:8, :].astype(jnp.int32)

        def fill(b, _):
            hot = (
                lax.broadcasted_iota(jnp.int32, (256, tokens), 0) + b * 256 == row_s[0:1, :]
            ).astype(F32).astype(BF)
            cs_s[block_of(b, 256), :] = dot(hot, cot_ref[...]).astype(BF)
            return 0

        lax.fori_loop(0, CHUNKS * rows // 256, fill, 0)
        for r in routes:
            r.start()

        gain, shift = vec_ref[PRE_GAIN:PRE_GAIN + 1, :], vec_ref[PRE_SHIFT:PRE_SHIFT + 1, :]

        def body(b, _):
            at = block_of(b, 128)
            unit, _ = unit_of(x_ref[at, :].astype(F32))
            low = (unit * gain + shift).astype(BF)
            norm_s[at, :] = low
            norm_ref[at, :] = low
            return 0

        lax.fori_loop(0, tokens // 128, body, 0)

    @pl.when((step >= 1) & (step <= 3))
    def _():
        out = dot(norm_s[...], w_ref[0]).astype(BF)
        hr_ref[0] = out
        hr_s[step - 1] = out

    @pl.when(step == 4)
    def _():
        for c in swaps():
            c.wait()
        for c in keeps():
            c.start()

    @pl.when((step >= 4) & (step <= 6))
    def _():
        out = dot(norm_s[...], wo_s[step - 4]).astype(BF)
        hr_ref[0] = out
        hr_s[step - 1] = out

    @pl.when(step == first_pair)
    def _():
        seg = seg_ref[...].astype(F32)
        seg_col = jnp.transpose(jnp.broadcast_to(seg, (128, tokens)))
        for i in range(BLOCKS):
            w, s = WIDTH[i], START[i]
            at_row = lax.broadcasted_iota(jnp.int32, (QB, w), 0) + i * QB
            at_key = lax.broadcasted_iota(jnp.int32, (QB, w), 1) + s
            same = seg_col[i * QB:(i + 1) * QB, 0:1] == seg[:, s:s + w]
            bias_s[:, OFFSET[i]:OFFSET[i] + w] = jnp.where(same & (at_key <= at_row), 0.0, -1e30)

    @pl.when((step >= first_pair) & (step < first_pair + pairs))
    def _():
        pair = step - first_pair
        per = half // 128
        side, lanes = lax.div(pair, per), block_of(lax.rem(pair, per), 128)
        query = hr_s[3 * side, :, lanes] * BF(HEAD_DIM ** -0.5)
        for i in range(BLOCKS):
            w, s = WIDTH[i], START[i]
            keys, values = hr_s[3 * side + 1, s:s + w, lanes], hr_s[3 * side + 2, s:s + w, lanes]
            bias = bias_s[:, OFFSET[i]:OFFSET[i] + w]
            parts = []
            for j in range(2):
                q = jnp.where(lane_pick(128, j == 0), query[i * QB:(i + 1) * QB], BF(0))
                scores = dot_nt(q, keys) + bias
                top = jnp.max(scores, axis=-1, keepdims=True)
                weights = jnp.exp(scores - top)
                probs = (weights * (1.0 / jnp.sum(weights, axis=-1, keepdims=True))).astype(BF)
                prob_ref[j, :, OFFSET[i]:OFFSET[i] + w] = probs
                parts.append(dot(probs, values))
            both = jnp.where(lane_pick(128, True), parts[0], parts[1])
            att_ref[i * QB:(i + 1) * QB, block_of(pair, 128)] = both.astype(BF)

    @pl.when(step == first_pair + pairs)
    def _():
        pbias = vec_ref[PROJ_BIAS:PROJ_BIAS + 1, :]
        gain, shift = vec_ref[MID_GAIN:MID_GAIN + 1, :], vec_ref[MID_SHIFT:MID_SHIFT + 1, :]

        def body(b, _):
            at = block_of(b, 128)
            branch = dot(att_ref[at, 0:half], p_ref[...]) + dot(att_ref[at, half:2 * half], po_s[...])
            middle = x_ref[at, :].astype(F32) + branch + pbias
            mid_ref[at, :] = middle
            unit, _ = unit_of(middle)
            low_s[at, :] = (unit * gain + shift).astype(BF)
            return 0

        lax.fori_loop(0, tokens // 128, body, 0)

        def fill(b, _):
            hot = (
                lax.broadcasted_iota(jnp.int32, (256, tokens), 0) + b * 256 == row_s[0:1, :]
            ).astype(F32).astype(BF)
            slot_ref[block_of(b, 256), :] = dot(hot, low_s[...]).astype(BF)
            return 0

        lax.fori_loop(0, CHUNKS * rows // 256, fill, 0)
        for c in keeps():
            c.wait()
        for r in routes:
            r.wait()


def front_call(n, cc, ids, cot, x, seg, vec, qkv, proj):
    tokens, width = x.shape
    half = proj.shape[0]
    pairs = width // 128
    rows = n * cc
    dma = pltpu.SemaphoreType.DMA
    sds = jax.ShapeDtypeStruct

    def pair_of(i):
        return jnp.clip(i - 7, 0, pairs - 1)

    return pl.pallas_call(
        functools.partial(front_kernel, n, cc, pairs),
        grid=(8 + pairs,),
        in_specs=[
            whole((1, tokens)), whole((tokens, width)), whole((tokens, width)), whole((1, tokens)),
            whole(vec.shape),
            pl.BlockSpec((1, width, half), lambda i: (jnp.clip(i - 1, 0, 2), 0, 0)), ANY,
            whole((half, width)), ANY,
        ],
        out_specs=[
            whole((tokens, 128)), whole((tokens, width)),
            pl.BlockSpec((1, tokens, half), lambda i: (jnp.clip(i - 1, 0, 5), 0, 0)),
            whole((tokens, width)), pl.BlockSpec((2, QB, BAND), lambda i: (pair_of(i), 0, 0)),
            whole((tokens, width)), whole((CHUNKS * rows, width)), ANY, ANY, ANY,
        ],
        out_shape=[
            sds((tokens, 128), jnp.int32), sds((tokens, width), BF), sds((6, tokens, half), BF),
            sds((tokens, width), BF), sds((2 * pairs, QB, BAND), BF), sds((tokens, width), F32),
            sds((CHUNKS * rows, width), BF), sds((CHUNKS, rows, width), BF), sds(qkv.shape, BF), sds(proj.shape, BF),
        ],
        scratch_shapes=[
            pltpu.VMEM((8, tokens), jnp.int32), pltpu.VMEM((CHUNKS * rows, width), BF),
            pltpu.VMEM((tokens, width), BF), pltpu.VMEM((6, tokens, half), BF), pltpu.VMEM(qkv.shape, BF),
            pltpu.VMEM(proj.shape, BF), pltpu.VMEM((QB, BAND), F32), pltpu.VMEM((tokens, width), BF),
            *route_sems(n, CHUNKS), dma((2,)), dma((2,)), dma((2,)),
        ],
        compiler_params=params(collective_id=1, has_side_effects=True),
        cost_estimate=cost(3e10, 6e7),
        name="front",
    )(ids, cot, x, seg, vec, qkv, qkv, proj, proj)


GELU_C = 0.7978845608028654
GELU_A = 0.044715
TILE = 512


def expert_kernel(
    n, cc, own_tiles, mid_ref, c_ref, uo_ref, ut_ref, do_ref, dt_ref, bo_ref, bt_ref, db_ref,
    act_ref, gh_ref, ub_ref, y_ref, dx_ref, x_out, back_out,
    x_s, g_s, y_s, dx_s, dxb_s, send, recv, local, xsem,
):
    step = pl.program_id(0)
    tiles = 2 * own_tiles
    phase, tile = lax.div(step, tiles), lax.rem(step, tiles)
    rows = n * cc
    ins = [
        Route(
            n, lambda e, c=c: mid_ref.at[block_of(c * n + e, cc)], lambda d, c=c: x_s.at[c, block_of(d, cc)],
            send.at[c], recv.at[c], local.at[c],
        )
        for c in range(CHUNKS)
    ]
    back = Route(
        n, lambda e: dxb_s.at[block_of(e, cc)], lambda d: back_out.at[block_of(d, cc)],
        send.at[CHUNKS], recv.at[CHUNKS], local.at[CHUNKS],
    )

    def keep(c):
        return pltpu.make_async_copy(x_s.at[c], x_out.at[c], xsem.at[c])

    @pl.when(step == 0)
    def _():
        greet(n, False)
        ins[0].start()
        ub_ref[...] = jnp.zeros_like(ub_ref)

    for c in range(CHUNKS):
        @pl.when(step == (c + 1) * tiles)
        def _():
            ins[c].wait()
            if c + 1 < CHUNKS:
                ins[c + 1].start()
            else:
                back.start()
            keep(c).start()

    lanes = block_of(tile, TILE)

    def early(down_ref):
        for c in range(CHUNKS):
            g_s[c, :, lanes] = dot_nt(c_ref[c], down_ref[...]).astype(BF)

    def late(c, up_ref, down_ref, b_ref):
        up, down = up_ref[...], down_ref[...]
        h = dot_nt(x_s[c], up) + b_ref[...].astype(F32)
        sq = h * h
        t = jnp.tanh(GELU_C * (h + GELU_A * (sq * h)))
        act = ((0.5 * h) * (1.0 + t)).astype(BF)
        act_ref[0] = act
        slope = 0.5 * (1.0 + t) + (0.5 * h) * ((1.0 - t * t) * (GELU_C * (1.0 + (3.0 * GELU_A) * sq)))
        gh = (g_s[c, :, lanes].astype(F32) * slope).astype(BF)
        gh_ref[0] = gh
        ub_ref[0:1, lanes] += jnp.sum(gh.astype(F32), axis=0, keepdims=True)
        y_s[...] += dot(act, down)
        dx_s[...] += dot(gh, up)

    @pl.when((phase >= 1) & (tile == 0))
    def _():
        y_s[...] = jnp.broadcast_to(db_ref[...].astype(F32), y_s.shape)
        dx_s[...] = jnp.zeros_like(dx_s)

    @pl.when((phase == 0) & (tile < own_tiles))
    def _():
        early(do_ref)

    @pl.when((phase == 0) & (tile >= own_tiles))
    def _():
        early(dt_ref)

    @pl.when((phase >= 1) & (tile < own_tiles))
    def _():
        late(phase - 1, uo_ref, do_ref, bo_ref)

    @pl.when((phase >= 1) & (tile >= own_tiles))
    def _():
        late(phase - 1, ut_ref, dt_ref, bt_ref)

    @pl.when((phase >= 1) & (tile == tiles - 1))
    def _():
        y_ref[0] = y_s[...].astype(BF)
        dx_ref[0] = dx_s[...].astype(BF)

    @pl.when((phase == 1) & (tile == tiles - 1))
    def _():
        dxb_s[...] = dx_s[...].astype(BF)

    @pl.when(step == (CHUNKS + 1) * tiles - 1)
    def _():
        for c in range(CHUNKS):
            keep(c).wait()
        back.wait()


def expert_call(n, cc, mid_slots, cot, up, down, bias, down_bias):
    up_own, up_oth = up
    down_own, down_oth = down
    b_own, b_oth = bias
    rows = n * cc
    hid, width = up_own.shape
    own_tiles = hid // TILE
    tiles = 2 * own_tiles
    sds = jax.ShapeDtypeStruct

    def first(i):
        return jnp.minimum(i % tiles, own_tiles - 1)

    def second(i):
        return jnp.maximum(i % tiles - own_tiles, 0)

    def up_first(i):
        return jnp.where(i < tiles, 0, first(i))

    def up_second(i):
        return jnp.where(i < tiles, 0, second(i))

    def chunk(i):
        return jnp.maximum(i // tiles - 1, 0)

    def column(i):
        return jnp.where(i < tiles, 0, i % tiles)

    col = pl.BlockSpec((1, rows, TILE), lambda i: (chunk(i), 0, column(i)))
    per_chunk = pl.BlockSpec((1, rows, width), lambda i: (chunk(i), 0, 0))
    return pl.pallas_call(
        functools.partial(expert_kernel, n, cc, own_tiles),
        grid=((CHUNKS + 1) * tiles,),
        in_specs=[
            ANY, whole(cot.shape),
            pl.BlockSpec((TILE, width), lambda i: (up_first(i), 0)),
            pl.BlockSpec((TILE, width), lambda i: (up_second(i), 0)),
            pl.BlockSpec((TILE, width), lambda i: (first(i), 0)),
            pl.BlockSpec((TILE, width), lambda i: (second(i), 0)),
            pl.BlockSpec((1, TILE), lambda i: (0, first(i))),
            pl.BlockSpec((1, TILE), lambda i: (0, second(i))),
            whole((1, width)),
        ],
        out_specs=[col, col, whole((8, 2 * hid)), per_chunk, per_chunk, ANY, ANY],
        out_shape=[
            sds((CHUNKS, rows, 2 * hid), BF), sds((CHUNKS, rows, 2 * hid), BF), sds((8, 2 * hid), F32),
            sds((CHUNKS, rows, width), BF), sds((CHUNKS, rows, width), BF), sds((CHUNKS, rows, width), BF),
            sds((rows, width), BF),
        ],
        scratch_shapes=[
            pltpu.VMEM((CHUNKS, rows, width), BF), pltpu.VMEM((CHUNKS, rows, 2 * hid), BF),
            pltpu.VMEM((rows, width), F32), pltpu.VMEM((rows, width), F32), pltpu.VMEM((rows, width), BF),
            *route_sems(n, CHUNKS + 1), pltpu.SemaphoreType.DMA((CHUNKS,)),
        ],
        compiler_params=params(collective_id=2, has_side_effects=True),
        cost_estimate=cost(5.2e10, 8e7),
        name="experts",
    )(mid_slots, cot, up_own, up_oth, down_own, down_oth, b_own, b_oth, down_bias)


def wgrad_kernel(
    n, cc, tiles, a_ref, g_ref, c_ref, x_ref, ub_ref, dx_ref,
    do_ref, up_ref, ubg_ref, cbg_ref, back1, back2,
    out_s, in_s, small_s, got_s, send, recv, local, dsend, drecv, ssend, srecv,
):
    step = pl.program_id(0)
    hid = ubg_ref.shape[1]
    routes = [
        Route(
            n, lambda e, c=c: dx_ref.at[c, block_of(e, cc)], lambda d, dst=dst: dst.at[block_of(d, cc)],
            send.at[k], recv.at[k], local.at[k],
        )
        for k, (c, dst) in enumerate(((1, back1), (2, back2)))
    ]

    def swap(k):
        return to_partner(out_s.at[k], in_s.at[k], dsend.at[k], drecv.at[k])

    small = to_partner(small_s, got_s, ssend, srecv)

    @pl.when(step == 0)
    def _():
        greet(n, True)
        routes[0].start()
        total = jnp.zeros((1, c_ref.shape[2]), F32)
        for c in range(CHUNKS):
            total = total + jnp.sum(c_ref[c].astype(F32), axis=0, keepdims=True)
        small_s[...] = jnp.zeros_like(small_s)
        small_s[0:1, 0:hid] = ub_ref[0:1, hid:2 * hid]
        small_s[0:1, hid:hid + total.shape[1]] = total
        small.start()

    @pl.when(step == 2 * tiles)
    def _():
        routes[0].wait()
        routes[1].start()
        small.wait()
        ubg_ref[...] = ub_ref[0:1, 0:hid] + got_s[0:1, 0:hid]
        cbg_ref[...] = small_s[0:1, hid:] + got_s[0:1, hid:]

    def product(left, right):
        total = dot_tn(left[0], right[0])
        for c in range(1, CHUNKS):
            total = total + dot_tn(left[c], right[c])
        return total

    for k in range(2 * tiles):
        @pl.when(step == k)
        def _():
            left, right = (a_ref, c_ref) if k < tiles else (g_ref, x_ref)
            out_s[k] = product(left, right).astype(BF)
            swap(k).start()

        @pl.when(step == 2 * tiles + k)
        def _():
            left, right, out = (a_ref, c_ref, do_ref) if k < tiles else (g_ref, x_ref, up_ref)
            total = product(left, right)
            swap(k).wait()
            out[...] = (total + in_s[k].astype(F32)).astype(BF)

    @pl.when(step == 4 * tiles - 1)
    def _():
        routes[1].wait()


def wgrad_call(n, cc, acts, ghs, cot, rows_in, ub, dx):
    _, rows, width = cot.shape
    hid = acts.shape[2] // 2
    tiles = hid // TILE
    dma = pltpu.SemaphoreType.DMA
    sds = jax.ShapeDtypeStruct

    def first(i):
        return jnp.minimum(i % (2 * tiles), tiles - 1)

    def second(i):
        return jnp.maximum(i % (2 * tiles) - tiles, 0)

    def other(i):
        return jnp.where(i < 2 * tiles, tiles, 0)

    a_spec = pl.BlockSpec((CHUNKS, rows, TILE), lambda i: (0, 0, other(i) + first(i)))
    g_spec = pl.BlockSpec((CHUNKS, rows, TILE), lambda i: (0, 0, other(i) + second(i)))

    def late(i):
        return jnp.where(i < 2 * tiles, 0, 1)

    d_spec = pl.BlockSpec((TILE, width), lambda i: (late(i) * first(i), 0))
    u_spec = pl.BlockSpec((TILE, width), lambda i: (late(i) * second(i), 0))
    return pl.pallas_call(
        functools.partial(wgrad_kernel, n, cc, tiles),
        grid=(4 * tiles,),
        in_specs=[a_spec, g_spec, whole(cot.shape), whole(rows_in.shape), whole(ub.shape), ANY],
        out_specs=[d_spec, u_spec, whole((1, hid)), whole((1, width)), ANY, ANY],
        out_shape=[
            sds((hid, width), BF), sds((hid, width), BF), sds((1, hid), F32), sds((1, width), F32),
            sds((rows, width), BF), sds((rows, width), BF),
        ],
        scratch_shapes=[
            pltpu.VMEM((2 * tiles, TILE, width), BF), pltpu.VMEM((2 * tiles, TILE, width), BF),
            pltpu.VMEM((8, hid + width), F32), pltpu.VMEM((8, hid + width), F32),
            *route_sems(n, 2), dma((2 * tiles,)), dma((2 * tiles,)), dma, dma,
        ],
        compiler_params=params(collective_id=3, has_side_effects=True),
        cost_estimate=cost(2.6e10, 8e7),
        name="weight_grads",
    )(acts, ghs, cot, rows_in, ub, dx)


def gather_rows(tcol, parts):
    total = None
    for c, part in enumerate(parts):
        rows = part.shape[0]
        hot = (
            lax.broadcasted_iota(jnp.int32, (tcol.shape[0], rows), 1) + c * rows == tcol[:, 0:1]
        ).astype(F32).astype(BF)
        term = dot(hot, part)
        total = term if total is None else total + term
    return total


def norm_back(grad, unit, inverse, gain):
    scaled = grad * gain
    inner = jnp.mean(scaled, axis=-1, keepdims=True)
    along = jnp.mean(scaled * unit, axis=-1, keepdims=True)
    return inverse * (scaled - inner - unit * along)


def middle_back_kernel(
    n, cc, blocks, tcol_ref, g0, g1, g2, mid_ref, cot_ref, vec_ref, own_ref, oth_ref, att_ref, y_src,
    gmid_ref, gatt_ref, pg_own, pg_oth, small_ref, y_dst, gb_s, send, recv, local,
):
    route = Route(
        n, lambda e: y_src.at[0, block_of(e, cc)], lambda d: y_dst.at[block_of(d, cc)],
        send.at[0], recv.at[0], local.at[0],
    )
    step = pl.program_id(0)
    half = own_ref.shape[0]
    tb = mid_ref.shape[0]

    @pl.when(step == 0)
    def _():
        greet(n, False)
        route.start()
        small_ref[...] = jnp.zeros_like(small_ref)

    grad = gather_rows(tcol_ref[...], (g0[...], g1[...], g2[...]))
    grad = grad.astype(BF).astype(F32)
    unit, inverse = unit_of(mid_ref[...])
    gmid = cot_ref[...].astype(F32) + norm_back(grad, unit, inverse, vec_ref[MID_GAIN:MID_GAIN + 1, :])
    gmid_ref[...] = gmid
    gb = gmid.astype(BF)
    gb_s[block_of(step, tb), :] = gb
    small_ref[2:3, :] += jnp.sum(grad * unit, axis=0, keepdims=True)
    small_ref[3:4, :] += jnp.sum(grad, axis=0, keepdims=True)
    small_ref[4:5, :] += jnp.sum(gb.astype(F32), axis=0, keepdims=True)
    gatt_ref[:, 0:half] = dot_nt(gb, own_ref[...]).astype(BF)
    gatt_ref[:, half:2 * half] = dot_nt(gb, oth_ref[...]).astype(BF)

    @pl.when(step == blocks - 1)
    def _():
        pg_own[...] = dot_tn(att_ref[:, 0:half], gb_s[...]).astype(BF)
        pg_oth[...] = dot_tn(att_ref[:, half:2 * half], gb_s[...]).astype(BF)
        route.wait()


def middle_back_call(n, cc, tcol, grads, middle, cot, vec, proj_own, proj_oth, att, y):
    tokens, width = middle.shape
    half = proj_own.shape[0]
    tb = 256
    rows = grads[0].shape[0]
    block = pl.BlockSpec((tb, width), lambda i: (i, 0))
    sds = jax.ShapeDtypeStruct
    return pl.pallas_call(
        functools.partial(middle_back_kernel, n, cc, tokens // tb),
        grid=(tokens // tb,),
        in_specs=[
            pl.BlockSpec((tb, 128), lambda i: (i, 0)), *[whole((rows, width))] * 3, block, block,
            whole(vec.shape), whole((half, width)), whole((half, width)), whole((tokens, width)), ANY,
        ],
        out_specs=[block, block, whole((half, width)), whole((half, width)), whole((8, width)), ANY],
        out_shape=[
            sds((tokens, width), F32), sds((tokens, width), BF), sds((half, width), BF), sds((half, width), BF),
            sds((8, width), F32), sds((rows, width), BF),
        ],
        scratch_shapes=[pltpu.VMEM((tokens, width), BF), *route_sems(n, 1)],
        compiler_params=params(collective_id=4, has_side_effects=True),
        cost_estimate=cost(1.2e10, 3e7),
        name="middle_back",
    )(tcol, *grads, middle, cot, vec, proj_own, proj_oth, att, y)


class Part:
    def __init__(self, index, base, length, order, me, refs):
        self.index, self.base, self.total, self.order, self.me = index, base, length, order, me
        self.acc, self.rcv, self.res, self.rs_send, self.rs_recv, self.ag_send, self.ag_recv = refs
        self.stages, self.stage = len(order), 0
        self.step = length >> len(order)

    def upper(self, s):
        return lax.rem(lax.div(self.me, 1 << self.order[s]), 2)

    def rows(self, start, length):
        return pl.ds(pl.multiple_of(start, 16), length)

    def start(self, s):
        at = self.base
        for k in range(s):
            at = at + self.upper(k) * (self.total >> (k + 1))
        return at

    def slot(self, s):
        return self.base + self.total - (self.total >> s)

    def copy(self):
        inward = self.stage < self.stages
        s = self.stage if inward else 2 * self.stages - 1 - self.stage
        bit = 1 << self.order[s]
        peer = {"expert": self.me + bit - 2 * bit * self.upper(s)}
        if inward:
            half = self.total >> (s + 1)
            away = self.start(s) + (1 - self.upper(s)) * half
            src, dst = self.acc.at[self.rows(away, half)], self.rcv.at[pl.ds(self.slot(s), half)]
            send, recv = self.rs_send, self.rs_recv
        else:
            src = dst = self.res.at[self.rows(self.start(s + 1), self.total >> (s + 1))]
            send, recv = self.ag_send, self.ag_recv
        return pltpu.make_async_remote_copy(
            src, dst, send.at[self.index, s], recv.at[self.index, s], device_id=peer, device_id_type=MESH
        )

    def begin(self):
        self.copy().start()

    def advance(self):
        self.copy().wait()
        s = self.stage
        if s < self.stages:
            keep, slot, step = self.start(s + 1), self.slot(s), self.step
            into = self.res if s == self.stages - 1 else self.acc

            def add(b, _):
                at = self.rows(keep + b * step, step)
                into[at, :] = (
                    self.acc[at, :].astype(F32) + self.rcv[self.rows(slot + b * step, step), :].astype(F32)
                ).astype(BF)
                return 0

            lax.fori_loop(0, (self.total >> (s + 1)) // step, add, 0)
        self.stage += 1
        if self.stage < 2 * self.stages:
            self.copy().start()


def back_kernel(
    n, cc, pairs, q_ref, k_ref, v_ref, prob_ref, do_ref, o_ref, x_ref, norm_ref, own_ref, oth_ref, gmid_ref,
    vec_ref, small_ref, pg_own, pg_oth, y_src,
    xg_ref, small_out, sum_out, z1, z2,
    dk_s, dv_s, gh_s, gnp_s, acc, rcv, res, got, pgot, snd, small_got,
    send, recv, local, dsend, drecv, rs_send, rs_recv, ag_send, ag_recv, sm_send, sm_recv, out_sem,
):
    step = pl.program_id(0)
    tokens, width = x_ref.shape
    half = own_ref.shape[2]
    scale = HEAD_DIM ** -0.5
    per = half // 128
    me = lax.axis_index("expert")
    stages = n.bit_length() - 1
    routes = [
        Route(
            n, lambda e, c=c: y_src.at[c, block_of(e, cc)], lambda d, z=z: z.at[block_of(d, cc)],
            send.at[c - 1], recv.at[c - 1], local.at[c - 1],
        )
        for c, z in ((1, z1), (2, z2))
    ]

    split = max(1, min(2, width // (32 * n)))
    size = width // split
    turn = max(1, stages - 1)
    refs = (acc, rcv, res, rs_send, rs_recv, ag_send, ag_recv)

    def part(i):
        order = [(i + s) % turn for s in range(turn)] + ([turn] if stages > turn else [])
        return Part(i, i * size, size, order, me, refs)

    proj_parts = [part(3 * split + i) for i in range(split)]
    head_parts = [[part(c * split + i) for i in range(split)] for c in range(3)]

    def dp_swap(c):
        src = snd.at[c] if c < 3 else pg_oth
        dst = got.at[c] if c < 3 else pgot
        return to_partner(src, dst, dsend.at[c], drecv.at[c])

    @pl.when(step == 0)
    def _():
        greet(n, True)
        dp_swap(3).start()
        routes[0].start()
        gnp_s[...] = jnp.zeros_like(gnp_s)

    @pl.when(step < pairs)
    def _():
        side, lanes = lax.div(step, per), block_of(lax.rem(step, per), 128)
        dk_s[...] = jnp.zeros_like(dk_s)
        dv_s[...] = jnp.zeros_like(dv_s)
        for i in range(BLOCKS):
            w, s = WIDTH[i], START[i]
            at = slice(i * QB, (i + 1) * QB)
            keys, values = k_ref[0, s:s + w, :], v_ref[0, s:s + w, :]
            go = do_ref[at, :]
            prod = go.astype(F32) * o_ref[at, :].astype(F32)
            query = q_ref[0, at, :]
            parts = []
            for j in range(2):
                pick = lane_pick(128, j == 0)
                go_j = jnp.where(pick, go, BF(0))
                q_j = jnp.where(pick, query, BF(0))
                inner = jnp.sum(jnp.where(pick, prod, 0.0), axis=-1, keepdims=True)
                probs = prob_ref[j, :, OFFSET[i]:OFFSET[i] + w]
                gp = dot_nt(go_j, values)
                gs = (probs.astype(F32) * (gp - inner)).astype(BF)
                parts.append(dot(gs, keys))
                dk_s[s:s + w, :] += dot_tn(gs, q_j)
                dv_s[s:s + w, :] += dot_tn(probs, go_j)
            gh_s[3 * side, at, lanes] = (jnp.where(lane_pick(128, True), parts[0], parts[1]) * scale).astype(BF)
        gh_s[3 * side + 1, :, lanes] = (dk_s[...] * scale).astype(BF)
        gh_s[3 * side + 2, :, lanes] = dv_s[...].astype(BF)

    def bring_to(parts, goal):
        while parts[0].stage < goal:
            for p in parts:
                p.advance()

    total_stages = 2 * stages

    @pl.when(step == 1)
    def _():
        dp_swap(3).wait()
        base = 3 * width
        for b in range(width // half):
            for p in range(half // 128):
                at = slice(p * 128, (p + 1) * 128)
                acc[base + b * half + p * 128:base + b * half + (p + 1) * 128, :] = (
                    pg_own[at, b * half:(b + 1) * half].astype(F32)
                    + pgot[at, b * half:(b + 1) * half].astype(F32)
                ).astype(BF)
        for p in proj_parts:
            p.begin()

    last = pairs + 6
    for t in range(2, last):
        goal = t - 1 if t < last - 1 else total_stages
        goal = min(goal, total_stages)
        prev = min(t - 2, total_stages)
        if goal > prev:
            @pl.when(step == t)
            def _():
                bring_to(proj_parts, goal)

    @pl.when(step == pairs - 1)
    def _():
        routes[0].wait()
        routes[1].start()

    for c in range(3):
        @pl.when(step == pairs + c)
        def _():
            g = gh_s[3 + c]
            snd[c] = dot_tn(norm_ref[...], g).astype(BF)
            dp_swap(c).start()
            gnp_s[...] += dot_nt(g, oth_ref[0])

        @pl.when(step == pairs + 3 + c)
        def _():
            g = gh_s[c]
            mine = dot_tn(norm_ref[...], g)
            dp_swap(c).wait()
            acc[c * width:(c + 1) * width, :] = (mine + got[c].astype(F32)).astype(BF)
            for p in head_parts[c]:
                p.begin()
            gnp_s[...] += dot_nt(g, own_ref[0])

    @pl.when(step == last)
    def _():
        small_out[...] = small_ref[...]

        def body(b, _):
            at = block_of(b, 128)
            grad = gnp_s[at, :]
            unit, inverse = unit_of(x_ref[at, :].astype(F32))
            xg_ref[at, :] = gmid_ref[at, :] + norm_back(grad, unit, inverse, vec_ref[PRE_GAIN:PRE_GAIN + 1, :])
            small_out[0:1, :] += jnp.sum(grad * unit, axis=0, keepdims=True)
            small_out[1:2, :] += jnp.sum(grad, axis=0, keepdims=True)
            return 0

        lax.fori_loop(0, tokens // 128, body, 0)

        def small_swap(k):
            if k == 0:
                peer = {"dp": 1 - lax.axis_index("dp")}
            else:
                bit = 1 << (k - 1)
                peer = {"expert": me + bit - 2 * bit * lax.rem(lax.div(me, bit), 2)}
            return pltpu.make_async_remote_copy(
                small_out, small_got.at[k], sm_send.at[k], sm_recv.at[k], device_id=peer, device_id_type=MESH
            )

        everything = [p for group in head_parts for p in group]
        small = small_swap(0)
        small.start()
        for s in range(total_stages):
            for p in everything:
                p.advance()
            if s <= stages:
                small.wait()
                small_out[...] += small_got[s]
                if s < stages:
                    small = small_swap(s + 1)
                    small.start()
        out = pltpu.make_async_copy(res, sum_out, out_sem)
        out.start()
        out.wait()
        routes[1].wait()


def back_call(n, cc, head_rows, probs, gatt, att, x, norm, own, oth, gmid, vec, small, pg_own, pg_oth, y):
    tokens, width = x.shape
    half = own.shape[2]
    pairs, per = width // 128, half // 128
    rows = n * cc
    stages = n.bit_length() - 1
    split = max(1, min(2, width // (32 * n)))
    parts = 4 * split
    sds, dma, once = jax.ShapeDtypeStruct, pltpu.SemaphoreType.DMA, pl.Buffered(1)
    total = 4 * width

    def pair_of(i):
        return jnp.minimum(i, pairs - 1)

    def head(c):
        return pl.BlockSpec((1, tokens, 128), lambda i: (3 * (pair_of(i) // per) + c, 0, pair_of(i) % per))

    def fixed(shape):
        return pl.BlockSpec(shape, lambda *_: (0,) * len(shape), pipeline_mode=once)

    cols = pl.BlockSpec((tokens, 128), lambda i: (0, pair_of(i)))
    return pl.pallas_call(
        functools.partial(back_kernel, n, cc, pairs),
        grid=(pairs + 7,),
        in_specs=[
            head(0), head(1), head(2), pl.BlockSpec((2, QB, BAND), lambda i: (pair_of(i), 0, 0)), cols, cols,
            fixed((tokens, width)), fixed((tokens, width)),
            pl.BlockSpec((1, width, half), lambda i: (jnp.clip(i - pairs - 3, 0, 2), 0, 0)),
            pl.BlockSpec((1, width, half), lambda i: (jnp.clip(i - pairs, 0, 2), 0, 0)),
            fixed((tokens, width)), fixed(vec.shape), fixed(small.shape), fixed((half, width)), ANY, ANY,
        ],
        out_specs=[fixed((tokens, width)), fixed(small.shape), ANY, ANY, ANY],
        out_shape=[
            sds((tokens, width), F32), sds(small.shape, F32), sds((total, half), BF),
            sds((rows, width), BF), sds((rows, width), BF),
        ],
        scratch_shapes=[
            pltpu.VMEM((tokens, 128), F32), pltpu.VMEM((tokens, 128), F32), pltpu.VMEM((6, tokens, half), BF),
            pltpu.VMEM((tokens, width), F32), pltpu.VMEM((total, half), BF), pltpu.VMEM((total, half), BF),
            pltpu.VMEM((total, half), BF), pltpu.VMEM((3, width, half), BF), pltpu.VMEM((half, width), BF),
            pltpu.VMEM((3, width, half), BF),
            pltpu.VMEM((1 + stages, *small.shape), F32),
            *route_sems(n, 2), dma((4,)), dma((4,)), dma((parts, stages)), dma((parts, stages)),
            dma((parts, stages)), dma((parts, stages)), dma((1 + stages,)), dma((1 + stages,)), dma,
        ],
        compiler_params=params(collective_id=5, has_side_effects=True),
        cost_estimate=cost(5.3e10, 9e7),
        name="back",
    )(head_rows, head_rows, head_rows, probs, gatt, att, x, norm, own, oth, gmid, vec, small, pg_own, pg_oth, y)


def result_kernel(tcol_ref, z0, z1, z2, mid_ref, sum_q, sum_p, xg_ref, wd_ref, wu_ref, out_ref, q_ref, p_ref, xo_ref, do_ref, uo_ref):
    rows = gather_rows(tcol_ref[...], (z0[...], z1[...], z2[...]))
    out_ref[...] = (mid_ref[...] + rows.astype(BF).astype(F32)).astype(BF)
    q_ref[...] = sum_q[...].astype(F32)
    p_ref[...] = sum_p[...].astype(F32)
    xo_ref[...] = xg_ref[...]
    do_ref[...] = wd_ref[...].astype(F32)
    uo_ref[...] = wu_ref[...].astype(F32)


def result_call(tcol, zs, middle, sums, xg, wd, wu):
    tokens, width = middle.shape
    half = sums.shape[1]
    hid = wd.shape[0]
    rows = zs[0].shape[0]
    steps = 8
    tb, qb, pb, wb = tokens // steps, 3 * width // steps, width // steps, hid // steps
    sds = jax.ShapeDtypeStruct
    side = half // pb

    def rows_of(size, cols):
        return pl.BlockSpec((size, cols), lambda i: (i, 0))

    p_out = pl.BlockSpec((pb, half), lambda i: (i % side, i // side))
    return pl.pallas_call(
        result_kernel,
        grid=(steps,),
        in_specs=[
            rows_of(tb, 128), *[whole((rows, width))] * 3, rows_of(tb, width), rows_of(qb, half),
            pl.BlockSpec((pb, half), lambda i: (3 * steps + i, 0)), rows_of(tb, width), rows_of(wb, width),
            rows_of(wb, width),
        ],
        out_specs=[rows_of(tb, width), rows_of(qb, half), p_out, rows_of(tb, width), rows_of(wb, width), rows_of(wb, width)],
        out_shape=[
            sds((tokens, width), BF), sds((3 * width, half), F32), sds((half, width), F32), sds((tokens, width), F32),
            sds((hid, width), F32), sds((hid, width), F32),
        ],
        compiler_params=params(),
        cost_estimate=cost(6 * tokens * rows * width, 6e7),
        name="results",
    )(tcol, *zs, middle, sums, sums, xg, wd, wu)


def on_device(
    tokens, cotangent, segment_ids, expert_ids, qkv_weight, proj_weight, proj_bias, pre_gain, pre_shift,
    mid_gain, mid_shift, up_weight, up_bias, down_weight, down_bias,
):
    n = lax.axis_size("expert")
    count, width = tokens.shape
    cc = 3 * count // (2 * n) // CHUNKS

    def swap(v):
        return lax.ppermute(v, "dp", [(0, 1), (1, 0)])

    down_own, up_own = down_weight[0], up_weight[0]
    up, down = (up_own, swap(up_own)), (down_own, swap(down_own))
    bias = (up_bias, swap(up_bias))
    vec = jnp.stack([pre_gain, pre_shift, proj_bias, mid_gain, mid_shift]).astype(F32)

    tcol, norm, head_rows, att, probs, middle, mid_slots, cot_rows, qkv_oth, proj_oth = front_call(
        n, cc, expert_ids.reshape(1, count), cotangent, tokens, segment_ids, vec, qkv_weight, proj_weight)
    acts, ghs, ub, y, dx, arrived, gm0 = expert_call(n, cc, mid_slots, cot_rows, up, down, bias, down_bias)
    down_grad, up_grad, upbias_grad, downbias_grad, gm1, gm2 = wgrad_call(n, cc, acts, ghs, cot_rows, arrived, ub, dx)

    gmid, gatt, pg_own, pg_oth, small, z0 = middle_back_call(
        n, cc, tcol, (gm0, gm1, gm2), middle, cotangent, vec, proj_weight, proj_oth, att, y)
    input_grad, small, sums, z1, z2 = back_call(
        n, cc, head_rows, probs, gatt, att, tokens, norm, qkv_weight, qkv_oth, gmid, vec, small, pg_own, pg_oth, y)
    output, qkv_grad, proj_grad, input_grad, down_grad, up_grad = result_call(
        tcol, (z0, z1, z2), middle, sums, input_grad, down_grad, up_grad)
    return (
        output, input_grad, qkv_grad.reshape(qkv_weight.shape), proj_grad, small[4], small[0], small[1], small[2], small[3],
        up_grad[None], upbias_grad, down_grad[None], downbias_grad,
    )


def solution(mesh):
    token = P(("dp", "expert"), None)
    in_specs = (
        token, token, token, token, P(None, None, "dp"), P("dp", None), P(), P(), P(), P(), P(),
        P("expert", "dp", None), P("expert", "dp"), P("expert", "dp", None), P("expert", None),
    )
    out_specs = (
        token, token, P(None, None, "dp"), P("dp", None), P(), P(), P(), P(), P(),
        P("expert", "dp", None), P("expert", "dp"), P("expert", "dp", None), P("expert", None),
    )
    return jax.shard_map(on_device, mesh=mesh, in_specs=in_specs, out_specs=out_specs, check_vma=False)
```

time: 1240 us -> 473 us (0.38)
  Pallas kernels: 0 us -> 457 us
  matrix products: 418 us -> 0 us
  waiting for transfers between devices: 334 us -> 0.01 us
  blocking collectives: 163 us -> 0 us
  other arithmetic: 157 us -> 0.62 us
  local copies, waits for them, and re-layouts: 110 us -> 6.87 us
  starting transfers between devices: 31.8 us -> 1.03 us
  between operations: 14.7 us -> 0.92 us
    pallas_call x0 -> x6, Pallas kernels: none -> 457 us  [the longest x1 151 us: back_call(): pl.pallas_call(functools.partial(back_kernel, n, cc, pairs), grid=(pairs...]
    dot_general x26 -> x0, matrix products: 418 us -> none  [the longest x4 64.2 us: masked_scores(): jnp.einsum('qhd,khd->hqk', query_rows, key_rows, preferred_element_type=j...]
    all_to_all x3 -> x0, waiting for transfers between devices: 169 us -> none  [the longest x2 112 us: route_grads(): lax.all_to_all(values, 'expert', split_axis=0, concat_axis=0, tiled=True)]
    psum x1 -> x0, waiting for transfers between devices: 109 us -> none  [on_device(): lax.psum((qkv_part, proj_part, small_pair), 'expert')]
    all_to_all x1 -> x0, blocking collectives: 79 us -> none  [route(): lax.all_to_all(values, 'expert', split_axis=0, concat_axis=0, tiled=True)]
    psum x1 -> x0, blocking collectives: 78.2 us -> none  [on_device(): lax.psum((qkv_part, proj_part, small_pair), 'expert')]
    convert_element_type x12 -> x1, other arithmetic: 68.1 us -> 0.62 us  [on_device(): jnp.stack([pre_gain, pre_shift, proj_bias, mid_gain, mid_shift]).astype(F32)]
    reduce_sum x10 -> x0, other arithmetic: 55.9 us -> none  [the longest x2 28.7 us: attend_forward(): totals = jnp.sum(weights, axis=-1, keepdims=True)]
  transfers between devices with their start and end apart: 12 -> 3, of which waited for: 9 -> 0; matrix products, arithmetic and copies ran while one was open for 17% -> 1% of each run, Pallas kernels for 0% -> 18%
where the time goes in v2:
time: 473 us; the launch traced here: 466 us
  Pallas kernels  457 us (97%)
  local copies, waits for them, and re-layouts  6.87 us (1%)
    pallas_call x1, Pallas kernels, back_call(): pl.pallas_call(functools.partial(back_kernel, n, cc, pairs), grid=(pairs...  151 us
    pallas_call x1, Pallas kernels, expert_call(): pl.pallas_call(functools.partial(expert_kernel, n, cc, own_tiles), grid=(...  109 us
    pallas_call x1, Pallas kernels, front_call(): pl.pallas_call(functools.partial(front_kernel, n, cc, pairs), grid=(8 + p...  81.8 us
    pallas_call x1, Pallas kernels, wgrad_call(): pl.pallas_call(functools.partial(wgrad_kernel, n, cc, tiles), grid=(4 * t...  62 us
    pallas_call x1, Pallas kernels, middle_back_call(): pl.pallas_call(functools.partial(middle_back_kernel, n, cc, tokens // tb)...  33.3 us
    pallas_call x1, Pallas kernels, result_call(): pl.pallas_call(result_kernel, grid=(steps,), in_specs=[rows_of(tb, 128),...  20.4 us
  transfers between devices with their start and end apart: 3, of which 0 were waited for; matrix products, arithmetic and copies ran while one was open for 1% of the time, Pallas kernels for 18%

profile of v2, /device:TPU:0, one launch (start us, length us, event | category | flops | bytes accessed | tf_op | source)
XLA Modules:
  0.0 466.4 jit_solution(2363661977186217774)
XLA Ops:
  0.6 0.5 collective-permute-start
  1.2 0.1 collective-permute-start.1
  1.2 0.4 collective-permute-start.2
  1.7 0.7 stack.20
  2.4 0.7 stack.18
  3.0 0.7 stack.19
  3.7 0.7 stack.21
  4.4 0.7 stack.22
  5.1 0.6 convert_element_type.3.vec_ref
  5.8 81.8 %front.1 = (s32[1024,128]{1,0:T(8,128)}, bf16[1024,1024]{1,0:T(8,128)(2,1)}, bf16[6,1024,512]{2,1,0:T(8,128)(2,1)}, bf16[1024,1024]{1,0:T(8,128)(2,1)}, bf16[16,...) custom-call(s32[1,1024]{1,0:T(1,128)} %bitcast.23, ...), custom_call_target="tpu_custom_call" | custom-call | flops 30000001024 | bytes 60000000 | tf_op jit(solution)/shard_map/front/pallas_call | solution.py:297
  87.6 0.0 collective-permute-done.2.bt_ref
  87.6 0.0 copy-start.2
  87.6 0.0 collective-permute-done.ut_ref
  87.6 0.0 collective-permute-done.1.dt_ref
  87.6 0.6 copy-done.2
  88.2 108.7 %experts.1 = (bf16[3,512,4096]{2,1,0:T(8,128)(2,1)}, bf16[3,512,4096]{2,1,0:T(8,128)(2,1)}, f32[8,4096]{1,0:T(8,128)}, bf16[3,512,1024]{2,1,0:T(8,128)(2,1)}, bf...) custom-call(bf16[1536,1024]{1,0:T(8,128)(2,1)} %get-tuple-element.54.mid_ref, ...), custom_call_target="tpu_custom_call" | custom-call | flops 51999997952 | bytes 80000000 | tf_op jit(solution)/shard_map/experts/pallas_call | solution.py:461
  196.9 62.0 %weight_grads.1 = (bf16[2048,1024]{1,0:T(8,128)(2,1)}, bf16[2048,1024]{1,0:T(8,128)(2,1)}, f32[1,2048]{1,0:T(1,128)}, f32[1,1024]{1,0:T(1,128)}, bf16[512,1024]{1,0:T(8,128)(2,1)}, /*index=5*/bf16[512,1024]{1,0:T(8,128)(2,1)}) custom-call(bf16[3,512,4096]{2,1,0:T(8,128)(2,1)} %get-tuple-element.57.a_ref, bf16[3,512,4096]{2,1,0:T(8,128)(2,1)} %get-tuple-element.58.g_ref, ...), custom_call_target="tpu_custom_call" | custom-call | flops 25999998976 | bytes 80000000 | tf_op jit(solution)/shard_map/weight_grads/pallas_call | solution.py:580
  258.8 33.3 %middle_back.1 = (f32[1024,1024]{1,0:T(8,128)}, bf16[1024,1024]{1,0:T(8,128)(2,1)}, bf16[512,1024]{1,0:T(8,128)(2,1)}, bf16[512,1024]{1,0:T(8,128)(2,1)}, f32[8,1024]{1,0:T(8,128)}, /*index=5*/bf16[512,1024]{1,0:T(8,128)(2,1)}) custom-call(s32[1024,128]{1,0:T(8,128)} %get-tuple-element.53.tcol_ref, bf16[512,1024]{1,0:T(8,128)(2,1)} %get-tuple-element.56.g0, ...), custom_call_target="tpu_custom_call" | custom-call | flops 12000000000 | bytes 30000000 | tf_op jit(solution)/shard_map/middle_back/pallas_call | solution.py:664
  292.2 150.8 %back.1 = (f32[1024,1024]{1,0:T(8,128)}, f32[8,1024]{1,0:T(8,128)}, bf16[4096,512]{1,0:T(8,128)(2,1)}, bf16[512,1024]{1,0:T(8,128)(2,1)}, bf16[512,1024]{1,0:T(8,128)(2,1)}) custom-call(bf16[6,1024,512]{2,1,0:T(8,128)(2,1)} %get-tuple-element.69.q_ref.k_ref.v_ref, bf16[6,1024,512]{2,1,0:T(8,128)(2,1)} %get-tuple-element.69.q_ref.k_ref.v_ref, ...), custom_call_target="tpu_custom_call" | custom-call | flops 52999999488 | bytes 90000000 | tf_op jit(solution)/shard_map/back/pallas_call | solution.py:937
  443.0 1.6 fusion
  444.6 0.0 copy-start
  444.6 0.0 copy-start.1
  444.6 20.4 %results.1 = (bf16[1024,1024]{1,0:T(8,128)(2,1)}, f32[3072,512]{1,0:T(8,128)}, f32[512,1024]{1,0:T(8,128)}, f32[1024,1024]{1,0:T(8,128)}, f32[2048,1024]{1,0:T(8,128)}, /*index=5*/f32[2048,1024]{1,0:T(8,128)}) custom-call(s32[1024,128]{1,0:T(8,128)} %get-tuple-element.53.tcol_ref, bf16[512,1024]{1,0:T(8,128)(2,1)} %get-tuple-element.68.z0, ...), custom_call_target="tpu_custom_call" | custom-call | flops 3221225472 | bytes 60000000 | tf_op jit(solution)/shard_map/results/pallas_call | solution.py:991
  465.0 0.0 copy-done
  465.0 0.6 copy.30
  465.6 0.0 copy-done.1
  465.6 0.6 copy.31
  (1 shorter events, 0.0 us)
Async XLA Ops:
  0.6 86.9 %collective-permute-start = (bf16[2048,1024]{1,0:T(8,128)(2,1)}, bf16[2048,1024]{1,0:T(8,128)(2,1)}, u32[]{:S(2)}, u32[]{:S(2)}) collective-permute-start(bf16[2048,1024]{1,0:T(8,128)(2,1)} %bitcast.19), channel_id=1, source_target_pairs={{0,16},{16,0},{1,17},{17,1},{2,18},{18,2},{3,19},{19,3},{4,20},{20... | collective-permute-start | bytes 12582920 | tf_op jit(solution)/shard_map/ppermute | solution.py:1019
  1.2 86.4 %collective-permute-start.1 = (bf16[2048,1024]{1,0:T(8,128)(2,1)}, bf16[2048,1024]{1,0:T(8,128)(2,1)}, u32[]{:S(2)}, u32[]{:S(2)}) collective-permute-start(bf16[2048,1024]{1,0:T(8,128)(2,1)} %bitcast.21), channel_id=1, source_target_pairs={{0,16},{16,0},{1,17},{17,1},{2,18},{18,2},{3,19},{19,3},{4,20},{20... | collective-permute-start | bytes 12582920 | tf_op jit(solution)/shard_map/ppermute | solution.py:1019
  1.2 86.3 %collective-permute-start.2 = (bf16[1,2048]{1,0:T(2,128)(2,1)}, bf16[1,2048]{1,0:T(2,128)(2,1)S(1)}, u32[]{:S(2)}, u32[]{:S(2)}) collective-permute-start(bf16[1,2048]{1,0:T(2,128)(2,1)} %bo_ref.1), channel_id=1, source_target_pairs={{0,16},{16,0},{1,17},{17,1},{2,18},{18,2},{3,19},{19,3},{4,20},{20... | collective-permute-start | bytes 12296 | tf_op jit(solution)/shard_map/ppermute | solution.py:1019
  87.6 0.6 copy-start.2
  444.6 20.4 %copy-start = (f32[1,2048]{1,0:T(1,128)S(1)}, f32[1,2048]{1,0:T(1,128)}, u32[]{:S(2)}) copy-start(f32[1,2048]{1,0:T(1,128)} %get-tuple-element.121) | copy-start | bytes 24580
  444.6 21.0 %copy-start.1 = (f32[1,1024]{1,0:T(1,128)S(1)}, f32[1,1024]{1,0:T(1,128)}, u32[]{:S(2)}) copy-start(f32[1,1024]{1,0:T(1,128)} %get-tuple-element.123) | copy-start | bytes 12292

commit v3 on v2

--- a/solution.py
+++ b/solution.py
@@ -127,7 +127,7 @@
 
 def front_kernel(
     n, cc, pairs, ids_ref, cot_ref, x_ref, seg_ref, vec_ref, w_ref, w_any, p_ref, p_any,
-    tcol_ref, norm_ref, hr_ref, att_ref, prob_ref, mid_ref, slot_ref, arr_ref, wo_out, po_out,
+    tcol_ref, norm_t, hr_ref, att_ref, att_t, prob_ref, mid_ref, slot_ref, arr_ref, wo_out, po_out,
     row_s, cs_s, norm_s, hr_s, wo_s, po_s, bias_s, low_s, send, recv, local, dsend, drecv, dlocal,
 ):
     step = pl.program_id(0)
@@ -196,7 +196,7 @@
             unit, _ = unit_of(x_ref[at, :].astype(F32))
             low = (unit * gain + shift).astype(BF)
             norm_s[at, :] = low
-            norm_ref[at, :] = low
+            norm_t[:, at] = jnp.transpose(low)
             return 0
 
         lax.fori_loop(0, tokens // 128, body, 0)
@@ -251,7 +251,9 @@
                 prob_ref[j, :, OFFSET[i]:OFFSET[i] + w] = probs
                 parts.append(dot(probs, values))
             both = jnp.where(lane_pick(128, True), parts[0], parts[1])
-            att_ref[i * QB:(i + 1) * QB, block_of(pair, 128)] = both.astype(BF)
+            both = both.astype(BF)
+            att_ref[i * QB:(i + 1) * QB, block_of(pair, 128)] = both
+            att_t[block_of(pair, 128), i * QB:(i + 1) * QB] = jnp.transpose(both)
 
     @pl.when(step == first_pair + pairs)
     def _():
@@ -304,14 +306,14 @@
             whole((half, width)), ANY,
         ],
         out_specs=[
-            whole((tokens, 128)), whole((tokens, width)),
+            whole((tokens, 128)), whole((width, tokens)),
             pl.BlockSpec((1, tokens, half), lambda i: (jnp.clip(i - 1, 0, 5), 0, 0)),
-            whole((tokens, width)), pl.BlockSpec((2, QB, BAND), lambda i: (pair_of(i), 0, 0)),
+            whole((tokens, width)), whole((width, tokens)), pl.BlockSpec((2, QB, BAND), lambda i: (pair_of(i), 0, 0)),
             whole((tokens, width)), whole((CHUNKS * rows, width)), ANY, ANY, ANY,
         ],
         out_shape=[
-            sds((tokens, 128), jnp.int32), sds((tokens, width), BF), sds((6, tokens, half), BF),
-            sds((tokens, width), BF), sds((2 * pairs, QB, BAND), BF), sds((tokens, width), F32),
+            sds((tokens, 128), jnp.int32), sds((width, tokens), BF), sds((6, tokens, half), BF),
+            sds((tokens, width), BF), sds((width, tokens), BF), sds((2 * pairs, QB, BAND), BF), sds((tokens, width), F32),
             sds((CHUNKS * rows, width), BF), sds((CHUNKS, rows, width), BF), sds(qkv.shape, BF), sds(proj.shape, BF),
         ],
         scratch_shapes=[
@@ -365,10 +367,7 @@
         @pl.when(step == (c + 1) * tiles)
         def _():
             ins[c].wait()
-            if c + 1 < CHUNKS:
-                ins[c + 1].start()
-            else:
-                back.start()
+            (ins[c + 1] if c + 1 < CHUNKS else back).start()
             keep(c).start()
 
     lanes = block_of(tile, TILE)
@@ -511,7 +510,8 @@
     @pl.when(step == 0)
     def _():
         greet(n, True)
-        routes[0].start()
+        for r in routes:
+            r.start()
         total = jnp.zeros((1, c_ref.shape[2]), F32)
         for c in range(CHUNKS):
             total = total + jnp.sum(c_ref[c].astype(F32), axis=0, keepdims=True)
@@ -522,8 +522,6 @@
 
     @pl.when(step == 2 * tiles)
     def _():
-        routes[0].wait()
-        routes[1].start()
         small.wait()
         ubg_ref[...] = ub_ref[0:1, 0:hid] + got_s[0:1, 0:hid]
         cbg_ref[...] = small_s[0:1, hid:] + got_s[0:1, hid:]
@@ -550,7 +548,8 @@
 
     @pl.when(step == 4 * tiles - 1)
     def _():
-        routes[1].wait()
+        for r in routes:
+            r.wait()
 
 
 def wgrad_call(n, cc, acts, ghs, cot, rows_in, ub, dx):
@@ -617,7 +616,7 @@
 
 
 def middle_back_kernel(
-    n, cc, blocks, tcol_ref, g0, g1, g2, mid_ref, cot_ref, vec_ref, own_ref, oth_ref, att_ref, y_src,
+    n, cc, blocks, tcol_ref, g0, g1, g2, mid_ref, cot_ref, vec_ref, own_ref, oth_ref, att_t, y_src,
     gmid_ref, gatt_ref, pg_own, pg_oth, small_ref, y_dst, gb_s, send, recv, local,
 ):
     route = Route(
@@ -649,12 +648,12 @@
 
     @pl.when(step == blocks - 1)
     def _():
-        pg_own[...] = dot_tn(att_ref[:, 0:half], gb_s[...]).astype(BF)
-        pg_oth[...] = dot_tn(att_ref[:, half:2 * half], gb_s[...]).astype(BF)
+        pg_own[...] = dot(att_t[0:half, :], gb_s[...]).astype(BF)
+        pg_oth[...] = dot(att_t[half:2 * half, :], gb_s[...]).astype(BF)
         route.wait()
 
 
-def middle_back_call(n, cc, tcol, grads, middle, cot, vec, proj_own, proj_oth, att, y):
+def middle_back_call(n, cc, tcol, grads, middle, cot, vec, proj_own, proj_oth, att_t, y):
     tokens, width = middle.shape
     half = proj_own.shape[0]
     tb = 256
@@ -677,13 +676,14 @@
         compiler_params=params(collective_id=4, has_side_effects=True),
         cost_estimate=cost(1.2e10, 3e7),
         name="middle_back",
-    )(tcol, *grads, middle, cot, vec, proj_own, proj_oth, att, y)
+    )(tcol, *grads, middle, cot, vec, proj_own, proj_oth, att_t, y)
 
 
 class Part:
-    def __init__(self, index, base, length, order, me, refs):
+    def __init__(self, index, base, length, order, me, refs, sems):
         self.index, self.base, self.total, self.order, self.me = index, base, length, order, me
-        self.acc, self.rcv, self.res, self.rs_send, self.rs_recv, self.ag_send, self.ag_recv = refs
+        self.acc, self.rcv, self.res = refs
+        self.rs_send, self.rs_recv, self.ag_send, self.ag_recv = sems
         self.stages, self.stage = len(order), 0
         self.step = length >> len(order)
 
@@ -743,17 +743,18 @@
 
 
 def back_kernel(
-    n, cc, pairs, q_ref, k_ref, v_ref, prob_ref, do_ref, o_ref, x_ref, norm_ref, own_ref, oth_ref, gmid_ref,
-    vec_ref, small_ref, pg_own, pg_oth, y_src,
-    xg_ref, small_out, sum_out, z1, z2,
-    dk_s, dv_s, gh_s, gnp_s, acc, rcv, res, got, pgot, snd, small_got,
+    n, cc, groups, q_ref, k_ref, v_ref, prob_ref, do_ref, o_ref, x_ref, norm_t, own_ref, oth_ref,
+    vec_ref, small_ref, pg_own, pg_oth, gmid_any, y_src,
+    xg_ref, small_out, sum_q, sum_p, z1, z2,
+    dk_s, dv_s, gh_s, gnp_s, acc, rcv, res, p_acc, p_rcv, p_res, got, pgot, snd, mine_s, small_got,
     send, recv, local, dsend, drecv, rs_send, rs_recv, ag_send, ag_recv, sm_send, sm_recv, out_sem,
 ):
     step = pl.program_id(0)
     tokens, width = x_ref.shape
     half = own_ref.shape[2]
     scale = HEAD_DIM ** -0.5
-    per = half // 128
+    last = 3 * groups
+    kind, group = lax.rem(step, 3), lax.div(step, 3)
     me = lax.axis_index("expert")
     stages = n.bit_length() - 1
     routes = [
@@ -764,33 +765,44 @@
         for c, z in ((1, z1), (2, z2))
     ]
 
-    split = max(1, min(2, width // (32 * n)))
+    split = 2 if width >= 32 * n else 1
     size = width // split
-    turn = max(1, stages - 1)
-    refs = (acc, rcv, res, rs_send, rs_recv, ag_send, ag_recv)
-
-    def part(i):
-        order = [(i + s) % turn for s in range(turn)] + ([turn] if stages > turn else [])
-        return Part(i, i * size, size, order, me, refs)
-
-    proj_parts = [part(3 * split + i) for i in range(split)]
-    head_parts = [[part(c * split + i) for i in range(split)] for c in range(3)]
-
-    def dp_swap(c):
-        src = snd.at[c] if c < 3 else pg_oth
-        dst = got.at[c] if c < 3 else pgot
-        return to_partner(src, dst, dsend.at[c], drecv.at[c])
+    sems = (rs_send, rs_recv, ag_send, ag_recv)
+    order = list(range(stages))
+    swapped = [1, 0, *order[2:]]
+
+    def parts_of(first, at, refs):
+        return [
+            Part(first + i, at * width + i * size, size, order if i % 2 == 0 else swapped, me, refs, sems)
+            for i in range(split)
+        ]
+
+    head_parts = [parts_of(k * split, k, (acc, rcv, res)) for k in range(groups)]
+    proj_parts = parts_of(groups * split, 0, (p_acc, p_rcv, p_res))
+
+    def dp_swap(k):
+        src, dst = (snd.at[k], got.at[k]) if k < groups else (pg_oth, pgot)
+        return to_partner(src, dst, dsend.at[k], drecv.at[k])
+
+    def bring_to(parts, goal):
+        while parts[0].stage < min(goal, 2 * stages):
+            for p in parts:
+                p.advance()
+
+    def seed(k):
+        return pltpu.make_async_copy(gmid_any, xg_ref, out_sem.at[2])
 
     @pl.when(step == 0)
     def _():
         greet(n, True)
-        dp_swap(3).start()
-        routes[0].start()
-        gnp_s[...] = jnp.zeros_like(gnp_s)
-
-    @pl.when(step < pairs)
-    def _():
-        side, lanes = lax.div(step, per), block_of(lax.rem(step, per), 128)
+        dp_swap(groups).start()
+        for r in routes:
+            r.start()
+        seed(0).start()
+
+    @pl.when((kind < 2) & (step < last))
+    def _():
+        side, lanes = 1 - kind, block_of(group, 128)
         dk_s[...] = jnp.zeros_like(dk_s)
         dv_s[...] = jnp.zeros_like(dv_s)
         for i in range(BLOCKS):
@@ -816,75 +828,42 @@
         gh_s[3 * side + 1, :, lanes] = (dk_s[...] * scale).astype(BF)
         gh_s[3 * side + 2, :, lanes] = dv_s[...].astype(BF)
 
-    def bring_to(parts, goal):
-        while parts[0].stage < goal:
-            for p in parts:
-                p.advance()
-
-    total_stages = 2 * stages
+    for k in range(groups):
+        @pl.when(step == 3 * k + 2)
+        def _():
+            at = slice(k * 128, (k + 1) * 128)
+            for c in range(3):
+                both = dot(norm_t[...], jnp.concatenate([gh_s[3 + c, :, at], gh_s[c, :, at]], axis=1))
+                snd[k, :, c * 128:(c + 1) * 128] = both[:, 0:128].astype(BF)
+                mine_s[:, c * 128:(c + 1) * 128] = both[:, 128:256]
+            dp_swap(k).start()
+
+        @pl.when(step == 3 * k + 3)
+        def _():
+            dp_swap(k).wait()
+            acc[k * width:(k + 1) * width, :] = (mine_s[...] + got[k].astype(F32)).astype(BF)
+            for p in head_parts[k]:
+                p.begin()
 
     @pl.when(step == 1)
     def _():
-        dp_swap(3).wait()
-        base = 3 * width
-        for b in range(width // half):
-            for p in range(half // 128):
-                at = slice(p * 128, (p + 1) * 128)
-                acc[base + b * half + p * 128:base + b * half + (p + 1) * 128, :] = (
-                    pg_own[at, b * half:(b + 1) * half].astype(F32)
-                    + pgot[at, b * half:(b + 1) * half].astype(F32)
-                ).astype(BF)
+        dp_swap(groups).wait()
+        rows = pgot.shape[0]
+        for b in range(width // rows):
+            at = slice(b * rows, (b + 1) * rows)
+            p_acc[at, :] = (pg_own[:, at].astype(F32) + pgot[:, at].astype(F32)).astype(BF)
         for p in proj_parts:
             p.begin()
 
-    last = pairs + 6
-    for t in range(2, last):
-        goal = t - 1 if t < last - 1 else total_stages
-        goal = min(goal, total_stages)
-        prev = min(t - 2, total_stages)
-        if goal > prev:
-            @pl.when(step == t)
-            def _():
-                bring_to(proj_parts, goal)
-
-    @pl.when(step == pairs - 1)
-    def _():
-        routes[0].wait()
-        routes[1].start()
-
-    for c in range(3):
-        @pl.when(step == pairs + c)
+    for t in range(3, last):
+        @pl.when(step == t)
         def _():
-            g = gh_s[3 + c]
-            snd[c] = dot_tn(norm_ref[...], g).astype(BF)
-            dp_swap(c).start()
-            gnp_s[...] += dot_nt(g, oth_ref[0])
-
-        @pl.when(step == pairs + 3 + c)
-        def _():
-            g = gh_s[c]
-            mine = dot_tn(norm_ref[...], g)
-            dp_swap(c).wait()
-            acc[c * width:(c + 1) * width, :] = (mine + got[c].astype(F32)).astype(BF)
-            for p in head_parts[c]:
-                p.begin()
-            gnp_s[...] += dot_nt(g, own_ref[0])
+            bring_to(proj_parts, sum(t >= m for m in (5, 7, 9, 11)))
+            for k in range(groups):
+                bring_to(head_parts[k], sum(t >= 3 * k + m for m in (7, 9, 11)))
 
     @pl.when(step == last)
     def _():
-        small_out[...] = small_ref[...]
-
-        def body(b, _):
-            at = block_of(b, 128)
-            grad = gnp_s[at, :]
-            unit, inverse = unit_of(x_ref[at, :].astype(F32))
-            xg_ref[at, :] = gmid_ref[at, :] + norm_back(grad, unit, inverse, vec_ref[PRE_GAIN:PRE_GAIN + 1, :])
-            small_out[0:1, :] += jnp.sum(grad * unit, axis=0, keepdims=True)
-            small_out[1:2, :] += jnp.sum(grad, axis=0, keepdims=True)
-            return 0
-
-        lax.fori_loop(0, tokens // 128, body, 0)
-
         def small_swap(k):
             if k == 0:
                 peer = {"dp": 1 - lax.axis_index("dp")}
@@ -895,116 +874,167 @@
                 small_out, small_got.at[k], sm_send.at[k], sm_recv.at[k], device_id=peer, device_id_type=MESH
             )
 
-        everything = [p for group in head_parts for p in group]
+        def turn():
+            for some in [proj_parts, *head_parts]:
+                for p in some:
+                    if p.stage < 2 * stages:
+                        p.advance()
+
+        for c in range(3):
+            if c:
+                turn()
+            term = dot_nt(gh_s[c], own_ref[c]) + dot_nt(gh_s[3 + c], oth_ref[c])
+            if c:
+                gnp_s[...] += term
+            else:
+                gnp_s[...] = term
+        turn()
+        seed(0).wait()
+        small_out[...] = small_ref[...]
+
+        def body(b, _):
+            at = block_of(b, 128)
+            grad = gnp_s[at, :]
+            unit, inverse = unit_of(x_ref[at, :].astype(F32))
+            xg_ref[at, :] = xg_ref[at, :] + norm_back(grad, unit, inverse, vec_ref[PRE_GAIN:PRE_GAIN + 1, :])
+            small_out[0:1, :] += jnp.sum(grad * unit, axis=0, keepdims=True)
+            small_out[1:2, :] += jnp.sum(grad, axis=0, keepdims=True)
+            return 0
+
+        lax.fori_loop(0, tokens // 128, body, 0)
         small = small_swap(0)
         small.start()
-        for s in range(total_stages):
-            for p in everything:
-                p.advance()
+        for s in range(2 * stages - 2):
+            turn()
             if s <= stages:
                 small.wait()
                 small_out[...] += small_got[s]
                 if s < stages:
                     small = small_swap(s + 1)
                     small.start()
-        out = pltpu.make_async_copy(res, sum_out, out_sem)
-        out.start()
-        out.wait()
-        routes[1].wait()
-
-
-def back_call(n, cc, head_rows, probs, gatt, att, x, norm, own, oth, gmid, vec, small, pg_own, pg_oth, y):
+        outs = [
+            pltpu.make_async_copy(res, sum_q, out_sem.at[0]),
+            pltpu.make_async_copy(p_res, sum_p, out_sem.at[1]),
+        ]
+        for out in outs:
+            out.start()
+        for out in outs:
+            out.wait()
+        for r in routes:
+            r.wait()
+
+
+def back_call(n, cc, head_rows, probs, gatt, att, x, norm_t, own, oth, gmid, vec, small, pg_own, pg_oth, y):
     tokens, width = x.shape
     half = own.shape[2]
-    pairs, per = width // 128, half // 128
+    groups = half // 128
+    last = 3 * groups
     rows = n * cc
     stages = n.bit_length() - 1
-    split = max(1, min(2, width // (32 * n)))
-    parts = 4 * split
+    parts = (groups + 1) * (2 if width >= 32 * n else 1)
     sds, dma, once = jax.ShapeDtypeStruct, pltpu.SemaphoreType.DMA, pl.Buffered(1)
-    total = 4 * width
-
-    def pair_of(i):
-        return jnp.minimum(i, pairs - 1)
+
+    def place(i):
+        i = jnp.minimum(i, last - 1)
+        return jnp.maximum(1 - i % 3, 0), i // 3
 
     def head(c):
-        return pl.BlockSpec((1, tokens, 128), lambda i: (3 * (pair_of(i) // per) + c, 0, pair_of(i) % per))
+        def index(i):
+            side, k = place(i)
+            return (3 * side + c, 0, k)
+
+        return pl.BlockSpec((1, tokens, 128), index)
+
+    def pair(i):
+        side, k = place(i)
+        return side * groups + k
 
     def fixed(shape):
         return pl.BlockSpec(shape, lambda *_: (0,) * len(shape), pipeline_mode=once)
 
-    cols = pl.BlockSpec((tokens, 128), lambda i: (0, pair_of(i)))
+    cols = pl.BlockSpec((tokens, 128), lambda i: (0, pair(i)))
+    sums = pltpu.VMEM((groups * width, 384), BF)
+    p_sums = pltpu.VMEM((width, half), BF)
     return pl.pallas_call(
-        functools.partial(back_kernel, n, cc, pairs),
-        grid=(pairs + 7,),
+        functools.partial(back_kernel, n, cc, groups),
+        grid=(last + 1,),
         in_specs=[
-            head(0), head(1), head(2), pl.BlockSpec((2, QB, BAND), lambda i: (pair_of(i), 0, 0)), cols, cols,
-            fixed((tokens, width)), fixed((tokens, width)),
-            pl.BlockSpec((1, width, half), lambda i: (jnp.clip(i - pairs - 3, 0, 2), 0, 0)),
-            pl.BlockSpec((1, width, half), lambda i: (jnp.clip(i - pairs, 0, 2), 0, 0)),
-            fixed((tokens, width)), fixed(vec.shape), fixed(small.shape), fixed((half, width)), ANY, ANY,
-        ],
-        out_specs=[fixed((tokens, width)), fixed(small.shape), ANY, ANY, ANY],
+            head(0), head(1), head(2), pl.BlockSpec((2, QB, BAND), lambda i: (pair(i), 0, 0)), cols, cols,
+            fixed((tokens, width)), fixed((width, tokens)), fixed(own.shape), fixed(oth.shape),
+            fixed(vec.shape), fixed(small.shape), fixed((half, width)), ANY, ANY, ANY,
+        ],
+        out_specs=[fixed((tokens, width)), fixed(small.shape), ANY, ANY, ANY, ANY],
         out_shape=[
-            sds((tokens, width), F32), sds(small.shape, F32), sds((total, half), BF),
+            sds((tokens, width), F32), sds(small.shape, F32), sds((groups * width, 384), BF), sds((width, half), BF),
             sds((rows, width), BF), sds((rows, width), BF),
         ],
         scratch_shapes=[
             pltpu.VMEM((tokens, 128), F32), pltpu.VMEM((tokens, 128), F32), pltpu.VMEM((6, tokens, half), BF),
-            pltpu.VMEM((tokens, width), F32), pltpu.VMEM((total, half), BF), pltpu.VMEM((total, half), BF),
-            pltpu.VMEM((total, half), BF), pltpu.VMEM((3, width, half), BF), pltpu.VMEM((half, width), BF),
-            pltpu.VMEM((3, width, half), BF),
+            pltpu.VMEM((tokens, width), F32), sums, sums, sums, p_sums, p_sums, p_sums,
+            pltpu.VMEM((groups, width, 384), BF), pltpu.VMEM((half, width), BF),
+            pltpu.VMEM((groups, width, 384), BF), pltpu.VMEM((width, 384), F32),
             pltpu.VMEM((1 + stages, *small.shape), F32),
-            *route_sems(n, 2), dma((4,)), dma((4,)), dma((parts, stages)), dma((parts, stages)),
-            dma((parts, stages)), dma((parts, stages)), dma((1 + stages,)), dma((1 + stages,)), dma,
+            *route_sems(n, 2), dma((groups + 1,)), dma((groups + 1,)), dma((parts, stages)), dma((parts, stages)),
+            dma((parts, stages)), dma((parts, stages)), dma((1 + stages,)), dma((1 + stages,)), dma((3,)),
         ],
         compiler_params=params(collective_id=5, has_side_effects=True),
         cost_estimate=cost(5.3e10, 9e7),
         name="back",
-    )(head_rows, head_rows, head_rows, probs, gatt, att, x, norm, own, oth, gmid, vec, small, pg_own, pg_oth, y)
+    )(
+        head_rows, head_rows, head_rows, probs, gatt, att, x, norm_t, own, oth, vec, small, pg_own, pg_oth, gmid, y
+    )
 
 
 def result_kernel(tcol_ref, z0, z1, z2, mid_ref, sum_q, sum_p, xg_ref, wd_ref, wu_ref, out_ref, q_ref, p_ref, xo_ref, do_ref, uo_ref):
     rows = gather_rows(tcol_ref[...], (z0[...], z1[...], z2[...]))
     out_ref[...] = (mid_ref[...] + rows.astype(BF).astype(F32)).astype(BF)
-    q_ref[...] = sum_q[...].astype(F32)
-    p_ref[...] = sum_p[...].astype(F32)
+    for c in range(3):
+        for k in range(sum_q.shape[0]):
+            q_ref[c, :, k * 128:(k + 1) * 128] = sum_q[k, :, c * 128:(c + 1) * 128].astype(F32)
+    half = sum_p.shape[2]
+    for b in range(sum_p.shape[0]):
+        p_ref[:, b * half:(b + 1) * half] = sum_p[b].astype(F32)
     xo_ref[...] = xg_ref[...]
     do_ref[...] = wd_ref[...].astype(F32)
     uo_ref[...] = wu_ref[...].astype(F32)
 
 
-def result_call(tcol, zs, middle, sums, xg, wd, wu):
+def result_call(tcol, zs, middle, sum_q, sum_p, xg, wd, wu):
     tokens, width = middle.shape
-    half = sums.shape[1]
+    half = sum_p.shape[1]
+    groups = half // 128
     hid = wd.shape[0]
     rows = zs[0].shape[0]
     steps = 8
-    tb, qb, pb, wb = tokens // steps, 3 * width // steps, width // steps, hid // steps
+    tb, qb, pb, wb = tokens // steps, width // steps, half // steps, hid // steps
     sds = jax.ShapeDtypeStruct
-    side = half // pb
+    sum_q = sum_q.reshape(groups, width, 384)
+    sum_p = sum_p.reshape(width // half, half, half)
 
     def rows_of(size, cols):
         return pl.BlockSpec((size, cols), lambda i: (i, 0))
 
-    p_out = pl.BlockSpec((pb, half), lambda i: (i % side, i // side))
     return pl.pallas_call(
         result_kernel,
         grid=(steps,),
         in_specs=[
-            rows_of(tb, 128), *[whole((rows, width))] * 3, rows_of(tb, width), rows_of(qb, half),
-            pl.BlockSpec((pb, half), lambda i: (3 * steps + i, 0)), rows_of(tb, width), rows_of(wb, width),
+            rows_of(tb, 128), *[whole((rows, width))] * 3, rows_of(tb, width),
+            pl.BlockSpec((groups, qb, 384), lambda i: (0, i, 0)),
+            pl.BlockSpec((width // half, pb, half), lambda i: (0, i, 0)), rows_of(tb, width), rows_of(wb, width),
             rows_of(wb, width),
         ],
-        out_specs=[rows_of(tb, width), rows_of(qb, half), p_out, rows_of(tb, width), rows_of(wb, width), rows_of(wb, width)],
+        out_specs=[
+            rows_of(tb, width), pl.BlockSpec((3, qb, half), lambda i: (0, i, 0)), rows_of(pb, width),
+            rows_of(tb, width), rows_of(wb, width), rows_of(wb, width),
+        ],
         out_shape=[
-            sds((tokens, width), BF), sds((3 * width, half), F32), sds((half, width), F32), sds((tokens, width), F32),
+            sds((tokens, width), BF), sds((3, width, half), F32), sds((half, width), F32), sds((tokens, width), F32),
             sds((hid, width), F32), sds((hid, width), F32),
         ],
         compiler_params=params(),
         cost_estimate=cost(6 * tokens * rows * width, 6e7),
         name="results",
-    )(tcol, *zs, middle, sums, sums, xg, wd, wu)
+    )(tcol, *zs, middle, sum_q, sum_p, xg, wd, wu)
 
 
 def on_device(
@@ -1023,19 +1053,19 @@
     bias = (up_bias, swap(up_bias))
     vec = jnp.stack([pre_gain, pre_shift, proj_bias, mid_gain, mid_shift]).astype(F32)
 
-    tcol, norm, head_rows, att, probs, middle, mid_slots, cot_rows, qkv_oth, proj_oth = front_call(
+    tcol, norm_t, head_rows, att, att_t, probs, middle, mid_slots, cot_rows, qkv_oth, proj_oth = front_call(
         n, cc, expert_ids.reshape(1, count), cotangent, tokens, segment_ids, vec, qkv_weight, proj_weight)
     acts, ghs, ub, y, dx, arrived, gm0 = expert_call(n, cc, mid_slots, cot_rows, up, down, bias, down_bias)
     down_grad, up_grad, upbias_grad, downbias_grad, gm1, gm2 = wgrad_call(n, cc, acts, ghs, cot_rows, arrived, ub, dx)
 
     gmid, gatt, pg_own, pg_oth, small, z0 = middle_back_call(
-        n, cc, tcol, (gm0, gm1, gm2), middle, cotangent, vec, proj_weight, proj_oth, att, y)
-    input_grad, small, sums, z1, z2 = back_call(
-        n, cc, head_rows, probs, gatt, att, tokens, norm, qkv_weight, qkv_oth, gmid, vec, small, pg_own, pg_oth, y)
+        n, cc, tcol, (gm0, gm1, gm2), middle, cotangent, vec, proj_weight, proj_oth, att_t, y)
+    input_grad, small, sum_q, sum_p, z1, z2 = back_call(
+        n, cc, head_rows, probs, gatt, att, tokens, norm_t, qkv_weight, qkv_oth, gmid, vec, small, pg_own, pg_oth, y)
     output, qkv_grad, proj_grad, input_grad, down_grad, up_grad = result_call(
-        tcol, (z0, z1, z2), middle, sums, input_grad, down_grad, up_grad)
+        tcol, (z0, z1, z2), middle, sum_q, sum_p, input_grad, down_grad, up_grad)
     return (
-        output, input_grad, qkv_grad.reshape(qkv_weight.shape), proj_grad, small[4], small[0], small[1], small[2], small[3],
+        output, input_grad, qkv_grad, proj_grad, small[4], small[0], small[1], small[2], small[3],
         up_grad[None], upbias_grad, down_grad[None], downbias_grad,
     )
 

time: 473 us -> 447 us (0.945)
  Pallas kernels: 457 us -> 431 us
    pallas_call x1, Pallas kernels: 151 us -> 124 us  [back_call(): pl.pallas_call(functools.partial(back_kernel, n, cc, groups), grid=(last...]
  transfers between devices with their start and end apart: 3 -> 3, of which waited for: 0 -> 0; matrix products, arithmetic and copies ran while one was open for 1% -> 1% of each run, Pallas kernels for 18% -> 19%
where the time goes in v3:
time: 447 us; the launch traced here: 441 us
  Pallas kernels  431 us (96%)
  local copies, waits for them, and re-layouts  6.87 us (2%)
    pallas_call x1, Pallas kernels, back_call(): pl.pallas_call(functools.partial(back_kernel, n, cc, groups), grid=(last...  124 us
    pallas_call x1, Pallas kernels, expert_call(): pl.pallas_call(functools.partial(expert_kernel, n, cc, own_tiles), grid=(...  109 us
    pallas_call x1, Pallas kernels, front_call(): pl.pallas_call(functools.partial(front_kernel, n, cc, pairs), grid=(8 + p...  82.5 us
    pallas_call x1, Pallas kernels, wgrad_call(): pl.pallas_call(functools.partial(wgrad_kernel, n, cc, tiles), grid=(4 * t...  61 us
    pallas_call x1, Pallas kernels, middle_back_call(): pl.pallas_call(functools.partial(middle_back_kernel, n, cc, tokens // tb)...  34.3 us
    pallas_call x1, Pallas kernels, result_call(): pl.pallas_call(result_kernel, grid=(steps,), in_specs=[rows_of(tb, 128),...  20.9 us
  transfers between devices with their start and end apart: 3, of which 0 were waited for; matrix products, arithmetic and copies ran while one was open for 1% of the time, Pallas kernels for 19%

profile of v3, /device:TPU:0, one launch (start us, length us, event | category | flops | bytes accessed | tf_op | source)
XLA Modules:
  0.0 440.6 jit_solution(17081520774194610141)
XLA Ops:
  0.6 0.5 collective-permute-start
  1.2 0.1 collective-permute-start.1
  1.2 0.4 collective-permute-start.2
  1.7 0.7 stack.20
  2.4 0.7 stack.18
  3.0 0.7 stack.19
  3.7 0.7 stack.21
  4.4 0.7 stack.22
  5.1 0.6 convert_element_type.3.vec_ref
  5.8 82.5 %front.1 = (s32[1024,128]{1,0:T(8,128)}, bf16[1024,1024]{1,0:T(8,128)(2,1)}, bf16[6,1024,512]{2,1,0:T(8,128)(2,1)}, bf16[1024,1024]{1,0:T(8,128)(2,1)}, bf16[102...) custom-call(s32[1,1024]{1,0:T(1,128)} %bitcast.25, ...), custom_call_target="tpu_custom_call" | custom-call | flops 30000001024 | bytes 60000000 | tf_op jit(solution)/shard_map/front/pallas_call | solution.py:299
  88.2 0.0 collective-permute-done.2.bt_ref
  88.3 0.0 copy-start.2
  88.3 0.0 collective-permute-done.ut_ref
  88.3 0.0 collective-permute-done.1.dt_ref
  88.3 0.6 copy-done.2
  88.9 108.9 %experts.1 = (bf16[3,512,4096]{2,1,0:T(8,128)(2,1)}, bf16[3,512,4096]{2,1,0:T(8,128)(2,1)}, f32[8,4096]{1,0:T(8,128)}, bf16[3,512,1024]{2,1,0:T(8,128)(2,1)}, bf...) custom-call(bf16[1536,1024]{1,0:T(8,128)(2,1)} %get-tuple-element.56.mid_ref, ...), custom_call_target="tpu_custom_call" | custom-call | flops 51999997952 | bytes 80000000 | tf_op jit(solution)/shard_map/experts/pallas_call | solution.py:460
  197.8 61.0 %weight_grads.1 = (bf16[2048,1024]{1,0:T(8,128)(2,1)}, bf16[2048,1024]{1,0:T(8,128)(2,1)}, f32[1,2048]{1,0:T(1,128)}, f32[1,1024]{1,0:T(1,128)}, bf16[512,1024]{1,0:T(8,128)(2,1)}, /*index=5*/bf16[512,1024]{1,0:T(8,128)(2,1)}) custom-call(bf16[3,512,4096]{2,1,0:T(8,128)(2,1)} %get-tuple-element.59.a_ref, bf16[3,512,4096]{2,1,0:T(8,128)(2,1)} %get-tuple-element.60.g_ref, ...), custom_call_target="tpu_custom_call" | custom-call | flops 25999998976 | bytes 80000000 | tf_op jit(solution)/shard_map/weight_grads/pallas_call | solution.py:579
  258.8 34.3 %middle_back.1 = (f32[1024,1024]{1,0:T(8,128)}, bf16[1024,1024]{1,0:T(8,128)(2,1)}, bf16[512,1024]{1,0:T(8,128)(2,1)}, bf16[512,1024]{1,0:T(8,128)(2,1)}, f32[8,1024]{1,0:T(8,128)}, /*index=5*/bf16[512,1024]{1,0:T(8,128)(2,1)}) custom-call(s32[1024,128]{1,0:T(8,128)} %get-tuple-element.55.tcol_ref, bf16[512,1024]{1,0:T(8,128)(2,1)} %get-tuple-element.58.g0, ...), custom_call_target="tpu_custom_call" | custom-call | flops 12000000000 | bytes 30000000 | tf_op jit(solution)/shard_map/middle_back/pallas_call | solution.py:663
  293.1 123.6 %back.1 = (f32[1024,1024]{1,0:T(8,128)}, f32[8,1024]{1,0:T(8,128)}, bf16[4096,384]{1,0:T(8,128)(2,1)}, bf16[1024,512]{1,0:T(8,128)(2,1)}, bf16[512,1024]{1,0:T(8,128)(2,1)}, /*index=5*/bf16[512,1024]{1,0:T(8,128)(2,1)}) custom-call(bf16[6,1024,512]{2,1,0:T(8,128)(2,1)} %get-tuple-element.71.q_ref.k_ref.v_ref, ...), custom_call_target="tpu_custom_call" | custom-call | flops 52999999488 | bytes 90000000 | tf_op jit(solution)/shard_map/back/pallas_call | solution.py:958
  416.7 1.6 fusion
  418.4 0.0 copy-start
  418.4 0.0 copy-start.1
  418.4 20.9 %results.1 = (bf16[1024,1024]{1,0:T(8,128)(2,1)}, f32[3,1024,512]{2,1,0:T(8,128)}, f32[512,1024]{1,0:T(8,128)}, f32[1024,1024]{1,0:T(8,128)}, f32[2048,1024]{1,0:T(8,128)}, /*index=5*/f32[2048,1024]{1,0:T(8,128)}) custom-call(s32[1024,128]{1,0:T(8,128)} %get-tuple-element.55.tcol_ref, bf16[512,1024]{1,0:T(8,128)(2,1)} %get-tuple-element.70.z0, ...), custom_call_target="tpu_custom_call" | custom-call | flops 3221225472 | bytes 60000000 | tf_op jit(solution)/shard_map/results/pallas_call | solution.py:1017
  439.2 0.0 copy-done
  439.2 0.6 copy.30
  439.8 0.0 copy-done.1
  439.8 0.6 copy.31
  (1 shorter events, 0.0 us)
Async XLA Ops:
  0.6 87.6 %collective-permute-start = (bf16[2048,1024]{1,0:T(8,128)(2,1)}, bf16[2048,1024]{1,0:T(8,128)(2,1)}, u32[]{:S(2)}, u32[]{:S(2)}) collective-permute-start(bf16[2048,1024]{1,0:T(8,128)(2,1)} %bitcast.21), channel_id=1, source_target_pairs={{0,16},{16,0},{1,17},{17,1},{2,18},{18,2},{3,19},{19,3},{4,20},{20... | collective-permute-start | bytes 12582920 | tf_op jit(solution)/shard_map/ppermute | solution.py:1049
  1.2 87.1 %collective-permute-start.1 = (bf16[2048,1024]{1,0:T(8,128)(2,1)}, bf16[2048,1024]{1,0:T(8,128)(2,1)}, u32[]{:S(2)}, u32[]{:S(2)}) collective-permute-start(bf16[2048,1024]{1,0:T(8,128)(2,1)} %bitcast.23), channel_id=1, source_target_pairs={{0,16},{16,0},{1,17},{17,1},{2,18},{18,2},{3,19},{19,3},{4,20},{20... | collective-permute-start | bytes 12582920 | tf_op jit(solution)/shard_map/ppermute | solution.py:1049
  1.2 87.0 %collective-permute-start.2 = (bf16[1,2048]{1,0:T(2,128)(2,1)}, bf16[1,2048]{1,0:T(2,128)(2,1)S(1)}, u32[]{:S(2)}, u32[]{:S(2)}) collective-permute-start(bf16[1,2048]{1,0:T(2,128)(2,1)} %bo_ref.1), channel_id=1, source_target_pairs={{0,16},{16,0},{1,17},{17,1},{2,18},{18,2},{3,19},{19,3},{4,20},{20... | collective-permute-start | bytes 12296 | tf_op jit(solution)/shard_map/ppermute | solution.py:1049
  88.3 0.6 copy-start.2
  418.4 20.9 %copy-start = (f32[1,2048]{1,0:T(1,128)S(1)}, f32[1,2048]{1,0:T(1,128)}, u32[]{:S(2)}) copy-start(f32[1,2048]{1,0:T(1,128)} %get-tuple-element.125) | copy-start | bytes 24580
  418.4 21.5 %copy-start.1 = (f32[1,1024]{1,0:T(1,128)S(1)}, f32[1,1024]{1,0:T(1,128)}, u32[]{:S(2)}) copy-start(f32[1,1024]{1,0:T(1,128)} %get-tuple-element.127) | copy-start | bytes 12292

commit v4 on v3

--- a/solution.py
+++ b/solution.py
@@ -122,11 +122,12 @@
     return (lanes < HEAD_DIM) if first else (lanes >= HEAD_DIM)
 
 
-PRE_GAIN, PRE_SHIFT, PROJ_BIAS, MID_GAIN, MID_SHIFT = range(5)
+def row_of(ref):
+    return ref[...].astype(F32).reshape(1, ref.shape[0])
 
 
 def front_kernel(
-    n, cc, pairs, ids_ref, cot_ref, x_ref, seg_ref, vec_ref, w_ref, w_any, p_ref, p_any,
+    n, cc, pairs, ids_ref, cot_ref, x_ref, seg_ref, pre_gain, pre_shift, proj_bias, mid_gain, mid_shift, w_ref, w_any, p_ref, p_any,
     tcol_ref, norm_t, hr_ref, att_ref, att_t, prob_ref, mid_ref, slot_ref, arr_ref, wo_out, po_out,
     row_s, cs_s, norm_s, hr_s, wo_s, po_s, bias_s, low_s, send, recv, local, dsend, drecv, dlocal,
 ):
@@ -185,11 +186,11 @@
             cs_s[block_of(b, 256), :] = dot(hot, cot_ref[...]).astype(BF)
             return 0
 
-        lax.fori_loop(0, CHUNKS * rows // 256, fill, 0)
-        for r in routes:
+        for c, r in enumerate(routes):
+            lax.fori_loop(c * rows // 256, (c + 1) * rows // 256, fill, 0)
             r.start()
 
-        gain, shift = vec_ref[PRE_GAIN:PRE_GAIN + 1, :], vec_ref[PRE_SHIFT:PRE_SHIFT + 1, :]
+        gain, shift = row_of(pre_gain), row_of(pre_shift)
 
         def body(b, _):
             at = block_of(b, 128)
@@ -257,8 +258,7 @@
 
     @pl.when(step == first_pair + pairs)
     def _():
-        pbias = vec_ref[PROJ_BIAS:PROJ_BIAS + 1, :]
-        gain, shift = vec_ref[MID_GAIN:MID_GAIN + 1, :], vec_ref[MID_SHIFT:MID_SHIFT + 1, :]
+        pbias, gain, shift = row_of(proj_bias), row_of(mid_gain), row_of(mid_shift)
 
         def body(b, _):
             at = block_of(b, 128)
@@ -285,7 +285,7 @@
             r.wait()
 
 
-def front_call(n, cc, ids, cot, x, seg, vec, qkv, proj):
+def front_call(n, cc, ids, cot, x, seg, vectors, qkv, proj):
     tokens, width = x.shape
     half = proj.shape[0]
     pairs = width // 128
@@ -301,7 +301,7 @@
         grid=(8 + pairs,),
         in_specs=[
             whole((1, tokens)), whole((tokens, width)), whole((tokens, width)), whole((1, tokens)),
-            whole(vec.shape),
+            *[whole((width,))] * 5,
             pl.BlockSpec((1, width, half), lambda i: (jnp.clip(i - 1, 0, 2), 0, 0)), ANY,
             whole((half, width)), ANY,
         ],
@@ -325,7 +325,7 @@
         compiler_params=params(collective_id=1, has_side_effects=True),
         cost_estimate=cost(3e10, 6e7),
         name="front",
-    )(ids, cot, x, seg, vec, qkv, qkv, proj, proj)
+    )(ids, cot, x, seg, *vectors, qkv, qkv, proj, proj)
 
 
 GELU_C = 0.7978845608028654
@@ -616,7 +616,7 @@
 
 
 def middle_back_kernel(
-    n, cc, blocks, tcol_ref, g0, g1, g2, mid_ref, cot_ref, vec_ref, own_ref, oth_ref, att_t, y_src,
+    n, cc, blocks, tcol_ref, g0, g1, g2, mid_ref, cot_ref, gain_ref, own_ref, oth_ref, att_t, y_src,
     gmid_ref, gatt_ref, pg_own, pg_oth, small_ref, y_dst, gb_s, send, recv, local,
 ):
     route = Route(
@@ -636,7 +636,7 @@
     grad = gather_rows(tcol_ref[...], (g0[...], g1[...], g2[...]))
     grad = grad.astype(BF).astype(F32)
     unit, inverse = unit_of(mid_ref[...])
-    gmid = cot_ref[...].astype(F32) + norm_back(grad, unit, inverse, vec_ref[MID_GAIN:MID_GAIN + 1, :])
+    gmid = cot_ref[...].astype(F32) + norm_back(grad, unit, inverse, row_of(gain_ref))
     gmid_ref[...] = gmid
     gb = gmid.astype(BF)
     gb_s[block_of(step, tb), :] = gb
@@ -653,7 +653,7 @@
         route.wait()
 
 
-def middle_back_call(n, cc, tcol, grads, middle, cot, vec, proj_own, proj_oth, att_t, y):
+def middle_back_call(n, cc, tcol, grads, middle, cot, gain, proj_own, proj_oth, att_t, y):
     tokens, width = middle.shape
     half = proj_own.shape[0]
     tb = 256
@@ -665,7 +665,7 @@
         grid=(tokens // tb,),
         in_specs=[
             pl.BlockSpec((tb, 128), lambda i: (i, 0)), *[whole((rows, width))] * 3, block, block,
-            whole(vec.shape), whole((half, width)), whole((half, width)), whole((tokens, width)), ANY,
+            whole((width,)), whole((half, width)), whole((half, width)), whole((tokens, width)), ANY,
         ],
         out_specs=[block, block, whole((half, width)), whole((half, width)), whole((8, width)), ANY],
         out_shape=[
@@ -676,7 +676,7 @@
         compiler_params=params(collective_id=4, has_side_effects=True),
         cost_estimate=cost(1.2e10, 3e7),
         name="middle_back",
-    )(tcol, *grads, middle, cot, vec, proj_own, proj_oth, att_t, y)
+    )(tcol, *grads, middle, cot, gain, proj_own, proj_oth, att_t, y)
 
 
 class Part:
@@ -744,7 +744,7 @@
 
 def back_kernel(
     n, cc, groups, q_ref, k_ref, v_ref, prob_ref, do_ref, o_ref, x_ref, norm_t, own_ref, oth_ref,
-    vec_ref, small_ref, pg_own, pg_oth, gmid_any, y_src,
+    gain_ref, small_ref, pg_own, pg_oth, gmid_any, y_src,
     xg_ref, small_out, sum_q, sum_p, z1, z2,
     dk_s, dv_s, gh_s, gnp_s, acc, rcv, res, p_acc, p_rcv, p_res, got, pgot, snd, mine_s, small_got,
     send, recv, local, dsend, drecv, rs_send, rs_recv, ag_send, ag_recv, sm_send, sm_recv, out_sem,
@@ -896,7 +896,7 @@
             at = block_of(b, 128)
             grad = gnp_s[at, :]
             unit, inverse = unit_of(x_ref[at, :].astype(F32))
-            xg_ref[at, :] = xg_ref[at, :] + norm_back(grad, unit, inverse, vec_ref[PRE_GAIN:PRE_GAIN + 1, :])
+            xg_ref[at, :] = xg_ref[at, :] + norm_back(grad, unit, inverse, row_of(gain_ref))
             small_out[0:1, :] += jnp.sum(grad * unit, axis=0, keepdims=True)
             small_out[1:2, :] += jnp.sum(grad, axis=0, keepdims=True)
             return 0
@@ -924,7 +924,7 @@
             r.wait()
 
 
-def back_call(n, cc, head_rows, probs, gatt, att, x, norm_t, own, oth, gmid, vec, small, pg_own, pg_oth, y):
+def back_call(n, cc, head_rows, probs, gatt, att, x, norm_t, own, oth, gmid, gain, small, pg_own, pg_oth, y):
     tokens, width = x.shape
     half = own.shape[2]
     groups = half // 128
@@ -961,7 +961,7 @@
         in_specs=[
             head(0), head(1), head(2), pl.BlockSpec((2, QB, BAND), lambda i: (pair(i), 0, 0)), cols, cols,
             fixed((tokens, width)), fixed((width, tokens)), fixed(own.shape), fixed(oth.shape),
-            fixed(vec.shape), fixed(small.shape), fixed((half, width)), ANY, ANY, ANY,
+            fixed((width,)), fixed(small.shape), fixed((half, width)), ANY, ANY, ANY,
         ],
         out_specs=[fixed((tokens, width)), fixed(small.shape), ANY, ANY, ANY, ANY],
         out_shape=[
@@ -981,11 +981,11 @@
         cost_estimate=cost(5.3e10, 9e7),
         name="back",
     )(
-        head_rows, head_rows, head_rows, probs, gatt, att, x, norm_t, own, oth, vec, small, pg_own, pg_oth, gmid, y
+        head_rows, head_rows, head_rows, probs, gatt, att, x, norm_t, own, oth, gain, small, pg_own, pg_oth, gmid, y
     )
 
 
-def result_kernel(tcol_ref, z0, z1, z2, mid_ref, sum_q, sum_p, xg_ref, wd_ref, wu_ref, out_ref, q_ref, p_ref, xo_ref, do_ref, uo_ref):
+def result_kernel(tcol_ref, z0, z1, z2, mid_ref, sum_q, sum_p, xg_ref, wd_ref, wu_ref, small_ref, out_ref, q_ref, p_ref, xo_ref, do_ref, uo_ref, *smalls):
     rows = gather_rows(tcol_ref[...], (z0[...], z1[...], z2[...]))
     out_ref[...] = (mid_ref[...] + rows.astype(BF).astype(F32)).astype(BF)
     for c in range(3):
@@ -997,9 +997,11 @@
     xo_ref[...] = xg_ref[...]
     do_ref[...] = wd_ref[...].astype(F32)
     uo_ref[...] = wu_ref[...].astype(F32)
-
-
-def result_call(tcol, zs, middle, sum_q, sum_p, xg, wd, wu):
+    for k, small in enumerate(smalls):
+        small[...] = small_ref[k:k + 1, :].reshape(small.shape)
+
+
+def result_call(tcol, zs, middle, sum_q, sum_p, xg, wd, wu, small):
     tokens, width = middle.shape
     half = sum_p.shape[1]
     groups = half // 128
@@ -1021,20 +1023,20 @@
             rows_of(tb, 128), *[whole((rows, width))] * 3, rows_of(tb, width),
             pl.BlockSpec((groups, qb, 384), lambda i: (0, i, 0)),
             pl.BlockSpec((width // half, pb, half), lambda i: (0, i, 0)), rows_of(tb, width), rows_of(wb, width),
-            rows_of(wb, width),
+            rows_of(wb, width), whole(small.shape),
         ],
         out_specs=[
             rows_of(tb, width), pl.BlockSpec((3, qb, half), lambda i: (0, i, 0)), rows_of(pb, width),
-            rows_of(tb, width), rows_of(wb, width), rows_of(wb, width),
+            rows_of(tb, width), rows_of(wb, width), rows_of(wb, width), *[whole((width,))] * 5,
         ],
         out_shape=[
             sds((tokens, width), BF), sds((3, width, half), F32), sds((half, width), F32), sds((tokens, width), F32),
-            sds((hid, width), F32), sds((hid, width), F32),
+            sds((hid, width), F32), sds((hid, width), F32), *[sds((width,), F32)] * 5,
         ],
         compiler_params=params(),
         cost_estimate=cost(6 * tokens * rows * width, 6e7),
         name="results",
-    )(tcol, *zs, middle, sum_q, sum_p, xg, wd, wu)
+    )(tcol, *zs, middle, sum_q, sum_p, xg, wd, wu, small)
 
 
 def on_device(
@@ -1051,21 +1053,21 @@
     down_own, up_own = down_weight[0], up_weight[0]
     up, down = (up_own, swap(up_own)), (down_own, swap(down_own))
     bias = (up_bias, swap(up_bias))
-    vec = jnp.stack([pre_gain, pre_shift, proj_bias, mid_gain, mid_shift]).astype(F32)
+    vectors = (pre_gain, pre_shift, proj_bias, mid_gain, mid_shift)
 
     tcol, norm_t, head_rows, att, att_t, probs, middle, mid_slots, cot_rows, qkv_oth, proj_oth = front_call(
-        n, cc, expert_ids.reshape(1, count), cotangent, tokens, segment_ids, vec, qkv_weight, proj_weight)
+        n, cc, expert_ids.reshape(1, count), cotangent, tokens, segment_ids, vectors, qkv_weight, proj_weight)
     acts, ghs, ub, y, dx, arrived, gm0 = expert_call(n, cc, mid_slots, cot_rows, up, down, bias, down_bias)
     down_grad, up_grad, upbias_grad, downbias_grad, gm1, gm2 = wgrad_call(n, cc, acts, ghs, cot_rows, arrived, ub, dx)
 
     gmid, gatt, pg_own, pg_oth, small, z0 = middle_back_call(
-        n, cc, tcol, (gm0, gm1, gm2), middle, cotangent, vec, proj_weight, proj_oth, att_t, y)
+        n, cc, tcol, (gm0, gm1, gm2), middle, cotangent, mid_gain, proj_weight, proj_oth, att_t, y)
     input_grad, small, sum_q, sum_p, z1, z2 = back_call(
-        n, cc, head_rows, probs, gatt, att, tokens, norm_t, qkv_weight, qkv_oth, gmid, vec, small, pg_own, pg_oth, y)
-    output, qkv_grad, proj_grad, input_grad, down_grad, up_grad = result_call(
-        tcol, (z0, z1, z2), middle, sum_q, sum_p, input_grad, down_grad, up_grad)
+        n, cc, head_rows, probs, gatt, att, tokens, norm_t, qkv_weight, qkv_oth, gmid, pre_gain, small, pg_own, pg_oth, y)
+    output, qkv_grad, proj_grad, input_grad, down_grad, up_grad, pregain, preshift, midgain, midshift, projbias = result_call(
+        tcol, (z0, z1, z2), middle, sum_q, sum_p, input_grad, down_grad, up_grad, small)
     return (
-        output, input_grad, qkv_grad, proj_grad, small[4], small[0], small[1], small[2], small[3],
+        output, input_grad, qkv_grad, proj_grad, projbias, pregain, preshift, midgain, midshift,
         up_grad[None], upbias_grad, down_grad[None], downbias_grad,
     )
 

time: 447 us -> 440 us (0.984)
  local copies, waits for them, and re-layouts: 6.87 us -> 1.77 us
  transfers between devices with their start and end apart: 3 -> 3, of which waited for: 0 -> 0; matrix products, arithmetic and copies ran while one was open for 1% -> 0% of each run, Pallas kernels for 19% -> 18%
where the time goes in v4:
time: 440 us; the launch traced here: 433 us
  Pallas kernels  429 us (98%)
    pallas_call x1, Pallas kernels, back_call(): pl.pallas_call(functools.partial(back_kernel, n, cc, groups), grid=(last...  124 us
    pallas_call x1, Pallas kernels, expert_call(): pl.pallas_call(functools.partial(expert_kernel, n, cc, own_tiles), grid=(...  109 us
    pallas_call x1, Pallas kernels, front_call(): pl.pallas_call(functools.partial(front_kernel, n, cc, pairs), grid=(8 + p...  79.7 us
    pallas_call x1, Pallas kernels, wgrad_call(): pl.pallas_call(functools.partial(wgrad_kernel, n, cc, tiles), grid=(4 * t...  61 us
    pallas_call x1, Pallas kernels, middle_back_call(): pl.pallas_call(functools.partial(middle_back_kernel, n, cc, tokens // tb)...  34.4 us
    pallas_call x1, Pallas kernels, result_call(): pl.pallas_call(result_kernel, grid=(steps,), in_specs=[rows_of(tb, 128),...  20.9 us
  transfers between devices with their start and end apart: 3, of which 0 were waited for; matrix products, arithmetic and copies ran while one was open for 0% of the time, Pallas kernels for 18%

profile of v4, /device:TPU:0, one launch (start us, length us, event | category | flops | bytes accessed | tf_op | source)
XLA Modules:
  0.0 432.8 jit_solution(16960787815637912470)
XLA Ops:
  0.6 0.5 collective-permute-start
  1.2 0.1 collective-permute-start.1
  1.2 0.4 collective-permute-start.2
  1.7 79.7 %front.1 = (s32[1024,128]{1,0:T(8,128)}, bf16[1024,1024]{1,0:T(8,128)(2,1)}, bf16[6,1024,512]{2,1,0:T(8,128)(2,1)}, bf16[1024,1024]{1,0:T(8,128)(2,1)}, bf16[102...) custom-call(s32[1,1024]{1,0:T(1,128)} %bitcast.15, ...), custom_call_target="tpu_custom_call" | custom-call | flops 30000001024 | bytes 60000000 | tf_op jit(solution)/shard_map/front/pallas_call | solution.py:299
  81.4 0.0 collective-permute-done.2.bt_ref
  81.4 0.0 copy-start.2
  81.4 0.0 collective-permute-done.ut_ref
  81.4 0.0 collective-permute-done.1.dt_ref
  81.4 0.6 copy-done.2
  82.0 109.1 %experts.1 = (bf16[3,512,4096]{2,1,0:T(8,128)(2,1)}, bf16[3,512,4096]{2,1,0:T(8,128)(2,1)}, f32[8,4096]{1,0:T(8,128)}, bf16[3,512,1024]{2,1,0:T(8,128)(2,1)}, bf...) custom-call(bf16[1536,1024]{1,0:T(8,128)(2,1)} %get-tuple-element.61.mid_ref, ...), custom_call_target="tpu_custom_call" | custom-call | flops 51999997952 | bytes 80000000 | tf_op jit(solution)/shard_map/experts/pallas_call | solution.py:460
  191.1 61.0 %weight_grads.1 = (bf16[2048,1024]{1,0:T(8,128)(2,1)}, bf16[2048,1024]{1,0:T(8,128)(2,1)}, f32[1,2048]{1,0:T(1,128)}, f32[1,1024]{1,0:T(1,128)}, bf16[512,1024]{1,0:T(8,128)(2,1)}, /*index=5*/bf16[512,1024]{1,0:T(8,128)(2,1)}) custom-call(bf16[3,512,4096]{2,1,0:T(8,128)(2,1)} %get-tuple-element.64.a_ref, bf16[3,512,4096]{2,1,0:T(8,128)(2,1)} %get-tuple-element.65.g_ref, ...), custom_call_target="tpu_custom_call" | custom-call | flops 25999998976 | bytes 80000000 | tf_op jit(solution)/shard_map/weight_grads/pallas_call | solution.py:579
  252.1 34.4 %middle_back.1 = (f32[1024,1024]{1,0:T(8,128)}, bf16[1024,1024]{1,0:T(8,128)(2,1)}, bf16[512,1024]{1,0:T(8,128)(2,1)}, bf16[512,1024]{1,0:T(8,128)(2,1)}, f32[8,1024]{1,0:T(8,128)}, /*index=5*/bf16[512,1024]{1,0:T(8,128)(2,1)}) custom-call(s32[1024,128]{1,0:T(8,128)} %get-tuple-element.60.tcol_ref, bf16[512,1024]{1,0:T(8,128)(2,1)} %get-tuple-element.63.g0, ...), custom_call_target="tpu_custom_call" | custom-call | flops 12000000000 | bytes 30000000 | tf_op jit(solution)/shard_map/middle_back/pallas_call | solution.py:663
  286.5 123.9 %back.1 = (f32[1024,1024]{1,0:T(8,128)}, f32[8,1024]{1,0:T(8,128)}, bf16[4096,384]{1,0:T(8,128)(2,1)}, bf16[1024,512]{1,0:T(8,128)(2,1)}, bf16[512,1024]{1,0:T(8,128)(2,1)}, /*index=5*/bf16[512,1024]{1,0:T(8,128)(2,1)}) custom-call(bf16[6,1024,512]{2,1,0:T(8,128)(2,1)} %get-tuple-element.76.q_ref.k_ref.v_ref, ...), custom_call_target="tpu_custom_call" | custom-call | flops 52999999488 | bytes 90000000 | tf_op jit(solution)/shard_map/back/pallas_call | solution.py:958
  410.4 0.0 copy-start
  410.4 0.0 copy-start.1
  410.4 20.9 %results.1 = (bf16[1024,1024]{1,0:T(8,128)(2,1)}, f32[3,1024,512]{2,1,0:T(8,128)}, f32[512,1024]{1,0:T(8,128)}, f32[1024,1024]{1,0:T(8,128)}, f32[2048,1024]{1,0...) custom-call(s32[1024,128]{1,0:T(8,128)} %get-tuple-element.60.tcol_r, ...), custom_call_target="tpu_custom_call" | custom-call | flops 3221225472 | bytes 60000000 | tf_op jit(solution)/shard_map/results/pallas_call | solution.py:1019
  431.4 0.0 copy-done
  431.4 0.6 copy.30
  432.0 0.0 copy-done.1
  432.0 0.6 copy.31
Async XLA Ops:
  0.6 80.8 %collective-permute-start = (bf16[2048,1024]{1,0:T(8,128)(2,1)}, bf16[2048,1024]{1,0:T(8,128)(2,1)}, u32[]{:S(2)}, u32[]{:S(2)}) collective-permute-start(bf16[2048,1024]{1,0:T(8,128)(2,1)} %bitcast.11), channel_id=1, source_target_pairs={{0,16},{16,0},{1,17},{17,1},{2,18},{18,2},{3,19},{19,3},{4,20},{20... | collective-permute-start | bytes 12582920 | tf_op jit(solution)/shard_map/ppermute | solution.py:1051
  1.2 80.3 %collective-permute-start.1 = (bf16[2048,1024]{1,0:T(8,128)(2,1)}, bf16[2048,1024]{1,0:T(8,128)(2,1)}, u32[]{:S(2)}, u32[]{:S(2)}) collective-permute-start(bf16[2048,1024]{1,0:T(8,128)(2,1)} %bitcast.13), channel_id=1, source_target_pairs={{0,16},{16,0},{1,17},{17,1},{2,18},{18,2},{3,19},{19,3},{4,20},{20... | collective-permute-start | bytes 12582920 | tf_op jit(solution)/shard_map/ppermute | solution.py:1051
  1.2 80.2 %collective-permute-start.2 = (bf16[1,2048]{1,0:T(2,128)(2,1)}, bf16[1,2048]{1,0:T(2,128)(2,1)S(1)}, u32[]{:S(2)}, u32[]{:S(2)}) collective-permute-start(bf16[1,2048]{1,0:T(2,128)(2,1)} %bo_ref.1), channel_id=1, source_target_pairs={{0,16},{16,0},{1,17},{17,1},{2,18},{18,2},{3,19},{19,3},{4,20},{20... | collective-permute-start | bytes 12296 | tf_op jit(solution)/shard_map/ppermute | solution.py:1051
  81.4 0.6 copy-start.2
  410.4 21.0 %copy-start = (f32[1,2048]{1,0:T(1,128)S(1)}, f32[1,2048]{1,0:T(1,128)}, u32[]{:S(2)}) copy-start(f32[1,2048]{1,0:T(1,128)} %get-tuple-element.130) | copy-start | bytes 24580
  410.4 21.6 %copy-start.1 = (f32[1,1024]{1,0:T(1,128)S(1)}, f32[1,1024]{1,0:T(1,128)}, u32[]{:S(2)}) copy-start(f32[1,1024]{1,0:T(1,128)} %get-tuple-element.132) | copy-start | bytes 12292

commit v5 on v4

--- a/solution.py
+++ b/solution.py
@@ -122,14 +122,18 @@
     return (lanes < HEAD_DIM) if first else (lanes >= HEAD_DIM)
 
 
+def two_heads(rows):
+    return jnp.concatenate([jnp.where(lane_pick(128, j == 0), rows, BF(0)) for j in range(2)], axis=0)
+
+
 def row_of(ref):
     return ref[...].astype(F32).reshape(1, ref.shape[0])
 
 
 def front_kernel(
-    n, cc, pairs, ids_ref, cot_ref, x_ref, seg_ref, pre_gain, pre_shift, proj_bias, mid_gain, mid_shift, w_ref, w_any, p_ref, p_any,
+    n, cc, pairs, ids_ref, cot_ref, x_any, seg_ref, pre_gain, pre_shift, proj_bias, mid_gain, mid_shift, w_ref, w_any, p_any,
     tcol_ref, norm_t, hr_ref, att_ref, att_t, prob_ref, mid_ref, slot_ref, arr_ref, wo_out, po_out,
-    row_s, cs_s, norm_s, hr_s, wo_s, po_s, bias_s, low_s, send, recv, local, dsend, drecv, dlocal,
+    x_ref, p_ref, row_s, cs_s, norm_s, hr_s, wo_s, po_s, bias_s, low_s, send, recv, local, dsend, drecv, dlocal,
 ):
     step = pl.program_id(0)
     tokens, width = x_ref.shape
@@ -156,8 +160,16 @@
             pltpu.make_async_copy(po_s, po_out, dlocal.at[1]),
         ]
 
+    def loads():
+        return [
+            pltpu.make_async_copy(x_any, x_ref, dlocal.at[2]),
+            pltpu.make_async_copy(p_any, p_ref, dlocal.at[3]),
+        ]
+
     @pl.when(step == 0)
     def _():
+        for c in loads():
+            c.start()
         greet(n, True)
         for c in swaps():
             c.start()
@@ -190,6 +202,8 @@
             lax.fori_loop(c * rows // 256, (c + 1) * rows // 256, fill, 0)
             r.start()
 
+        for c in loads():
+            c.wait()
         gain, shift = row_of(pre_gain), row_of(pre_shift)
 
         def body(b, _):
@@ -242,16 +256,17 @@
             w, s = WIDTH[i], START[i]
             keys, values = hr_s[3 * side + 1, s:s + w, lanes], hr_s[3 * side + 2, s:s + w, lanes]
             bias = bias_s[:, OFFSET[i]:OFFSET[i] + w]
+            scores = dot_nt(two_heads(query[i * QB:(i + 1) * QB]), keys)
             parts = []
             for j in range(2):
-                q = jnp.where(lane_pick(128, j == 0), query[i * QB:(i + 1) * QB], BF(0))
-                scores = dot_nt(q, keys) + bias
-                top = jnp.max(scores, axis=-1, keepdims=True)
-                weights = jnp.exp(scores - top)
+                masked = scores[j * QB:(j + 1) * QB] + bias
+                top = jnp.max(masked, axis=-1, keepdims=True)
+                weights = jnp.exp(masked - top)
                 probs = (weights * (1.0 / jnp.sum(weights, axis=-1, keepdims=True))).astype(BF)
                 prob_ref[j, :, OFFSET[i]:OFFSET[i] + w] = probs
-                parts.append(dot(probs, values))
-            both = jnp.where(lane_pick(128, True), parts[0], parts[1])
+                parts.append(probs)
+            out = dot(jnp.concatenate(parts, axis=0), values)
+            both = jnp.where(lane_pick(128, True), out[0:QB], out[QB:2 * QB])
             both = both.astype(BF)
             att_ref[i * QB:(i + 1) * QB, block_of(pair, 128)] = both
             att_t[block_of(pair, 128), i * QB:(i + 1) * QB] = jnp.transpose(both)
@@ -300,10 +315,10 @@
         functools.partial(front_kernel, n, cc, pairs),
         grid=(8 + pairs,),
         in_specs=[
-            whole((1, tokens)), whole((tokens, width)), whole((tokens, width)), whole((1, tokens)),
+            whole((1, tokens)), whole((tokens, width)), ANY, whole((1, tokens)),
             *[whole((width,))] * 5,
             pl.BlockSpec((1, width, half), lambda i: (jnp.clip(i - 1, 0, 2), 0, 0)), ANY,
-            whole((half, width)), ANY,
+            ANY,
         ],
         out_specs=[
             whole((tokens, 128)), whole((width, tokens)),
@@ -317,15 +332,16 @@
             sds((CHUNKS * rows, width), BF), sds((CHUNKS, rows, width), BF), sds(qkv.shape, BF), sds(proj.shape, BF),
         ],
         scratch_shapes=[
+            pltpu.VMEM((tokens, width), BF), pltpu.VMEM((half, width), BF),
             pltpu.VMEM((8, tokens), jnp.int32), pltpu.VMEM((CHUNKS * rows, width), BF),
             pltpu.VMEM((tokens, width), BF), pltpu.VMEM((6, tokens, half), BF), pltpu.VMEM(qkv.shape, BF),
             pltpu.VMEM(proj.shape, BF), pltpu.VMEM((QB, BAND), F32), pltpu.VMEM((tokens, width), BF),
-            *route_sems(n, CHUNKS), dma((2,)), dma((2,)), dma((2,)),
+            *route_sems(n, CHUNKS), dma((2,)), dma((2,)), dma((4,)),
         ],
         compiler_params=params(collective_id=1, has_side_effects=True),
         cost_estimate=cost(3e10, 6e7),
         name="front",
-    )(ids, cot, x, seg, *vectors, qkv, qkv, proj, proj)
+    )(ids, cot, x, seg, *vectors, qkv, qkv, proj)
 
 
 GELU_C = 0.7978845608028654
@@ -488,9 +504,9 @@
 
 
 def wgrad_kernel(
-    n, cc, tiles, a_ref, g_ref, c_ref, x_ref, ub_ref, dx_ref,
+    n, cc, tiles, a_ref, g_ref, c_any, x_any, ub_ref, dx_ref,
     do_ref, up_ref, ubg_ref, cbg_ref, back1, back2,
-    out_s, in_s, small_s, got_s, send, recv, local, dsend, drecv, ssend, srecv,
+    c_ref, x_ref, out_s, in_s, small_s, got_s, send, recv, local, dsend, drecv, ssend, srecv, lsem,
 ):
     step = pl.program_id(0)
     hid = ubg_ref.shape[1]
@@ -507,11 +523,20 @@
 
     small = to_partner(small_s, got_s, ssend, srecv)
 
+    def loads():
+        return [
+            pltpu.make_async_copy(c_any, c_ref, lsem.at[0]),
+            pltpu.make_async_copy(x_any, x_ref, lsem.at[1]),
+        ]
+
     @pl.when(step == 0)
     def _():
+        for c in loads():
+            c.start()
         greet(n, True)
         for r in routes:
             r.start()
+        loads()[0].wait()
         total = jnp.zeros((1, c_ref.shape[2]), F32)
         for c in range(CHUNKS):
             total = total + jnp.sum(c_ref[c].astype(F32), axis=0, keepdims=True)
@@ -536,6 +561,8 @@
         @pl.when(step == k)
         def _():
             left, right = (a_ref, c_ref) if k < tiles else (g_ref, x_ref)
+            if k == tiles:
+                loads()[1].wait()
             out_s[k] = product(left, right).astype(BF)
             swap(k).start()
 
@@ -579,16 +606,16 @@
     return pl.pallas_call(
         functools.partial(wgrad_kernel, n, cc, tiles),
         grid=(4 * tiles,),
-        in_specs=[a_spec, g_spec, whole(cot.shape), whole(rows_in.shape), whole(ub.shape), ANY],
+        in_specs=[a_spec, g_spec, ANY, ANY, whole(ub.shape), ANY],
         out_specs=[d_spec, u_spec, whole((1, hid)), whole((1, width)), ANY, ANY],
         out_shape=[
             sds((hid, width), BF), sds((hid, width), BF), sds((1, hid), F32), sds((1, width), F32),
             sds((rows, width), BF), sds((rows, width), BF),
         ],
         scratch_shapes=[
-            pltpu.VMEM((2 * tiles, TILE, width), BF), pltpu.VMEM((2 * tiles, TILE, width), BF),
+            pltpu.VMEM(cot.shape, BF), pltpu.VMEM(rows_in.shape, BF), pltpu.VMEM((2 * tiles, TILE, width), BF), pltpu.VMEM((2 * tiles, TILE, width), BF),
             pltpu.VMEM((8, hid + width), F32), pltpu.VMEM((8, hid + width), F32),
-            *route_sems(n, 2), dma((2 * tiles,)), dma((2 * tiles,)), dma, dma,
+            *route_sems(n, 2), dma((2 * tiles,)), dma((2 * tiles,)), dma, dma, dma((2,)),
         ],
         compiler_params=params(collective_id=3, has_side_effects=True),
         cost_estimate=cost(2.6e10, 8e7),
@@ -616,8 +643,9 @@
 
 
 def middle_back_kernel(
-    n, cc, blocks, tcol_ref, g0, g1, g2, mid_ref, cot_ref, gain_ref, own_ref, oth_ref, att_t, y_src,
-    gmid_ref, gatt_ref, pg_own, pg_oth, small_ref, y_dst, gb_s, send, recv, local,
+    n, cc, blocks, tcol_ref, g0_any, g1_any, g2_any, mid_ref, cot_ref, gain_ref, own_any, oth_any, att_any, y_src,
+    gmid_ref, gatt_ref, pg_own, pg_oth, small_ref, y_dst,
+    gb_s, g0, g1, g2, own_ref, oth_ref, att_t, send, recv, local, lsem,
 ):
     route = Route(
         n, lambda e: y_src.at[0, block_of(e, cc)], lambda d: y_dst.at[block_of(d, cc)],
@@ -627,11 +655,19 @@
     half = own_ref.shape[0]
     tb = mid_ref.shape[0]
 
+    def load(k):
+        src = (g0_any, g1_any, g2_any, own_any, oth_any, att_any)[k]
+        return pltpu.make_async_copy(src, (g0, g1, g2, own_ref, oth_ref, att_t)[k], lsem.at[k])
+
     @pl.when(step == 0)
     def _():
+        for k in range(6):
+            load(k).start()
         greet(n, False)
         route.start()
         small_ref[...] = jnp.zeros_like(small_ref)
+        for k in range(5):
+            load(k).wait()
 
     grad = gather_rows(tcol_ref[...], (g0[...], g1[...], g2[...]))
     grad = grad.astype(BF).astype(F32)
@@ -648,6 +684,7 @@
 
     @pl.when(step == blocks - 1)
     def _():
+        load(5).wait()
         pg_own[...] = dot(att_t[0:half, :], gb_s[...]).astype(BF)
         pg_oth[...] = dot(att_t[half:2 * half, :], gb_s[...]).astype(BF)
         route.wait()
@@ -664,15 +701,19 @@
         functools.partial(middle_back_kernel, n, cc, tokens // tb),
         grid=(tokens // tb,),
         in_specs=[
-            pl.BlockSpec((tb, 128), lambda i: (i, 0)), *[whole((rows, width))] * 3, block, block,
-            whole((width,)), whole((half, width)), whole((half, width)), whole((tokens, width)), ANY,
+            pl.BlockSpec((tb, 128), lambda i: (i, 0)), ANY, ANY, ANY, block, block,
+            whole((width,)), ANY, ANY, ANY, ANY,
         ],
         out_specs=[block, block, whole((half, width)), whole((half, width)), whole((8, width)), ANY],
         out_shape=[
             sds((tokens, width), F32), sds((tokens, width), BF), sds((half, width), BF), sds((half, width), BF),
             sds((8, width), F32), sds((rows, width), BF),
         ],
-        scratch_shapes=[pltpu.VMEM((tokens, width), BF), *route_sems(n, 1)],
+        scratch_shapes=[
+            pltpu.VMEM((tokens, width), BF), *[pltpu.VMEM((rows, width), BF)] * CHUNKS, pltpu.VMEM((half, width), BF),
+            pltpu.VMEM((half, width), BF), pltpu.VMEM((width, tokens), BF), *route_sems(n, 1),
+            pltpu.SemaphoreType.DMA((6,)),
+        ],
         compiler_params=params(collective_id=4, has_side_effects=True),
         cost_estimate=cost(1.2e10, 3e7),
         name="middle_back",
@@ -743,10 +784,10 @@
 
 
 def back_kernel(
-    n, cc, groups, q_ref, k_ref, v_ref, prob_ref, do_ref, o_ref, x_ref, norm_t, own_ref, oth_ref,
+    n, cc, groups, q_ref, k_ref, v_ref, prob_ref, do_ref, o_ref, x_any, norm_any, own_any, oth_any,
     gain_ref, small_ref, pg_own, pg_oth, gmid_any, y_src,
     xg_ref, small_out, sum_q, sum_p, z1, z2,
-    dk_s, dv_s, gh_s, gnp_s, acc, rcv, res, p_acc, p_rcv, p_res, got, pgot, snd, mine_s, small_got,
+    x_ref, norm_t, own_ref, oth_ref, dk_s, dv_s, gh_s, gnp_s, acc, rcv, res, p_acc, p_rcv, p_res, got, pgot, snd, mine_s, small_got,
     send, recv, local, dsend, drecv, rs_send, rs_recv, ag_send, ag_recv, sm_send, sm_recv, out_sem,
 ):
     step = pl.program_id(0)
@@ -789,8 +830,10 @@
             for p in parts:
                 p.advance()
 
-    def seed(k):
-        return pltpu.make_async_copy(gmid_any, xg_ref, out_sem.at[2])
+    def fetch(k):
+        src = (gmid_any, norm_any, own_any, oth_any, x_any)[k]
+        dst = (xg_ref, norm_t, own_ref, oth_ref, x_ref)[k]
+        return pltpu.make_async_copy(src, dst, out_sem.at[2 + k])
 
     @pl.when(step == 0)
     def _():
@@ -798,7 +841,8 @@
         dp_swap(groups).start()
         for r in routes:
             r.start()
-        seed(0).start()
+        for k in (1, 2, 3, 4, 0):
+            fetch(k).start()
 
     @pl.when((kind < 2) & (step < last))
     def _():
@@ -812,25 +856,25 @@
             go = do_ref[at, :]
             prod = go.astype(F32) * o_ref[at, :].astype(F32)
             query = q_ref[0, at, :]
-            parts = []
-            for j in range(2):
-                pick = lane_pick(128, j == 0)
-                go_j = jnp.where(pick, go, BF(0))
-                q_j = jnp.where(pick, query, BF(0))
-                inner = jnp.sum(jnp.where(pick, prod, 0.0), axis=-1, keepdims=True)
-                probs = prob_ref[j, :, OFFSET[i]:OFFSET[i] + w]
-                gp = dot_nt(go_j, values)
-                gs = (probs.astype(F32) * (gp - inner)).astype(BF)
-                parts.append(dot(gs, keys))
-                dk_s[s:s + w, :] += dot_tn(gs, q_j)
-                dv_s[s:s + w, :] += dot_tn(probs, go_j)
-            gh_s[3 * side, at, lanes] = (jnp.where(lane_pick(128, True), parts[0], parts[1]) * scale).astype(BF)
+            query, go_two = two_heads(query), two_heads(go)
+            inner = jnp.concatenate(
+                [jnp.sum(jnp.where(lane_pick(128, j == 0), prod, 0.0), axis=-1, keepdims=True) for j in range(2)], axis=0
+            )
+            probs = prob_ref[:, :, OFFSET[i]:OFFSET[i] + w].reshape(2 * QB, w)
+            gp = dot_nt(go_two, values)
+            gs = (probs.astype(F32) * (gp - inner)).astype(BF)
+            gq = dot(gs, keys)
+            dk_s[s:s + w, :] += dot_tn(gs, query)
+            dv_s[s:s + w, :] += dot_tn(probs, go_two)
+            gh_s[3 * side, at, lanes] = (jnp.where(lane_pick(128, True), gq[0:QB], gq[QB:2 * QB]) * scale).astype(BF)
         gh_s[3 * side + 1, :, lanes] = (dk_s[...] * scale).astype(BF)
         gh_s[3 * side + 2, :, lanes] = dv_s[...].astype(BF)
 
     for k in range(groups):
         @pl.when(step == 3 * k + 2)
         def _():
+            if k == 0:
+                fetch(1).wait()
             at = slice(k * 128, (k + 1) * 128)
             for c in range(3):
                 both = dot(norm_t[...], jnp.concatenate([gh_s[3 + c, :, at], gh_s[c, :, at]], axis=1))
@@ -880,6 +924,8 @@
                     if p.stage < 2 * stages:
                         p.advance()
 
+        fetch(2).wait()
+        fetch(3).wait()
         for c in range(3):
             if c:
                 turn()
@@ -889,7 +935,8 @@
             else:
                 gnp_s[...] = term
         turn()
-        seed(0).wait()
+        fetch(0).wait()
+        fetch(4).wait()
         small_out[...] = small_ref[...]
 
         def body(b, _):
@@ -960,7 +1007,7 @@
         grid=(last + 1,),
         in_specs=[
             head(0), head(1), head(2), pl.BlockSpec((2, QB, BAND), lambda i: (pair(i), 0, 0)), cols, cols,
-            fixed((tokens, width)), fixed((width, tokens)), fixed(own.shape), fixed(oth.shape),
+            ANY, ANY, ANY, ANY,
             fixed((width,)), fixed(small.shape), fixed((half, width)), ANY, ANY, ANY,
         ],
         out_specs=[fixed((tokens, width)), fixed(small.shape), ANY, ANY, ANY, ANY],
@@ -969,13 +1016,14 @@
             sds((rows, width), BF), sds((rows, width), BF),
         ],
         scratch_shapes=[
+            pltpu.VMEM((tokens, width), BF), pltpu.VMEM((width, tokens), BF), pltpu.VMEM(own.shape, BF), pltpu.VMEM(oth.shape, BF),
             pltpu.VMEM((tokens, 128), F32), pltpu.VMEM((tokens, 128), F32), pltpu.VMEM((6, tokens, half), BF),
             pltpu.VMEM((tokens, width), F32), sums, sums, sums, p_sums, p_sums, p_sums,
             pltpu.VMEM((groups, width, 384), BF), pltpu.VMEM((half, width), BF),
             pltpu.VMEM((groups, width, 384), BF), pltpu.VMEM((width, 384), F32),
             pltpu.VMEM((1 + stages, *small.shape), F32),
             *route_sems(n, 2), dma((groups + 1,)), dma((groups + 1,)), dma((parts, stages)), dma((parts, stages)),
-            dma((parts, stages)), dma((parts, stages)), dma((1 + stages,)), dma((1 + stages,)), dma((3,)),
+            dma((parts, stages)), dma((parts, stages)), dma((1 + stages,)), dma((1 + stages,)), dma((7,)),
         ],
         compiler_params=params(collective_id=5, has_side_effects=True),
         cost_estimate=cost(5.3e10, 9e7),

time: 440 us -> 431 us (0.980)
  Pallas kernels: 429 us -> 421 us
  transfers between devices with their start and end apart: 3 -> 3, of which waited for: 0 -> 0; matrix products, arithmetic and copies ran while one was open for 0% -> 0% of each run, Pallas kernels for 18% -> 19%
where the time goes in v5:
time: 431 us; the launch traced here: 424 us
  Pallas kernels  421 us (98%)
    pallas_call x1, Pallas kernels, back_call(): pl.pallas_call(functools.partial(back_kernel, n, cc, groups), grid=(last...  121 us
    pallas_call x1, Pallas kernels, expert_call(): pl.pallas_call(functools.partial(expert_kernel, n, cc, own_tiles), grid=(...  109 us
    pallas_call x1, Pallas kernels, front_call(): pl.pallas_call(functools.partial(front_kernel, n, cc, pairs), grid=(8 + p...  78.7 us
    pallas_call x1, Pallas kernels, wgrad_call(): pl.pallas_call(functools.partial(wgrad_kernel, n, cc, tiles), grid=(4 * t...  58.8 us
    pallas_call x1, Pallas kernels, middle_back_call(): pl.pallas_call(functools.partial(middle_back_kernel, n, cc, tokens // tb)...  32 us
    pallas_call x1, Pallas kernels, result_call(): pl.pallas_call(result_kernel, grid=(steps,), in_specs=[rows_of(tb, 128),...  20.9 us
  transfers between devices with their start and end apart: 3, of which 0 were waited for; matrix products, arithmetic and copies ran while one was open for 0% of the time, Pallas kernels for 19%

profile of v5, /device:TPU:0, one launch (start us, length us, event | category | flops | bytes accessed | tf_op | source)
XLA Modules:
  0.0 424.4 jit_solution(15782439017462875794)
XLA Ops:
  0.6 0.5 collective-permute-start
  1.2 0.1 collective-permute-start.1
  1.2 0.4 collective-permute-start.2
  1.7 78.7 %front.1 = (s32[1024,128]{1,0:T(8,128)}, bf16[1024,1024]{1,0:T(8,128)(2,1)}, bf16[6,1024,512]{2,1,0:T(8,128)(2,1)}, bf16[1024,1024]{1,0:T(8,128)(2,1)}, bf16[102...) custom-call(s32[1,1024]{1,0:T(1,128)} %bitcast.15, ...), custom_call_target="tpu_custom_call" | custom-call | flops 30000001024 | bytes 60000000 | tf_op jit(solution)/shard_map/front/pallas_call | solution.py:314
  80.3 0.0 collective-permute-done.2.bt_ref
  80.3 0.0 copy-start.2
  80.4 0.0 collective-permute-done.ut_ref
  80.4 0.0 collective-permute-done.1.dt_ref
  80.4 0.6 copy-done.2
  81.0 109.2 %experts.1 = (bf16[3,512,4096]{2,1,0:T(8,128)(2,1)}, bf16[3,512,4096]{2,1,0:T(8,128)(2,1)}, f32[8,4096]{1,0:T(8,128)}, bf16[3,512,1024]{2,1,0:T(8,128)(2,1)}, bf...) custom-call(bf16[1536,1024]{1,0:T(8,128)(2,1)} %get-tuple-element.61.mid_ref, ...), custom_call_target="tpu_custom_call" | custom-call | flops 51999997952 | bytes 80000000 | tf_op jit(solution)/shard_map/experts/pallas_call | solution.py:476
  190.2 58.8 %weight_grads.1 = (bf16[2048,1024]{1,0:T(8,128)(2,1)}, bf16[2048,1024]{1,0:T(8,128)(2,1)}, f32[1,2048]{1,0:T(1,128)}, f32[1,1024]{1,0:T(1,128)}, bf16[512,1024]{1,0:T(8,128)(2,1)}, /*index=5*/bf16[512,1024]{1,0:T(8,128)(2,1)}) custom-call(bf16[3,512,4096]{2,1,0:T(8,128)(2,1)} %get-tuple-element.64.a_ref, bf16[3,512,4096]{2,1,0:T(8,128)(2,1)} %get-tuple-element.65.g_ref, ...), custom_call_target="tpu_custom_call" | custom-call | flops 25999998976 | bytes 80000000 | tf_op jit(solution)/shard_map/weight_grads/pallas_call | solution.py:606
  249.0 32.0 %middle_back.1 = (f32[1024,1024]{1,0:T(8,128)}, bf16[1024,1024]{1,0:T(8,128)(2,1)}, bf16[512,1024]{1,0:T(8,128)(2,1)}, bf16[512,1024]{1,0:T(8,128)(2,1)}, f32[8,1024]{1,0:T(8,128)}, /*index=5*/bf16[512,1024]{1,0:T(8,128)(2,1)}) custom-call(s32[1024,128]{1,0:T(8,128)} %get-tuple-element.60.tcol_ref, bf16[512,1024]{1,0:T(8,128)(2,1)} %get-tuple-element.63.g0_any, ...), custom_call_target="tpu_custom_call" | custom-call | flops 12000000000 | bytes 30000000 | tf_op jit(solution)/shard_map/middle_back/pallas_call | solution.py:700
  281.0 121.0 %back.1 = (f32[1024,1024]{1,0:T(8,128)}, f32[8,1024]{1,0:T(8,128)}, bf16[4096,384]{1,0:T(8,128)(2,1)}, bf16[1024,512]{1,0:T(8,128)(2,1)}, bf16[512,1024]{1,0:T(8,128)(2,1)}, /*index=5*/bf16[512,1024]{1,0:T(8,128)(2,1)}) custom-call(bf16[6,1024,512]{2,1,0:T(8,128)(2,1)} %get-tuple-element.76.q_ref.k_ref.v_ref, ...), custom_call_target="tpu_custom_call" | custom-call | flops 52999999488 | bytes 90000000 | tf_op jit(solution)/shard_map/back/pallas_call | solution.py:1005
  402.0 0.0 copy-start
  402.1 0.0 copy-start.1
  402.1 20.9 %results.1 = (bf16[1024,1024]{1,0:T(8,128)(2,1)}, f32[3,1024,512]{2,1,0:T(8,128)}, f32[512,1024]{1,0:T(8,128)}, f32[1024,1024]{1,0:T(8,128)}, f32[2048,1024]{1,0...) custom-call(s32[1024,128]{1,0:T(8,128)} %get-tuple-element.60.tcol_r, ...), custom_call_target="tpu_custom_call" | custom-call | flops 3221225472 | bytes 60000000 | tf_op jit(solution)/shard_map/results/pallas_call | solution.py:1067
  423.0 0.0 copy-done
  423.0 0.6 copy.30
  423.6 0.0 copy-done.1
  423.6 0.6 copy.31
Async XLA Ops:
  0.6 79.7 %collective-permute-start = (bf16[2048,1024]{1,0:T(8,128)(2,1)}, bf16[2048,1024]{1,0:T(8,128)(2,1)}, u32[]{:S(2)}, u32[]{:S(2)}) collective-permute-start(bf16[2048,1024]{1,0:T(8,128)(2,1)} %bitcast.11), channel_id=1, source_target_pairs={{0,16},{16,0},{1,17},{17,1},{2,18},{18,2},{3,19},{19,3},{4,20},{20... | collective-permute-start | bytes 12582920 | tf_op jit(solution)/shard_map/ppermute | solution.py:1099
  1.2 79.2 %collective-permute-start.1 = (bf16[2048,1024]{1,0:T(8,128)(2,1)}, bf16[2048,1024]{1,0:T(8,128)(2,1)}, u32[]{:S(2)}, u32[]{:S(2)}) collective-permute-start(bf16[2048,1024]{1,0:T(8,128)(2,1)} %bitcast.13), channel_id=1, source_target_pairs={{0,16},{16,0},{1,17},{17,1},{2,18},{18,2},{3,19},{19,3},{4,20},{20... | collective-permute-start | bytes 12582920 | tf_op jit(solution)/shard_map/ppermute | solution.py:1099
  1.2 79.1 %collective-permute-start.2 = (bf16[1,2048]{1,0:T(2,128)(2,1)}, bf16[1,2048]{1,0:T(2,128)(2,1)S(1)}, u32[]{:S(2)}, u32[]{:S(2)}) collective-permute-start(bf16[1,2048]{1,0:T(2,128)(2,1)} %bo_ref.1), channel_id=1, source_target_pairs={{0,16},{16,0},{1,17},{17,1},{2,18},{18,2},{3,19},{19,3},{4,20},{20... | collective-permute-start | bytes 12296 | tf_op jit(solution)/shard_map/ppermute | solution.py:1099
  80.3 0.6 copy-start.2
  402.0 21.0 %copy-start = (f32[1,2048]{1,0:T(1,128)S(1)}, f32[1,2048]{1,0:T(1,128)}, u32[]{:S(2)}) copy-start(f32[1,2048]{1,0:T(1,128)} %get-tuple-element.130) | copy-start | bytes 24580
  402.1 21.6 %copy-start.1 = (f32[1,1024]{1,0:T(1,128)S(1)}, f32[1,1024]{1,0:T(1,128)}, u32[]{:S(2)}) copy-start(f32[1,1024]{1,0:T(1,128)} %get-tuple-element.132) | copy-start | bytes 12292

commit v6 on v5

--- a/solution.py
+++ b/solution.py
@@ -350,9 +350,9 @@
 
 
 def expert_kernel(
-    n, cc, own_tiles, mid_ref, c_ref, uo_ref, ut_ref, do_ref, dt_ref, bo_ref, bt_ref, db_ref,
+    n, cc, own_tiles, mid_ref, c_any, uo_ref, ut_ref, do_ref, dt_ref, bo_ref, bt_ref, db_ref,
     act_ref, gh_ref, ub_ref, y_ref, dx_ref, x_out, back_out,
-    x_s, g_s, y_s, dx_s, dxb_s, send, recv, local, xsem,
+    c_ref, x_s, g_s, y_s, dx_s, dxb_s, send, recv, local, xsem,
 ):
     step = pl.program_id(0)
     tiles = 2 * own_tiles
@@ -375,9 +375,12 @@
 
     @pl.when(step == 0)
     def _():
+        load = pltpu.make_async_copy(c_any, c_ref, xsem.at[CHUNKS])
+        load.start()
         greet(n, False)
         ins[0].start()
         ub_ref[...] = jnp.zeros_like(ub_ref)
+        load.wait()
 
     for c in range(CHUNKS):
         @pl.when(step == (c + 1) * tiles)
@@ -477,7 +480,7 @@
         functools.partial(expert_kernel, n, cc, own_tiles),
         grid=((CHUNKS + 1) * tiles,),
         in_specs=[
-            ANY, whole(cot.shape),
+            ANY, ANY,
             pl.BlockSpec((TILE, width), lambda i: (up_first(i), 0)),
             pl.BlockSpec((TILE, width), lambda i: (up_second(i), 0)),
             pl.BlockSpec((TILE, width), lambda i: (first(i), 0)),
@@ -493,9 +496,9 @@
             sds((rows, width), BF),
         ],
         scratch_shapes=[
-            pltpu.VMEM((CHUNKS, rows, width), BF), pltpu.VMEM((CHUNKS, rows, 2 * hid), BF),
+            pltpu.VMEM(cot.shape, BF), pltpu.VMEM((CHUNKS, rows, width), BF), pltpu.VMEM((CHUNKS, rows, 2 * hid), BF),
             pltpu.VMEM((rows, width), F32), pltpu.VMEM((rows, width), F32), pltpu.VMEM((rows, width), BF),
-            *route_sems(n, CHUNKS + 1), pltpu.SemaphoreType.DMA((CHUNKS,)),
+            *route_sems(n, CHUNKS + 1), pltpu.SemaphoreType.DMA((CHUNKS + 1,)),
         ],
         compiler_params=params(collective_id=2, has_side_effects=True),
         cost_estimate=cost(5.2e10, 8e7),
@@ -786,8 +789,8 @@
 def back_kernel(
     n, cc, groups, q_ref, k_ref, v_ref, prob_ref, do_ref, o_ref, x_any, norm_any, own_any, oth_any,
     gain_ref, small_ref, pg_own, pg_oth, gmid_any, y_src,
-    xg_ref, small_out, sum_q, sum_p, z1, z2,
-    x_ref, norm_t, own_ref, oth_ref, dk_s, dv_s, gh_s, gnp_s, acc, rcv, res, p_acc, p_rcv, p_res, got, pgot, snd, mine_s, small_got,
+    xg_out, small_out, sum_q, sum_p, z1, z2,
+    xg_ref, x_ref, norm_t, own_ref, oth_ref, dk_s, dv_s, gh_s, gnp_s, acc, rcv, res, p_acc, p_rcv, p_res, got, pgot, snd, mine_s, small_got,
     send, recv, local, dsend, drecv, rs_send, rs_recv, ag_send, ag_recv, sm_send, sm_recv, out_sem,
 ):
     step = pl.program_id(0)
@@ -949,6 +952,8 @@
             return 0
 
         lax.fori_loop(0, tokens // 128, body, 0)
+        done = pltpu.make_async_copy(xg_ref, xg_out, out_sem.at[7])
+        done.start()
         small = small_swap(0)
         small.start()
         for s in range(2 * stages - 2):
@@ -967,6 +972,7 @@
             out.start()
         for out in outs:
             out.wait()
+        done.wait()
         for r in routes:
             r.wait()
 
@@ -1010,12 +1016,13 @@
             ANY, ANY, ANY, ANY,
             fixed((width,)), fixed(small.shape), fixed((half, width)), ANY, ANY, ANY,
         ],
-        out_specs=[fixed((tokens, width)), fixed(small.shape), ANY, ANY, ANY, ANY],
+        out_specs=[ANY, fixed(small.shape), ANY, ANY, ANY, ANY],
         out_shape=[
             sds((tokens, width), F32), sds(small.shape, F32), sds((groups * width, 384), BF), sds((width, half), BF),
             sds((rows, width), BF), sds((rows, width), BF),
         ],
         scratch_shapes=[
+            pltpu.VMEM((tokens, width), F32),
             pltpu.VMEM((tokens, width), BF), pltpu.VMEM((width, tokens), BF), pltpu.VMEM(own.shape, BF), pltpu.VMEM(oth.shape, BF),
             pltpu.VMEM((tokens, 128), F32), pltpu.VMEM((tokens, 128), F32), pltpu.VMEM((6, tokens, half), BF),
             pltpu.VMEM((tokens, width), F32), sums, sums, sums, p_sums, p_sums, p_sums,
@@ -1023,7 +1030,7 @@
             pltpu.VMEM((groups, width, 384), BF), pltpu.VMEM((width, 384), F32),
             pltpu.VMEM((1 + stages, *small.shape), F32),
             *route_sems(n, 2), dma((groups + 1,)), dma((groups + 1,)), dma((parts, stages)), dma((parts, stages)),
-            dma((parts, stages)), dma((parts, stages)), dma((1 + stages,)), dma((1 + stages,)), dma((7,)),
+            dma((parts, stages)), dma((parts, stages)), dma((1 + stages,)), dma((1 + stages,)), dma((8,)),
         ],
         compiler_params=params(collective_id=5, has_side_effects=True),
         cost_estimate=cost(5.3e10, 9e7),

time: 431 us -> 428 us (level)
  no operation moved by 1% of the time
where the time goes in v6:
time: 428 us; the launch traced here: 421 us
  Pallas kernels  418 us (98%)
    pallas_call x1, Pallas kernels, back_call(): pl.pallas_call(functools.partial(back_kernel, n, cc, groups), grid=(last...  119 us
    pallas_call x1, Pallas kernels, expert_call(): pl.pallas_call(functools.partial(expert_kernel, n, cc, own_tiles), grid=(...  108 us
    pallas_call x1, Pallas kernels, front_call(): pl.pallas_call(functools.partial(front_kernel, n, cc, pairs), grid=(8 + p...  78.7 us
    pallas_call x1, Pallas kernels, wgrad_call(): pl.pallas_call(functools.partial(wgrad_kernel, n, cc, tiles), grid=(4 * t...  58.9 us
    pallas_call x1, Pallas kernels, middle_back_call(): pl.pallas_call(functools.partial(middle_back_kernel, n, cc, tokens // tb)...  31.9 us
    pallas_call x1, Pallas kernels, result_call(): pl.pallas_call(result_kernel, grid=(steps,), in_specs=[rows_of(tb, 128),...  20.9 us
  transfers between devices with their start and end apart: 3, of which 0 were waited for; matrix products, arithmetic and copies ran while one was open for 0% of the time, Pallas kernels for 19%

profile of v6, /device:TPU:0, one launch (start us, length us, event | category | flops | bytes accessed | tf_op | source)
XLA Modules:
  0.0 421.3 jit_solution(1312421400727021908)
XLA Ops:
  0.6 0.5 collective-permute-start
  1.2 0.1 collective-permute-start.1
  1.2 0.4 collective-permute-start.2
  1.7 78.7 %front.1 = (s32[1024,128]{1,0:T(8,128)}, bf16[1024,1024]{1,0:T(8,128)(2,1)}, bf16[6,1024,512]{2,1,0:T(8,128)(2,1)}, bf16[1024,1024]{1,0:T(8,128)(2,1)}, bf16[102...) custom-call(s32[1,1024]{1,0:T(1,128)} %bitcast.15, ...), custom_call_target="tpu_custom_call" | custom-call | flops 30000001024 | bytes 60000000 | tf_op jit(solution)/shard_map/front/pallas_call | solution.py:314
  80.3 0.0 collective-permute-done.2.bt_ref
  80.3 0.0 copy-start.2
  80.4 0.0 collective-permute-done.ut_ref
  80.4 0.0 collective-permute-done.1.dt_ref
  80.4 0.6 copy-done.2
  81.0 108.1 %experts.1 = (bf16[3,512,4096]{2,1,0:T(8,128)(2,1)}, bf16[3,512,4096]{2,1,0:T(8,128)(2,1)}, f32[8,4096]{1,0:T(8,128)}, bf16[3,512,1024]{2,1,0:T(8,128)(2,1)}, bf...) custom-call(bf16[1536,1024]{1,0:T(8,128)(2,1)} %get-tuple-element.61.mid_ref, ...), custom_call_target="tpu_custom_call" | custom-call | flops 51999997952 | bytes 80000000 | tf_op jit(solution)/shard_map/experts/pallas_call | solution.py:479
  189.0 58.9 %weight_grads.1 = (bf16[2048,1024]{1,0:T(8,128)(2,1)}, bf16[2048,1024]{1,0:T(8,128)(2,1)}, f32[1,2048]{1,0:T(1,128)}, f32[1,1024]{1,0:T(1,128)}, bf16[512,1024]{1,0:T(8,128)(2,1)}, /*index=5*/bf16[512,1024]{1,0:T(8,128)(2,1)}) custom-call(bf16[3,512,4096]{2,1,0:T(8,128)(2,1)} %get-tuple-element.64.a_ref, bf16[3,512,4096]{2,1,0:T(8,128)(2,1)} %get-tuple-element.65.g_ref, ...), custom_call_target="tpu_custom_call" | custom-call | flops 25999998976 | bytes 80000000 | tf_op jit(solution)/shard_map/weight_grads/pallas_call | solution.py:609
  247.9 31.9 %middle_back.1 = (f32[1024,1024]{1,0:T(8,128)}, bf16[1024,1024]{1,0:T(8,128)(2,1)}, bf16[512,1024]{1,0:T(8,128)(2,1)}, bf16[512,1024]{1,0:T(8,128)(2,1)}, f32[8,1024]{1,0:T(8,128)}, /*index=5*/bf16[512,1024]{1,0:T(8,128)(2,1)}) custom-call(s32[1024,128]{1,0:T(8,128)} %get-tuple-element.60.tcol_ref, bf16[512,1024]{1,0:T(8,128)(2,1)} %get-tuple-element.63.g0_any, ...), custom_call_target="tpu_custom_call" | custom-call | flops 12000000000 | bytes 30000000 | tf_op jit(solution)/shard_map/middle_back/pallas_call | solution.py:703
  279.9 119.1 %back.1 = (f32[1024,1024]{1,0:T(8,128)}, f32[8,1024]{1,0:T(8,128)}, bf16[4096,384]{1,0:T(8,128)(2,1)}, bf16[1024,512]{1,0:T(8,128)(2,1)}, bf16[512,1024]{1,0:T(8,128)(2,1)}, /*index=5*/bf16[512,1024]{1,0:T(8,128)(2,1)}) custom-call(bf16[6,1024,512]{2,1,0:T(8,128)(2,1)} %get-tuple-element.76.q_ref.k_ref.v_ref, ...), custom_call_target="tpu_custom_call" | custom-call | flops 52999999488 | bytes 90000000 | tf_op jit(solution)/shard_map/back/pallas_call | solution.py:1011
  399.0 0.0 copy-start
  399.0 0.0 copy-start.1
  399.0 20.9 %results.1 = (bf16[1024,1024]{1,0:T(8,128)(2,1)}, f32[3,1024,512]{2,1,0:T(8,128)}, f32[512,1024]{1,0:T(8,128)}, f32[1024,1024]{1,0:T(8,128)}, f32[2048,1024]{1,0...) custom-call(s32[1024,128]{1,0:T(8,128)} %get-tuple-element.60.tcol_r, ...), custom_call_target="tpu_custom_call" | custom-call | flops 3221225472 | bytes 60000000 | tf_op jit(solution)/shard_map/results/pallas_call | solution.py:1074
  419.9 0.0 copy-done
  419.9 0.6 copy.30
  420.5 0.0 copy-done.1
  420.5 0.6 copy.31
Async XLA Ops:
  0.6 79.7 %collective-permute-start = (bf16[2048,1024]{1,0:T(8,128)(2,1)}, bf16[2048,1024]{1,0:T(8,128)(2,1)}, u32[]{:S(2)}, u32[]{:S(2)}) collective-permute-start(bf16[2048,1024]{1,0:T(8,128)(2,1)} %bitcast.11), channel_id=1, source_target_pairs={{0,16},{16,0},{1,17},{17,1},{2,18},{18,2},{3,19},{19,3},{4,20},{20... | collective-permute-start | bytes 12582920 | tf_op jit(solution)/shard_map/ppermute | solution.py:1106
  1.2 79.2 %collective-permute-start.1 = (bf16[2048,1024]{1,0:T(8,128)(2,1)}, bf16[2048,1024]{1,0:T(8,128)(2,1)}, u32[]{:S(2)}, u32[]{:S(2)}) collective-permute-start(bf16[2048,1024]{1,0:T(8,128)(2,1)} %bitcast.13), channel_id=1, source_target_pairs={{0,16},{16,0},{1,17},{17,1},{2,18},{18,2},{3,19},{19,3},{4,20},{20... | collective-permute-start | bytes 12582920 | tf_op jit(solution)/shard_map/ppermute | solution.py:1106
  1.2 79.1 %collective-permute-start.2 = (bf16[1,2048]{1,0:T(2,128)(2,1)}, bf16[1,2048]{1,0:T(2,128)(2,1)S(1)}, u32[]{:S(2)}, u32[]{:S(2)}) collective-permute-start(bf16[1,2048]{1,0:T(2,128)(2,1)} %bo_ref.1), channel_id=1, source_target_pairs={{0,16},{16,0},{1,17},{17,1},{2,18},{18,2},{3,19},{19,3},{4,20},{20... | collective-permute-start | bytes 12296 | tf_op jit(solution)/shard_map/ppermute | solution.py:1106
  80.3 0.6 copy-start.2
  399.0 21.0 %copy-start = (f32[1,2048]{1,0:T(1,128)S(1)}, f32[1,2048]{1,0:T(1,128)}, u32[]{:S(2)}) copy-start(f32[1,2048]{1,0:T(1,128)} %get-tuple-element.130) | copy-start | bytes 24580
  399.0 21.6 %copy-start.1 = (f32[1,1024]{1,0:T(1,128)S(1)}, f32[1,1024]{1,0:T(1,128)}, u32[]{:S(2)}) copy-start(f32[1,1024]{1,0:T(1,128)} %get-tuple-element.132) | copy-start | bytes 12292
